TPU v7x, 32 devices: a whole 2x2x4 slice. The times are simulated.
32 devices in a mesh: grp: 8 (over z, x), reg: 4 (over y, core).
Axes of the slice: x: 2, y: 2, z: 4, core: 2. Of those that a mesh axis runs over, the one named last changes fastest.
Arguments:
- orbitals: bfloat16 [4, 8, 512, 1024], P('reg', 'grp'), may hold values from -6 to 6
- occupied: bfloat16 [4, 8, 8, 512], P('reg', 'grp'), may hold values from -0.59765625 to 0.59765625
- panel_index: int32 [128], replicated, may hold values from 0 to 1023, as said below
- screening: bfloat16 [224, 512, 512], P(('grp', 'reg')), may hold values from -0.25 to 0.25
- block_region: int32 [224, 1], P(('grp', 'reg')), may hold values from 0 to 3; in each aligned block of 7 rows (0 to 6, 7 to 13, ...) at most 2 rows name the same one
- block_row: int32 [224], P(('grp', 'reg')), may hold values from 0 to 7
- block_col: int32 [224], P(('grp', 'reg')), may hold values from 0 to 7
Outputs:
- sigma: float32 [4, 128, 128], P('reg')
Inputs may be any that keep to these rules, and one draw needn't show every extreme that they name: `panel_index`: the 128 indices are distinct. Among the 7 blocks of one device (aligned rows of block_region), at most 2 name the same region.
All inputs are finite; a program needn't handle non-finite values.
Results may differ from a plain program's by a relative error of at most 0.0054.
Values may be sent and summed in bfloat16 or wider, within the bound.
No kernel may reach another device: no remote copies, remote signals or barrier semaphores. Data moves between devices by JAX's collectives and lax.ppermute only.
A program may use at most 192 MiB of HBM per device.

v0:
```python
import jax
import jax.numpy as jnp
from jax import lax
from jax.sharding import PartitionSpec as P

CAP = 2


def form_pairs(orbital_rows, occupied_rows):
    pairs = orbital_rows[..., :, None, :].astype(jnp.float32) * jnp.swapaxes(occupied_rows, -1, -2)[
        ..., None
    ].astype(jnp.float32)
    return pairs.astype(jnp.bfloat16)


def shards(orbitals, occupied, panel_index, screening, block_region, block_row, block_col):
    regions = lax.axis_size("reg")
    panel_orbs = jnp.take(orbitals[0], panel_index, axis=2)
    occ_rows = occupied[0]
    grid_points = screening.shape[1]
    panel_width = panel_orbs.shape[2]
    occ_count = occ_rows.shape[1]
    held_count = screening.shape[0]
    slot_count = regions * CAP
    destination = block_region[:, 0]
    membership = (destination[:, None] == jnp.arange(regions, dtype=jnp.int32)[None, :]).astype(
        jnp.int32
    )
    earlier = jnp.cumsum(membership, axis=0) - membership
    slot_of = destination * CAP + jnp.sum(earlier * membership, axis=1)
    matched = (slot_of[None, :] == jnp.arange(slot_count, dtype=jnp.int32)[:, None]).astype(
        jnp.int32
    )
    filled = jnp.sum(matched, axis=1)
    source = jnp.sum(matched * jnp.arange(held_count, dtype=jnp.int32)[None, :], axis=1)
    outgoing = jnp.take(screening, source, axis=0) * filled[:, None, None].astype(jnp.bfloat16)
    labels = jnp.stack(
        [jnp.take(block_row, source) * filled, jnp.take(block_col, source) * filled, filled], axis=1
    )
    gathered = lax.all_gather(form_pairs(panel_orbs, occ_rows), "grp", axis=0, tiled=True)

    def select_pairs(indices):
        return jnp.take(gathered, indices, axis=0)

    incoming, arrived = (
        lax.all_to_all(
            outgoing.reshape(regions, CAP, grid_points, grid_points),
            "reg",
            split_axis=0,
            concat_axis=0,
            tiled=True,
        ),
        lax.all_to_all(
            labels.reshape(regions, CAP, 3), "reg", split_axis=0, concat_axis=0, tiled=True
        ),
    )
    incoming = incoming.reshape(slot_count, grid_points, grid_points)
    arrived = arrived.reshape(slot_count, 3)
    col_pairs = select_pairs(arrived[:, 1]).reshape(
        slot_count, grid_points, occ_count * panel_width
    )
    screened = jnp.einsum(
        "spq,sqc->spc", incoming, col_pairs, preferred_element_type=jnp.float32
    ).astype(jnp.bfloat16)
    row_pairs = select_pairs(arrived[:, 0]).reshape(
        slot_count, grid_points * occ_count, panel_width
    )
    partial_sigma = jnp.einsum(
        "sri,srj->ij",
        row_pairs,
        screened.reshape(slot_count, grid_points * occ_count, panel_width),
        preferred_element_type=jnp.float32,
    )
    sigma = lax.psum(partial_sigma, "grp")
    return sigma[None]


def solution(mesh):
    in_specs = (
        P("reg", "grp", None, None),
        P("reg", "grp", None, None),
        P(),
        P(("grp", "reg"), None, None),
        P(("grp", "reg"), None),
        P(("grp", "reg")),
        P(("grp", "reg")),
    )
    out_specs = P("reg", None, None)
    return jax.shard_map(shards, mesh=mesh, in_specs=in_specs, out_specs=out_specs, check_vma=False)
```

profile of v0, /device:TPU:0, one launch (start us, length us, event | category | flops | bytes accessed | tf_op | source)
XLA Modules:
  0.0 287.2 jit_solution(3734475109991441804)
XLA Ops:
  6.5 0.0 copy-start
  6.5 0.0 all-gather.2.cloned.1.call-start
  6.5 0.7 compare_select_fusion.5
  7.2 0.7 compare_and_fusion.4
  7.9 1.5 copy.23
  9.4 0.8 gather_fusion
  10.2 0.1 convert_bitcast_fusion
  10.3 0.1 copy.24
  10.5 0.7 convert_bitcast_fusion.1
  11.2 0.1 copy.25
  11.3 1.5 multiply_convert_fusion
  12.8 0.0 all-gather.2.cloned.1.call-update
  12.9 0.7 fusion.8
  13.5 0.2 reduce_window_sum.11
  13.7 0.7 select_reduce_fusion.1
  14.4 0.7 multiply_add_fusion
  15.1 0.2 convert_reduce_fusion
  15.2 0.0 copy-done
  15.2 0.6 gather_fusion.2
  15.9 1.3 gather_fusion.3
  17.2 0.1 stack.14
  17.3 0.1 stack.12
  17.4 0.1 stack.13
  17.5 0.7 copy.22
  18.2 4.2 %all-to-all-start = ((s32[4,2,3]{2,1,0:T(2,128)}), s32[4,2,3]{2,1,0:T(2,128)S(1)}, u32[]{:S(2)}, u32[]{:S(2)}) async-start(s32[4,2,3]{2,1,0:T(2,128)} %copy.22), calls=%async_computation | async-start | bytes 8192 | tf_op jit(solution)/shard_map/all_to_all | solution.py:53
  22.4 0.1 reduce_sum.34
  22.5 0.1 convert_element_type.65
  22.6 5.3 %gather_fusion.1 = bf16[8,512,512]{2,1,0:T(8,128)(2,1)} fusion(bf16[7,512,512]{2,1,0:T(8,128)(2,1)} %param.14, s32[1024]{0:T(1024)S(1)} %pad_clamp_fusion.1), kind=kCustom, calls=%fused_computation.5 | custom fusion | bytes 8388640 | tf_op jit(solution)/shard_map/jit(_take)/gather | solution.py:36
  27.9 4.6 %select_multiply_fusion = bf16[4,2,512,512]{3,2,1,0:T(8,128)(2,1)} fusion(bf16[4,2,512,512]{3,2,1,0:T(8,128)(2,1)} %bitcast.32, pred[4,2]{1,0:T(4,128)(4,1)S(1)} %compare_and_fusion.3, bf16[4,2]{1,0:T(4,128)(2,1)S(1)} %convert_element_type.65), kind=kLoop, calls=%fused_computation.13 | loop fusion | flops 4194304 | bytes 8388632 | tf_op jit(solution)/shard_map/mul | solution.py:36
  32.4 0.0 all-to-all-done
  32.4 4.9 %all-to-all-start.1 = ((bf16[4,2,512,512]{3,2,1,0:T(8,128)(2,1)}), bf16[4,2,512,512]{3,2,1,0:T(8,128)(2,1)}, u32[]{:S(2)}, u32[]{:S(2)}) async-start(bf16[4,2,512,512]{3,2,1,0:T(8,128)(2,1)} %select_multiply_fusion), calls=%async_computation.1 | async-start | bytes 8388608 | tf_op jit(solution)/shard_map/all_to_all | solution.py:46
  37.4 0.0 all-reduce.2.cloned.1.call-start
  37.4 0.2 slice_reduce_fusion.1
  37.7 103.0 %all-gather.2.cloned.1.call-done = bf16[8,512,8,128]{3,2,1,0:T(8,128)(2,1)} async-done(((bf16[1,512,8,128]{3,2,1,0:T(8,128)(2,1)}), bf16[8,512,8,128]{3,2,1,0:T(8,128)(2,1)}) %all-gather.2.cloned.1.call-update) | async-done | bytes 8388624 | tf_op jit(solution)/shard_map/all_gather | solution.py:40
  140.7 8.1 %gather_fusion.5 = bf16[8,512,8,128]{3,2,1,0:T(8,128)(2,1)} fusion(bf16[8,512,8,128]{3,2,1,0:T(8,128)(2,1)} %all-gather.2.cloned.1.call-done, s32[1024]{0:T(1024)S(1)} %pad_clamp_fusion), kind=kCustom, calls=%fused_computation.3.clone | custom fusion | bytes 16777248 | tf_op jit(solution)/shard_map/jit(_take)/gather | solution.py:43
  148.7 7.5 %broadcast_select_fusion = bf16[8,512,8,128]{3,2,1,0:T(8,128)(2,1)} fusion(bf16[8,512,8,128]{3,2,1,0:T(8,128)(2,1)} %gather_fusion.5, pred[8]{0:T(512)(128)(4,1)S(1)} %get-tuple-element.16), kind=kLoop, calls=%fused_computation.9 | loop fusion | flops 4194304 | bytes 16777224 | tf_op jit(solution)/shard_map/jit(_take)/select_n | solution.py:43
  156.2 13.3 %reshape.130 = bf16[8,512,1024]{2,1,0:T(8,128)(2,1)} reshape(bf16[8,512,8,128]{3,2,1,0:T(8,128)(2,1)} %broadcast_select_fusion) | data formatting | bytes 16777216 | tf_op jit(solution)/shard_map/reshape | solution.py:59
  169.5 0.0 all-to-all-done.1
  169.5 12.4 %convolution_convert_fusion = bf16[8,512,1024]{2,1,0:T(8,128)(2,1)} fusion(bf16[8,512,512]{2,1,0:T(8,128)(2,1)} %bitcast.11, bf16[8,512,1024]{2,1,0:T(8,128)(2,1)} %reshape.130), kind=kOutput, calls=%fused_computation.11 | convolution fusion | flops 4299161600 | bytes 20971520 | tf_op jit(solution)/shard_map/spq,sqc->spc/dot_general | solution.py:62
  181.9 13.3 %reshape.131 = bf16[8,4096,128]{2,1,0:T(8,128)(2,1)} reshape(bf16[8,512,1024]{2,1,0:T(8,128)(2,1)} %convolution_convert_fusion) | data formatting | bytes 16777216 | tf_op jit(solution)/shard_map/reshape | solution.py:71
  195.2 8.0 %gather_fusion.4 = bf16[8,512,8,128]{3,2,1,0:T(8,128)(2,1)} fusion(bf16[8,512,8,128]{3,2,1,0:T(8,128)(2,1)} %all-gather.2.cloned.1.call-done, s32[1024]{0:T(1024)S(1)} %pad_clamp_fusion.2), kind=kCustom, calls=%fused_computation.1.clone | custom fusion | bytes 16777248 | tf_op jit(solution)/shard_map/jit(_take)/gather | solution.py:43
  203.2 0.0 copy-start.1
  203.2 9.1 %fusion.5 = f32[1,128,128]{2,1,0:T(8,128)} fusion(bf16[8,4096,128]{2,1,0:T(8,128)(2,1)} %reshape.131, bf16[8,512,8,128]{3,2,1,0:T(8,128)(2,1)} %gather_fusion.4, pred[8]{0:T(512)(128)(4,1)S(1)} %get-tuple-element.17), kind=kOutput, calls=%fused_computation.15 | convolution fusion | flops 1077936128 | bytes 16842760 | tf_op jit(solution)/shard_map/sri,srj->ij/dot_general | solution.py:68
  212.3 0.0 all-reduce.2.cloned.1.call-update
  212.3 66.6 %all-reduce.2.cloned.1.call-done = f32[1,128,128]{2,1,0:T(8,128)} async-done(((f32[1,128,128]{2,1,0:T(8,128)}), f32[1,128,128]{2,1,0:T(8,128)}) %all-reduce.2.cloned.1.call-update) | async-done | bytes 65552 | tf_op jit(solution)/shard_map/psum | solution.py:74
  278.9 1.5 copy.29
  280.4 0.0 copy-done.1
  (12 shorter events, 0.1 us)
Async XLA Ops:
  6.5 8.7 %copy-start = (s32[7]{0:T(128)S(1)}, s32[7]{0:T(128)}, u32[]{:S(2)}) copy-start(s32[7]{0:T(128)} %param.16) | copy-start | bytes 88
  6.5 134.1 %all-gather.2.cloned.1.call-start = ((), (), s32[]{:S(2)}) async-start(), calls=%async_computation.2 | async-start | bytes 9437184 | tf_op jit(solution)/shard_map/all_gather | solution.py:40
  18.2 14.3 %all-to-all-start = ((s32[4,2,3]{2,1,0:T(2,128)}), s32[4,2,3]{2,1,0:T(2,128)S(1)}, u32[]{:S(2)}, u32[]{:S(2)}) async-start(s32[4,2,3]{2,1,0:T(2,128)} %copy.22), calls=%async_computation | async-start | bytes 8192 | tf_op jit(solution)/shard_map/all_to_all | solution.py:53
  32.4 137.0 %all-to-all-start.1 = ((bf16[4,2,512,512]{3,2,1,0:T(8,128)(2,1)}), bf16[4,2,512,512]{3,2,1,0:T(8,128)(2,1)}, u32[]{:S(2)}, u32[]{:S(2)}) async-start(bf16[4,2,512,512]{3,2,1,0:T(8,128)(2,1)} %select_multiply_fusion), calls=%async_computation.1 | async-start | bytes 8388608 | tf_op jit(solution)/shard_map/all_to_all | solution.py:46
  37.4 241.5 %all-reduce.2.cloned.1.call-start = ((), (), s32[]{:S(2)}) async-start(), calls=%async_computation.3 | async-start | bytes 131072 | tf_op jit(solution)/shard_map/psum | solution.py:74
  203.2 77.2 %copy-start.1 = (s32[7]{0:T(128)S(1)}, s32[7]{0:T(128)}, u32[]{:S(2)}) copy-start(s32[7]{0:T(128)} %param.16) | copy-start | bytes 88
Sparse Core Ops, SparseCore 0:
  13.0 127.6 all-gather.1
  212.5 66.4 all-reduce.1
where the time goes:
time: 289 us; the launch traced here: 287 us
  waiting for transfers between devices  170 us (59%)
  local copies, waits for them, and re-layouts  55.2 us (19%)
  matrix products  21.5 us (7%)
  other arithmetic  18.1 us (6%)
  between operations  13.5 us (5%)
  starting transfers between devices  9.22 us (3%)
    all_gather x1, waiting for transfers between devices, shards(): lax.all_gather(form_pairs(panel_orbs, occ_rows), 'grp', axis=0, tiled=True)  103 us
    psum x1, waiting for transfers between devices, shards(): sigma = lax.psum(partial_sigma, 'grp')  66.6 us
    gather x2, local copies, waits for them, and re-layouts, select_pairs(): return jnp.take(gathered, indices, axis=0)  16 us
    reshape x1, local copies, waits for them, and re-layouts, shards(): select_pairs(arrived[:, 1])  13.3 us
    reshape x1, local copies, waits for them, and re-layouts, shards(): screened.reshape(slot_count, grid_points * occ_count, panel_width)  13.3 us
    dot_general x1, matrix products, shards(): jnp.einsum('spq,sqc->spc', incoming, col_pairs, preferred_element_type=jn...  12.4 us
    dot_general x1, matrix products, shards(): jnp.einsum('sri,srj->ij', row_pairs, screened.reshape(slot_count, grid_po...  9.12 us
    select_n x2, other arithmetic, select_pairs(): return jnp.take(gathered, indices, axis=0)  7.47 us
  transfers between devices with their start and end apart: 4, of which 2 were waited for; matrix products, arithmetic and copies ran while one was open for 15% of the time, Pallas kernels for 0%

commit v1 on v0

v1 whole, which is shorter than its diff:
```python
import jax
import jax.numpy as jnp
from jax import lax
from jax.experimental import pallas as pl
from jax.experimental.pallas import tpu as pltpu
from jax.sharding import PartitionSpec as P

AXES = ("grp", "reg")
VMEM_LIMIT = 48 * 1024 * 1024


def pack_kernel(index_ref, orbitals_ref, occupied_ref, packed_ref):
    points, orbs = orbitals_ref.shape
    width = index_ref.shape[1]
    occ_count = occupied_ref.shape[0]
    rows = lax.broadcasted_iota(jnp.int32, (orbs, width), 0)
    chosen = jnp.where(rows == index_ref[...], 1.0, 0.0).astype(jnp.bfloat16)
    panel = jnp.dot(orbitals_ref[...], chosen, preferred_element_type=jnp.float32)
    packed_ref[:points, :] = panel.astype(jnp.bfloat16)
    occ = occupied_ref[...].astype(jnp.float32)
    slabs = [occ[:, at : at + width] for at in range(0, points, width)]
    packed_ref[points:, :] = jnp.concatenate(slabs, axis=0).astype(jnp.bfloat16)


def pack(panel_index, orbitals, occupied):
    points = orbitals.shape[0]
    width = panel_index.shape[0]
    occ_rows = occupied.shape[0] * points // width
    return pl.pallas_call(
        pack_kernel,
        out_shape=jax.ShapeDtypeStruct((points + occ_rows, width), jnp.bfloat16),
        compiler_params=pltpu.CompilerParams(vmem_limit_bytes=VMEM_LIMIT),
    )(panel_index[None, :], orbitals, occupied)


def sigma_kernel(pieces, points, occ_count, *refs):
    labels_ref, own_ref, other_ref = refs[:3]
    piece_refs = refs[3 : 3 + len(pieces)]
    out_ref, packed, blocks, piece_sems, block_sems = refs[3 + len(pieces) :]
    held = own_ref.shape[0]
    width = packed.shape[2]

    def piece_copy(n):
        slot, first, rows = pieces[n]
        return pltpu.make_async_copy(
            piece_refs[n], packed.at[slot, pl.ds(first, rows)], piece_sems.at[n]
        )

    def block_copy(source, n, at):
        return pltpu.make_async_copy(source.at[n], blocks.at[at], block_sems.at[at])

    for n in range(held):
        for source, at in ((own_ref, n), (other_ref, held + n)):

            @pl.when(labels_ref[at, 0] >= 0)
            def _():
                block_copy(source, n, at).start()

    for n in range(len(pieces)):
        piece_copy(n).start()
    out_ref[...] = jnp.zeros_like(out_ref)
    for n in range(len(pieces)):
        piece_copy(n).wait()

    def occupied_of(slot):
        rows = packed[slot, points:, :].astype(jnp.float32)
        slabs = [rows[at : at + occ_count] for at in range(0, rows.shape[0], occ_count)]
        return jnp.concatenate(slabs, axis=1).astype(jnp.bfloat16)

    for n in range(held):
        for source, at in ((own_ref, n), (other_ref, held + n)):
            place, row, col = labels_ref[at, 0], labels_ref[at, 1], labels_ref[at, 2]

            @pl.when(place >= 0)
            def _():
                block_copy(source, n, at).wait()
                overlap = lax.dot_general(
                    occupied_of(row),
                    occupied_of(col),
                    (((0,), (0,)), ((), ())),
                    preferred_element_type=jnp.float32,
                )
                dressed = (blocks[at].astype(jnp.float32) * overlap).astype(jnp.bfloat16)
                screened = jnp.dot(
                    dressed, packed[col, :points, :], preferred_element_type=jnp.float32
                ).astype(jnp.bfloat16)
                out_ref[place] += lax.dot_general(
                    packed[row, :points, :],
                    screened,
                    (((0,), (0,)), ((), ())),
                    preferred_element_type=jnp.float32,
                )


def partial_sigma(labels, own, other, pieces, arrays, slots, regions, points, occ_count):
    rows, width = arrays[0].shape
    rows = max(first + count for _, first, count in pieces)
    held = own.shape[0]
    return pl.pallas_call(
        lambda *refs: sigma_kernel(pieces, points, occ_count, *refs),
        out_shape=jax.ShapeDtypeStruct((regions, width, width), jnp.float32),
        in_specs=[pl.BlockSpec(memory_space=pltpu.SMEM)]
        + [pl.BlockSpec(memory_space=pl.ANY)] * (2 + len(arrays)),
        scratch_shapes=[
            pltpu.VMEM((slots, rows, width), jnp.bfloat16),
            pltpu.VMEM((2 * held,) + own.shape[1:], jnp.bfloat16),
            pltpu.SemaphoreType.DMA((len(arrays),)),
            pltpu.SemaphoreType.DMA((2 * held,)),
        ],
        compiler_params=pltpu.CompilerParams(vmem_limit_bytes=VMEM_LIMIT),
    )(labels, own, other, *arrays)


def swap(array, mask, count):
    return lax.ppermute(array, AXES, [(i, i ^ mask) for i in range(count)])


def gather(packed, count, first_bit):
    bits = []
    while first_bit < count:
        bits.append(first_bit)
        first_bit *= 2
    rows = packed.shape[0]
    half = rows // 32 * 16
    far = bits[2:]
    column = [(0, packed)]
    for mask in range(far[0], count, far[0]):
        column.append((mask, swap(packed, mask, count)))
    y, x = bits[0], bits[1]
    found = []
    for mask, array in column:
        over_x, over_y = swap(array, x, count), swap(array, y, count)
        found += [(mask, 0, array), (mask ^ x, 0, over_x), (mask ^ y, 0, over_y)]
        found.append((mask ^ x ^ y, 0, swap(over_x[:half], y, count)))
        found.append((mask ^ x ^ y, half, swap(over_y[half:], x, count)))
    return found


def total(values):
    while len(values) > 1:
        values = [values[n] + values[n + 1] for n in range(0, len(values), 2)]
    return values[0]


def shards(orbitals, occupied, panel_index, screening, block_region, block_row, block_col):
    groups, regions = lax.axis_size("grp"), lax.axis_size("reg")
    count = groups * regions
    me = lax.axis_index("grp") * regions + lax.axis_index("reg")
    core = lax.axis_index("reg") % 2
    points, occ_count = screening.shape[1], occupied.shape[2]

    labels = jnp.stack([block_region[:, 0], block_row, block_col], axis=1)
    both = jnp.concatenate([labels, swap(labels, 1, count)], axis=0)
    region = both[:, 0]
    place = jnp.where(region % 2 == core, (region ^ lax.axis_index("reg")) // 2, -1)
    slot = ((both[:, 1:] * regions + region[:, None]) ^ me) // 2
    labels = jnp.concatenate([place[:, None], slot], axis=1)
    other = swap(screening, 1, count)

    packed = pack(panel_index, orbitals[0, 0], occupied[0, 0])
    found = gather(packed, count, 2)
    pieces = [(mask // 2, first, array.shape[0]) for mask, first, array in found]
    sums = partial_sigma(
        labels,
        screening,
        other,
        pieces,
        [array for _, _, array in found],
        count // 2,
        regions // 2,
        points,
        occ_count,
    )
    stage = []
    for low in (0, regions):
        for mask in range(0, regions, 2):
            part = sums[mask // 2]
            stage.append(swap(part, low ^ mask, count) if low ^ mask else part)
    sigma = total(stage)
    bit = 2 * regions
    while bit < count:
        top = min(4 * bit, count)
        sigma = total([sigma] + [swap(sigma, mask, count) for mask in range(bit, top, bit)])
        bit = top
    return sigma[None]


def solution(mesh):
    in_specs = (
        P("reg", "grp", None, None),
        P("reg", "grp", None, None),
        P(),
        P(("grp", "reg"), None, None),
        P(("grp", "reg"), None),
        P(("grp", "reg")),
        P(("grp", "reg")),
    )
    out_specs = P("reg", None, None)
    return jax.shard_map(shards, mesh=mesh, in_specs=in_specs, out_specs=out_specs, check_vma=False)
```

time: 289 us -> 71.8 us (0.25)
  waiting for transfers between devices: 170 us -> 19.5 us
  local copies, waits for them, and re-layouts: 55.2 us -> 4.78 us
  starting transfers between devices: 9.22 us -> 34.4 us
  matrix products: 21.5 us -> 0 us
  other arithmetic: 18.1 us -> 2.15 us
  between operations: 13.5 us -> 0.14 us
  Pallas kernels: 0 us -> 10.5 us
    all_gather x1 -> x0, waiting for transfers between devices: 103 us -> none  [shards(): lax.all_gather(form_pairs(panel_orbs, occ_rows), 'grp', axis=0, tiled=True)]
    psum x1 -> x0, waiting for transfers between devices: 66.6 us -> none  [shards(): sigma = lax.psum(partial_sigma, 'grp')]
    ppermute x0 -> x27, starting transfers between devices: none -> 34.4 us  [swap(): return lax.ppermute(array, AXES, [(i, i ^ mask) for i in range(count)])]
    reshape x2 -> x0, local copies, waits for them, and re-layouts: 26.6 us -> none  [the longest x1 13.3 us: shards(): select_pairs(arrived[:, 1])]
    gather x6 -> x0, local copies, waits for them, and re-layouts: 24.1 us -> none  [the longest x2 16 us: select_pairs(): return jnp.take(gathered, indices, axis=0)]
    dot_general x2 -> x0, matrix products: 21.5 us -> none  [the longest x1 12.4 us: shards(): jnp.einsum('spq,sqc->spc', incoming, col_pairs, preferred_element_type=jn...]
    ppermute x0 -> x27, waiting for transfers between devices: none -> 19.5 us  [swap(): return lax.ppermute(array, AXES, [(i, i ^ mask) for i in range(count)])]
    pallas_call x0 -> x2, Pallas kernels: none -> 10.5 us  [the longest x1 10 us: partial_sigma(): pl.pallas_call(lambda *refs: sigma_kernel(pieces, points, occ_count, *ref...]
  transfers between devices with their start and end apart: 4 -> 27, of which waited for: 2 -> 15; matrix products, arithmetic and copies ran while one was open for 15% -> 2% of each run, Pallas kernels for 0% -> 1%
where the time goes in v1:
time: 71.8 us; the launch traced here: 71.5 us
  starting transfers between devices  34.4 us (48%)
  waiting for transfers between devices  19.5 us (27%)
  Pallas kernels  10.5 us (15%)
  local copies, waits for them, and re-layouts  4.78 us (7%)
  other arithmetic  2.15 us (3%)
    ppermute x27, starting transfers between devices, swap(): return lax.ppermute(array, AXES, [(i, i ^ mask) for i in range(count)])  34.4 us
    ppermute x27, waiting for transfers between devices, swap(): return lax.ppermute(array, AXES, [(i, i ^ mask) for i in range(count)])  19.5 us
    pallas_call x1, Pallas kernels, partial_sigma(): pl.pallas_call(lambda *refs: sigma_kernel(pieces, points, occ_count, *ref...  10 us
    unnamed x8, local copies, waits for them, and re-layouts  4.61 us
  transfers between devices with their start and end apart: 27, of which 15 were waited for; matrix products, arithmetic and copies ran while one was open for 2% of the time, Pallas kernels for 1%

profile of v1, /device:TPU:0, one launch (start us, length us, event | category | flops | bytes accessed | tf_op | source)
XLA Modules:
  0.0 71.5 jit_solution(11327177127764575154)
XLA Ops:
  0.0 0.5 collective-permute-start.1
  0.5 1.2 %copy-done.1 = bf16[1,1,512,1024]{3,2,1,0:T(8,128)(2,1)S(1)} copy-done((bf16[1,1,512,1024]{3,2,1,0:T(8,128)(2,1)S(1)}, bf16[1,1,512,1024]{3,2,1,0:T(8,128)(2,1)}, u32[]{:S(2)}) %copy-start.1) | copy-done | bytes 1048600
  1.7 0.7 copy-done.2
  2.4 0.7 copy-done.3
  3.0 0.4 shard_map.73.refs_3_
  3.5 4.7 %collective-permute-start.16 = (bf16[544,128]{1,0:T(8,128)(2,1)S(1)}, bf16[544,128]{1,0:T(8,128)(2,1)S(1)}, u32[]{:S(2)}, u32[]{:S(2)}) collective-permute-start(bf16[544,128]{1,0:T(8,128)(2,1)S(1)} %shard_map.73.refs_3_), channel_id=1, source_target_pairs={{0,24},{1,25},{2,26},{3,27},{4,28},{5,29},{6,30},{7,31},{8,16},{9,... | collective-permute-start | bytes 417800 | tf_op jit(solution)/shard_map/ppermute | solution.py:115
  8.1 0.6 collective-permute-start.6
  8.8 0.7 pad_add_fusion
  9.5 1.1 %collective-permute-done = s32[7,3]{0,1:T(4,128)S(1)} collective-permute-done((s32[7,3]{0,1:T(4,128)S(1)}, s32[7,3]{0,1:T(4,128)S(1)}, u32[]{:S(2)}, u32[]{:S(2)}) %collective-permute-start) | collective-permute-done | bytes 116 | tf_op jit(solution)/shard_map/ppermute | solution.py:115
  10.7 1.7 %collective-permute-start.3 = (bf16[544,128]{1,0:T(8,128)(2,1)S(1)}, bf16[544,128]{1,0:T(8,128)(2,1)S(1)}, u32[]{:S(2)}, u32[]{:S(2)}) collective-permute-start(bf16[544,128]{1,0:T(8,128)(2,1)S(1)} %shard_map.73.refs_3_), channel_id=1, source_target_pairs={{0,2},{1,3},{2,0},{3,1},{4,6},{5,7},{6,4},{7,5},{8,10},{9,11},{10,... | collective-permute-start | bytes 417800 | tf_op jit(solution)/shard_map/ppermute | solution.py:115
  12.4 0.4 collective-permute-done.16.refs_18_
  12.8 1.6 %collective-permute-start.2 = (bf16[544,128]{1,0:T(8,128)(2,1)S(1)}, bf16[544,128]{1,0:T(8,128)(2,1)S(1)}, u32[]{:S(2)}, u32[]{:S(2)}) collective-permute-start(bf16[544,128]{1,0:T(8,128)(2,1)S(1)} %shard_map.73.refs_3_), channel_id=1, source_target_pairs={{0,4},{1,5},{2,6},{3,7},{4,0},{5,1},{6,2},{7,3},{8,12},{9,13},{10,... | collective-permute-start | bytes 417800 | tf_op jit(solution)/shard_map/ppermute | solution.py:115
  14.4 6.2 %collective-permute-done.11.refs_13_ = bf16[544,128]{1,0:T(8,128)(2,1)S(1)} collective-permute-done((bf16[544,128]{1,0:T(8,128)(2,1)S(1)}, bf16[544,128]{1,0:T(8,128)(2,1)S(1)}, u32[]{:S(2)}, u32[]{:S(2)}) %collective-permute-start.11) | collective-permute-done | bytes 139296 | tf_op jit(solution)/shard_map/ppermute | solution.py:115
  20.6 1.5 %collective-permute-start.18 = (bf16[544,128]{1,0:T(8,128)(2,1)S(1)}, bf16[544,128]{1,0:T(8,128)(2,1)S(1)}, u32[]{:S(2)}, u32[]{:S(2)}) collective-permute-start(bf16[544,128]{1,0:T(8,128)(2,1)S(1)} %collective-permute-done.16.refs_18_), channel_id=1, source_target_pairs={{0,2},{1,3},{2,0},{3,1},{4,6},{5,7},{6,4},{7,5},{8,10},{9,11},{10,... | collective-permute-start | bytes 417800 | tf_op jit(solution)/shard_map/ppermute | solution.py:115
  22.1 1.5 %collective-permute-start.17 = (bf16[544,128]{1,0:T(8,128)(2,1)S(1)}, bf16[544,128]{1,0:T(8,128)(2,1)S(1)}, u32[]{:S(2)}, u32[]{:S(2)}) collective-permute-start(bf16[544,128]{1,0:T(8,128)(2,1)S(1)} %collective-permute-done.16.refs_18_), channel_id=1, source_target_pairs={{0,4},{1,5},{2,6},{3,7},{4,0},{5,1},{6,2},{7,3},{8,12},{9,13},{10,... | collective-permute-start | bytes 417800 | tf_op jit(solution)/shard_map/ppermute | solution.py:115
  23.6 0.8 %pad_add_fusion.1 = s32[14,3]{0,1:T(4,128)S(1)} fusion(s32[7,3]{0,1:T(4,128)S(1)} %collective-permute-done, s32[7,1]{0,1:T(1,128)} %bitcast.19, s32[7,1]{0,1:T(1,128)} %bitcast.21, s32[7,1]{0,1:T(1,128)} %param.11), kind=kLoop, calls=%fused_computation.7 | loop fusion | flops 126 | bytes 336 | tf_op jit(solution)/shard_map/concatenate | solution.py:153
  24.4 0.5 collective-permute-start.13
  24.9 0.5 collective-permute-start.12
  25.4 0.5 collective-permute-done.18.refs_20_
  25.9 2.3 %collective-permute-start.8 = (bf16[544,128]{1,0:T(8,128)(2,1)S(1)}, bf16[544,128]{1,0:T(8,128)(2,1)S(1)}, u32[]{:S(2)}, u32[]{:S(2)}) collective-permute-start(bf16[544,128]{1,0:T(8,128)(2,1)S(1)} %collective-permute-done.6.refs_8_), channel_id=1, source_target_pairs={{0,2},{1,3},{2,0},{3,1},{4,6},{5,7},{6,4},{7,5},{8,10},{9,11},{10,... | collective-permute-start | bytes 417800 | tf_op jit(solution)/shard_map/ppermute | solution.py:115
  28.2 2.0 %collective-permute-start.7 = (bf16[544,128]{1,0:T(8,128)(2,1)S(1)}, bf16[544,128]{1,0:T(8,128)(2,1)S(1)}, u32[]{:S(2)}, u32[]{:S(2)}) collective-permute-start(bf16[544,128]{1,0:T(8,128)(2,1)S(1)} %collective-permute-done.6.refs_8_), channel_id=1, source_target_pairs={{0,4},{1,5},{2,6},{3,7},{4,0},{5,1},{6,2},{7,3},{8,12},{9,13},{10,... | collective-permute-start | bytes 417800 | tf_op jit(solution)/shard_map/ppermute | solution.py:115
  30.3 0.4 collective-permute-done.13.refs_15_
  30.6 0.9 %collective-permute-start.5 = (bf16[272,128]{1,0:T(8,128)(2,1)S(1)}, bf16[272,128]{1,0:T(8,128)(2,1)S(1)}, u32[]{:S(2)}, u32[]{:S(2)}) collective-permute-start(bf16[272,128]{1,0:T(8,128)(2,1)S(1)} %slice.51), channel_id=1, source_target_pairs={{0,4},{1,5},{2,6},{3,7},{4,0},{5,1},{6,2},{7,3},{8,12},{9,13},{10,... | collective-permute-start | bytes 208904 | tf_op jit(solution)/shard_map/ppermute | solution.py:115
  31.5 1.6 %collective-permute-start.4 = (bf16[272,128]{1,0:T(8,128)(2,1)S(1)}, bf16[272,128]{1,0:T(8,128)(2,1)S(1)}, u32[]{:S(2)}, u32[]{:S(2)}) collective-permute-start(bf16[272,128]{1,0:T(8,128)(2,1)S(1)} %slice.50), channel_id=1, source_target_pairs={{0,2},{1,3},{2,0},{3,1},{4,6},{5,7},{6,4},{7,5},{8,10},{9,11},{10,... | collective-permute-start | bytes 208904 | tf_op jit(solution)/shard_map/ppermute | solution.py:115
  33.2 0.8 %collective-permute-start.20 = (bf16[272,128]{1,0:T(8,128)(2,1)S(1)}, bf16[272,128]{1,0:T(8,128)(2,1)S(1)}, u32[]{:S(2)}, u32[]{:S(2)}) collective-permute-start(bf16[272,128]{1,0:T(8,128)(2,1)S(1)} %slice.57), channel_id=1, source_target_pairs={{0,4},{1,5},{2,6},{3,7},{4,0},{5,1},{6,2},{7,3},{8,12},{9,13},{10,... | collective-permute-start | bytes 208904 | tf_op jit(solution)/shard_map/ppermute | solution.py:115
  34.0 0.7 collective-permute-done.7.refs_9_
  34.6 1.4 %collective-permute-start.19 = (bf16[272,128]{1,0:T(8,128)(2,1)S(1)}, bf16[272,128]{1,0:T(8,128)(2,1)S(1)}, u32[]{:S(2)}, u32[]{:S(2)}) collective-permute-start(bf16[272,128]{1,0:T(8,128)(2,1)S(1)} %slice.56), channel_id=1, source_target_pairs={{0,2},{1,3},{2,0},{3,1},{4,6},{5,7},{6,4},{7,5},{8,10},{9,11},{10,... | collective-permute-start | bytes 208904 | tf_op jit(solution)/shard_map/ppermute | solution.py:115
  36.1 0.9 %collective-permute-start.15 = (bf16[272,128]{1,0:T(8,128)(2,1)S(1)}, bf16[272,128]{1,0:T(8,128)(2,1)S(1)}, u32[]{:S(2)}, u32[]{:S(2)}) collective-permute-start(bf16[272,128]{1,0:T(8,128)(2,1)S(1)} %slice.55), channel_id=1, source_target_pairs={{0,4},{1,5},{2,6},{3,7},{4,0},{5,1},{6,2},{7,3},{8,12},{9,13},{10,... | collective-permute-start | bytes 208904 | tf_op jit(solution)/shard_map/ppermute | solution.py:115
  37.0 1.2 %collective-permute-start.14 = (bf16[272,128]{1,0:T(8,128)(2,1)S(1)}, bf16[272,128]{1,0:T(8,128)(2,1)S(1)}, u32[]{:S(2)}, u32[]{:S(2)}) collective-permute-start(bf16[272,128]{1,0:T(8,128)(2,1)S(1)} %slice.54), channel_id=1, source_target_pairs={{0,2},{1,3},{2,0},{3,1},{4,6},{5,7},{6,4},{7,5},{8,10},{9,11},{10,... | collective-permute-start | bytes 208904 | tf_op jit(solution)/shard_map/ppermute | solution.py:115
  38.2 0.6 collective-permute-start.10
  38.8 0.6 collective-permute-done.19.refs_21_
  39.4 1.5 %collective-permute-start.9 = (bf16[272,128]{1,0:T(8,128)(2,1)S(1)}, bf16[272,128]{1,0:T(8,128)(2,1)S(1)}, u32[]{:S(2)}, u32[]{:S(2)}) collective-permute-start(bf16[272,128]{1,0:T(8,128)(2,1)S(1)} %slice.52), channel_id=1, source_target_pairs={{0,2},{1,3},{2,0},{3,1},{4,6},{5,7},{6,4},{7,5},{8,10},{9,11},{10,... | collective-permute-start | bytes 208904 | tf_op jit(solution)/shard_map/ppermute | solution.py:115
  41.0 0.3 collective-permute-done.14.refs_16_
  41.3 1.2 %collective-permute-done.10.refs_12_ = bf16[272,128]{1,0:T(8,128)(2,1)S(1)} collective-permute-done((bf16[272,128]{1,0:T(8,128)(2,1)S(1)}, bf16[272,128]{1,0:T(8,128)(2,1)S(1)}, u32[]{:S(2)}, u32[]{:S(2)}) %collective-permute-start.10) | collective-permute-done | bytes 69664 | tf_op jit(solution)/shard_map/ppermute | solution.py:115
  42.5 1.2 %collective-permute-done.9.refs_11_ = bf16[272,128]{1,0:T(8,128)(2,1)S(1)} collective-permute-done((bf16[272,128]{1,0:T(8,128)(2,1)S(1)}, bf16[272,128]{1,0:T(8,128)(2,1)S(1)}, u32[]{:S(2)}, u32[]{:S(2)}) %collective-permute-start.9) | collective-permute-done | bytes 69664 | tf_op jit(solution)/shard_map/ppermute | solution.py:115
  43.7 2.0 %copy-done = bf16[7,512,512]{2,1,0:T(8,128)(2,1)S(1)} copy-done((bf16[7,512,512]{2,1,0:T(8,128)(2,1)S(1)}, bf16[7,512,512]{2,1,0:T(8,128)(2,1)}, u32[]{:S(2)}) %copy-start) | copy-done | bytes 3670040
  45.8 10.0 %shard_map.74 = f32[2,128,128]{2,1,0:T(8,128)S(1)} custom-call(s32[14,3]{1,0:T(8,128)S(1)} %copy.14.refs_0_, bf16[7,512,512]{2,1,0:T(8,128)(2,1)S(1)} %copy-done, bf16[7,512,512]{2,1,0:T(8,128)(2,1)} %collective-permute-done.1.refs_2_, bf16[544,128]{1,0:T(8,128)(2,1)S(1)} %shard_map.73.refs_3_, bf16[544,128]{1,0:T(8,128)(2,1)S(1)} %collective-permute-done.2.refs_4_, ...), custom_call_target="tpu_custom_call" | custom-call | tf_op jit(solution)/shard_map/pallas_call | solution.py:99
  55.8 1.4 %collective-permute-start.22 = (f32[128,128]{1,0:T(8,128)S(1)}, f32[128,128]{1,0:T(8,128)S(1)}, u32[]{:S(2)}, u32[]{:S(2)}) collective-permute-start(f32[128,128]{1,0:T(8,128)S(1)} %get-tuple-element.6), channel_id=1, source_target_pairs={{0,4},{1,5},{2,6},{3,7},{4,0},{5,1},{6,2},{7,3},{8,12},{9,13},{10,... | collective-permute-start | bytes 196616 | tf_op jit(solution)/shard_map/ppermute | solution.py:115
  57.3 1.6 %collective-permute-start.23 = (f32[128,128]{1,0:T(8,128)S(1)}, f32[128,128]{1,0:T(8,128)S(1)}, u32[]{:S(2)}, u32[]{:S(2)}) collective-permute-start(f32[128,128]{1,0:T(8,128)S(1)} %get-tuple-element.5), channel_id=1, source_target_pairs={{0,6},{1,7},{2,4},{3,5},{4,2},{5,3},{6,0},{7,1},{8,14},{9,15},{10,... | collective-permute-start | bytes 196616 | tf_op jit(solution)/shard_map/ppermute | solution.py:115
  58.9 0.5 collective-permute-start.21
  59.4 0.8 %collective-permute-done.22 = f32[128,128]{1,0:T(8,128)S(1)} collective-permute-done((f32[128,128]{1,0:T(8,128)S(1)}, f32[128,128]{1,0:T(8,128)S(1)}, u32[]{:S(2)}, u32[]{:S(2)}) %collective-permute-start.22) | collective-permute-done | bytes 65568 | tf_op jit(solution)/shard_map/ppermute | solution.py:115
  60.2 2.2 %collective-permute-done.23 = f32[128,128]{1,0:T(8,128)S(1)} collective-permute-done((f32[128,128]{1,0:T(8,128)S(1)}, f32[128,128]{1,0:T(8,128)S(1)}, u32[]{:S(2)}, u32[]{:S(2)}) %collective-permute-start.23) | collective-permute-done | bytes 65568 | tf_op jit(solution)/shard_map/ppermute | solution.py:115
  62.4 0.7 %collective-permute-done.21 = f32[128,128]{1,0:T(8,128)S(1)} collective-permute-done((f32[128,128]{1,0:T(8,128)S(1)}, f32[128,128]{1,0:T(8,128)S(1)}, u32[]{:S(2)}, u32[]{:S(2)}) %collective-permute-start.21) | collective-permute-done | bytes 65568 | tf_op jit(solution)/shard_map/ppermute | solution.py:115
  63.2 2.5 %collective-permute-start.26 = (f32[128,128]{1,0:T(8,128)S(1)}, f32[128,128]{1,0:T(8,128)S(1)}, u32[]{:S(2)}, u32[]{:S(2)}) collective-permute-start(f32[128,128]{1,0:T(8,128)S(1)} %add_add_fusion), channel_id=1, source_target_pairs={{0,24},{1,25},{2,26},{3,27},{4,28},{5,29},{6,30},{7,31},{8,16},{9,... | collective-permute-start | bytes 196616 | tf_op jit(solution)/shard_map/ppermute | solution.py:115
  65.7 1.9 %collective-permute-start.24 = (f32[128,128]{1,0:T(8,128)S(1)}, f32[128,128]{1,0:T(8,128)S(1)}, u32[]{:S(2)}, u32[]{:S(2)}) collective-permute-start(f32[128,128]{1,0:T(8,128)S(1)} %add_add_fusion), channel_id=1, source_target_pairs={{0,8},{1,9},{2,10},{3,11},{4,12},{5,13},{6,14},{7,15},{8,0},{9,1},... | collective-permute-start | bytes 196616 | tf_op jit(solution)/shard_map/ppermute | solution.py:115
  67.6 1.7 %collective-permute-done.26 = f32[128,128]{1,0:T(8,128)S(1)} collective-permute-done((f32[128,128]{1,0:T(8,128)S(1)}, f32[128,128]{1,0:T(8,128)S(1)}, u32[]{:S(2)}, u32[]{:S(2)}) %collective-permute-start.26) | collective-permute-done | bytes 65568 | tf_op jit(solution)/shard_map/ppermute | solution.py:115
  69.3 1.6 %collective-permute-done.25 = f32[128,128]{1,0:T(8,128)S(1)} collective-permute-done((f32[128,128]{1,0:T(8,128)S(1)}, f32[128,128]{1,0:T(8,128)S(1)}, u32[]{:S(2)}, u32[]{:S(2)}) %collective-permute-start.25) | collective-permute-done | bytes 65568 | tf_op jit(solution)/shard_map/ppermute | solution.py:115
  70.9 0.6 add_bitcast_fusion
  (33 shorter events, 0.3 us)
Async XLA Ops:
  0.0 43.7 %collective-permute-start.1 = (bf16[7,512,512]{2,1,0:T(8,128)(2,1)}, bf16[7,512,512]{2,1,0:T(8,128)(2,1)}, u32[]{:S(2)}, u32[]{:S(2)}) collective-permute-start(bf16[7,512,512]{2,1,0:T(8,128)(2,1)} %refs_1_.1), channel_id=1, source_target_pairs={{0,1},{1,0},{2,3},{3,2},{4,5},{5,4},{6,7},{7,6},{8,9},{9,8},{10,11... | collective-permute-start | bytes 11010056 | tf_op jit(solution)/shard_map/ppermute | solution.py:115
  0.5 1.2 %copy-start.1 = (bf16[1,1,512,1024]{3,2,1,0:T(8,128)(2,1)S(1)}, bf16[1,1,512,1024]{3,2,1,0:T(8,128)(2,1)}, u32[]{:S(2)}) copy-start(bf16[1,1,512,1024]{3,2,1,0:T(8,128)(2,1)} %param.7) | copy-start | bytes 3145732
  1.7 0.7 copy-start.2
  2.4 0.7 copy-start.3
  3.5 9.3 %collective-permute-start.16 = (bf16[544,128]{1,0:T(8,128)(2,1)S(1)}, bf16[544,128]{1,0:T(8,128)(2,1)S(1)}, u32[]{:S(2)}, u32[]{:S(2)}) collective-permute-start(bf16[544,128]{1,0:T(8,128)(2,1)S(1)} %shard_map.73.refs_3_), channel_id=1, source_target_pairs={{0,24},{1,25},{2,26},{3,27},{4,28},{5,29},{6,30},{7,31},{8,16},{9,... | collective-permute-start | bytes 417800 | tf_op jit(solution)/shard_map/ppermute | solution.py:115
  8.1 12.4 %collective-permute-start.11 = (bf16[544,128]{1,0:T(8,128)(2,1)S(1)}, bf16[544,128]{1,0:T(8,128)(2,1)S(1)}, u32[]{:S(2)}, u32[]{:S(2)}) collective-permute-start(bf16[544,128]{1,0:T(8,128)(2,1)S(1)} %shard_map.73.refs_3_), channel_id=1, source_target_pairs={{0,16},{1,17},{2,18},{3,19},{4,20},{5,21},{6,22},{7,23},{8,24},{9,... | collective-permute-start | bytes 417800 | tf_op jit(solution)/shard_map/ppermute | solution.py:115
  8.1 14.0 %collective-permute-start.6 = (bf16[544,128]{1,0:T(8,128)(2,1)S(1)}, bf16[544,128]{1,0:T(8,128)(2,1)S(1)}, u32[]{:S(2)}, u32[]{:S(2)}) collective-permute-start(bf16[544,128]{1,0:T(8,128)(2,1)S(1)} %shard_map.73.refs_3_), channel_id=1, source_target_pairs={{0,8},{1,9},{2,10},{3,11},{4,12},{5,13},{6,14},{7,15},{8,0},{9,1},... | collective-permute-start | bytes 417800 | tf_op jit(solution)/shard_map/ppermute | solution.py:115
  9.5 1.2 %collective-permute-start = (s32[7,3]{0,1:T(4,128)S(1)}, s32[7,3]{0,1:T(4,128)S(1)}, u32[]{:S(2)}, u32[]{:S(2)}) collective-permute-start(s32[7,3]{0,1:T(4,128)S(1)} %pad_add_fusion), channel_id=1, source_target_pairs={{0,1},{1,0},{2,3},{3,2},{4,5},{5,4},{6,7},{7,6},{8,9},{9,8},{10,11... | collective-permute-start | bytes 260 | tf_op jit(solution)/shard_map/ppermute | solution.py:115
  10.7 13.7 %collective-permute-start.3 = (bf16[544,128]{1,0:T(8,128)(2,1)S(1)}, bf16[544,128]{1,0:T(8,128)(2,1)S(1)}, u32[]{:S(2)}, u32[]{:S(2)}) collective-permute-start(bf16[544,128]{1,0:T(8,128)(2,1)S(1)} %shard_map.73.refs_3_), channel_id=1, source_target_pairs={{0,2},{1,3},{2,0},{3,1},{4,6},{5,7},{6,4},{7,5},{8,10},{9,11},{10,... | collective-permute-start | bytes 417800 | tf_op jit(solution)/shard_map/ppermute | solution.py:115
  12.8 12.1 %collective-permute-start.2 = (bf16[544,128]{1,0:T(8,128)(2,1)S(1)}, bf16[544,128]{1,0:T(8,128)(2,1)S(1)}, u32[]{:S(2)}, u32[]{:S(2)}) collective-permute-start(bf16[544,128]{1,0:T(8,128)(2,1)S(1)} %shard_map.73.refs_3_), channel_id=1, source_target_pairs={{0,4},{1,5},{2,6},{3,7},{4,0},{5,1},{6,2},{7,3},{8,12},{9,13},{10,... | collective-permute-start | bytes 417800 | tf_op jit(solution)/shard_map/ppermute | solution.py:115
  20.6 5.3 %collective-permute-start.18 = (bf16[544,128]{1,0:T(8,128)(2,1)S(1)}, bf16[544,128]{1,0:T(8,128)(2,1)S(1)}, u32[]{:S(2)}, u32[]{:S(2)}) collective-permute-start(bf16[544,128]{1,0:T(8,128)(2,1)S(1)} %collective-permute-done.16.refs_18_), channel_id=1, source_target_pairs={{0,2},{1,3},{2,0},{3,1},{4,6},{5,7},{6,4},{7,5},{8,10},{9,11},{10,... | collective-permute-start | bytes 417800 | tf_op jit(solution)/shard_map/ppermute | solution.py:115
  22.1 6.1 %collective-permute-start.17 = (bf16[544,128]{1,0:T(8,128)(2,1)S(1)}, bf16[544,128]{1,0:T(8,128)(2,1)S(1)}, u32[]{:S(2)}, u32[]{:S(2)}) collective-permute-start(bf16[544,128]{1,0:T(8,128)(2,1)S(1)} %collective-permute-done.16.refs_18_), channel_id=1, source_target_pairs={{0,4},{1,5},{2,6},{3,7},{4,0},{5,1},{6,2},{7,3},{8,12},{9,13},{10,... | collective-permute-start | bytes 417800 | tf_op jit(solution)/shard_map/ppermute | solution.py:115
  24.4 6.2 %collective-permute-start.13 = (bf16[544,128]{1,0:T(8,128)(2,1)S(1)}, bf16[544,128]{1,0:T(8,128)(2,1)S(1)}, u32[]{:S(2)}, u32[]{:S(2)}) collective-permute-start(bf16[544,128]{1,0:T(8,128)(2,1)S(1)} %collective-permute-done.11.refs_13_), channel_id=1, source_target_pairs={{0,2},{1,3},{2,0},{3,1},{4,6},{5,7},{6,4},{7,5},{8,10},{9,11},{10,... | collective-permute-start | bytes 417800 | tf_op jit(solution)/shard_map/ppermute | solution.py:115
  24.9 6.6 %collective-permute-start.12 = (bf16[544,128]{1,0:T(8,128)(2,1)S(1)}, bf16[544,128]{1,0:T(8,128)(2,1)S(1)}, u32[]{:S(2)}, u32[]{:S(2)}) collective-permute-start(bf16[544,128]{1,0:T(8,128)(2,1)S(1)} %collective-permute-done.11.refs_13_), channel_id=1, source_target_pairs={{0,4},{1,5},{2,6},{3,7},{4,0},{5,1},{6,2},{7,3},{8,12},{9,13},{10,... | collective-permute-start | bytes 417800 | tf_op jit(solution)/shard_map/ppermute | solution.py:115
  25.9 7.3 %collective-permute-start.8 = (bf16[544,128]{1,0:T(8,128)(2,1)S(1)}, bf16[544,128]{1,0:T(8,128)(2,1)S(1)}, u32[]{:S(2)}, u32[]{:S(2)}) collective-permute-start(bf16[544,128]{1,0:T(8,128)(2,1)S(1)} %collective-permute-done.6.refs_8_), channel_id=1, source_target_pairs={{0,2},{1,3},{2,0},{3,1},{4,6},{5,7},{6,4},{7,5},{8,10},{9,11},{10,... | collective-permute-start | bytes 417800 | tf_op jit(solution)/shard_map/ppermute | solution.py:115
  28.2 6.4 %collective-permute-start.7 = (bf16[544,128]{1,0:T(8,128)(2,1)S(1)}, bf16[544,128]{1,0:T(8,128)(2,1)S(1)}, u32[]{:S(2)}, u32[]{:S(2)}) collective-permute-start(bf16[544,128]{1,0:T(8,128)(2,1)S(1)} %collective-permute-done.6.refs_8_), channel_id=1, source_target_pairs={{0,4},{1,5},{2,6},{3,7},{4,0},{5,1},{6,2},{7,3},{8,12},{9,13},{10,... | collective-permute-start | bytes 417800 | tf_op jit(solution)/shard_map/ppermute | solution.py:115
  30.6 5.5 %collective-permute-start.5 = (bf16[272,128]{1,0:T(8,128)(2,1)S(1)}, bf16[272,128]{1,0:T(8,128)(2,1)S(1)}, u32[]{:S(2)}, u32[]{:S(2)}) collective-permute-start(bf16[272,128]{1,0:T(8,128)(2,1)S(1)} %slice.51), channel_id=1, source_target_pairs={{0,4},{1,5},{2,6},{3,7},{4,0},{5,1},{6,2},{7,3},{8,12},{9,13},{10,... | collective-permute-start | bytes 208904 | tf_op jit(solution)/shard_map/ppermute | solution.py:115
  31.5 5.5 %collective-permute-start.4 = (bf16[272,128]{1,0:T(8,128)(2,1)S(1)}, bf16[272,128]{1,0:T(8,128)(2,1)S(1)}, u32[]{:S(2)}, u32[]{:S(2)}) collective-permute-start(bf16[272,128]{1,0:T(8,128)(2,1)S(1)} %slice.50), channel_id=1, source_target_pairs={{0,2},{1,3},{2,0},{3,1},{4,6},{5,7},{6,4},{7,5},{8,10},{9,11},{10,... | collective-permute-start | bytes 208904 | tf_op jit(solution)/shard_map/ppermute | solution.py:115
  33.2 5.1 %collective-permute-start.20 = (bf16[272,128]{1,0:T(8,128)(2,1)S(1)}, bf16[272,128]{1,0:T(8,128)(2,1)S(1)}, u32[]{:S(2)}, u32[]{:S(2)}) collective-permute-start(bf16[272,128]{1,0:T(8,128)(2,1)S(1)} %slice.57), channel_id=1, source_target_pairs={{0,4},{1,5},{2,6},{3,7},{4,0},{5,1},{6,2},{7,3},{8,12},{9,13},{10,... | collective-permute-start | bytes 208904 | tf_op jit(solution)/shard_map/ppermute | solution.py:115
  34.6 4.8 %collective-permute-start.19 = (bf16[272,128]{1,0:T(8,128)(2,1)S(1)}, bf16[272,128]{1,0:T(8,128)(2,1)S(1)}, u32[]{:S(2)}, u32[]{:S(2)}) collective-permute-start(bf16[272,128]{1,0:T(8,128)(2,1)S(1)} %slice.56), channel_id=1, source_target_pairs={{0,2},{1,3},{2,0},{3,1},{4,6},{5,7},{6,4},{7,5},{8,10},{9,11},{10,... | collective-permute-start | bytes 208904 | tf_op jit(solution)/shard_map/ppermute | solution.py:115
  36.1 5.0 %collective-permute-start.15 = (bf16[272,128]{1,0:T(8,128)(2,1)S(1)}, bf16[272,128]{1,0:T(8,128)(2,1)S(1)}, u32[]{:S(2)}, u32[]{:S(2)}) collective-permute-start(bf16[272,128]{1,0:T(8,128)(2,1)S(1)} %slice.55), channel_id=1, source_target_pairs={{0,4},{1,5},{2,6},{3,7},{4,0},{5,1},{6,2},{7,3},{8,12},{9,13},{10,... | collective-permute-start | bytes 208904 | tf_op jit(solution)/shard_map/ppermute | solution.py:115
  37.0 4.3 %collective-permute-start.14 = (bf16[272,128]{1,0:T(8,128)(2,1)S(1)}, bf16[272,128]{1,0:T(8,128)(2,1)S(1)}, u32[]{:S(2)}, u32[]{:S(2)}) collective-permute-start(bf16[272,128]{1,0:T(8,128)(2,1)S(1)} %slice.54), channel_id=1, source_target_pairs={{0,2},{1,3},{2,0},{3,1},{4,6},{5,7},{6,4},{7,5},{8,10},{9,11},{10,... | collective-permute-start | bytes 208904 | tf_op jit(solution)/shard_map/ppermute | solution.py:115
  38.2 4.3 %collective-permute-start.10 = (bf16[272,128]{1,0:T(8,128)(2,1)S(1)}, bf16[272,128]{1,0:T(8,128)(2,1)S(1)}, u32[]{:S(2)}, u32[]{:S(2)}) collective-permute-start(bf16[272,128]{1,0:T(8,128)(2,1)S(1)} %slice.53), channel_id=1, source_target_pairs={{0,4},{1,5},{2,6},{3,7},{4,0},{5,1},{6,2},{7,3},{8,12},{9,13},{10,... | collective-permute-start | bytes 208904 | tf_op jit(solution)/shard_map/ppermute | solution.py:115
  39.4 4.3 %collective-permute-start.9 = (bf16[272,128]{1,0:T(8,128)(2,1)S(1)}, bf16[272,128]{1,0:T(8,128)(2,1)S(1)}, u32[]{:S(2)}, u32[]{:S(2)}) collective-permute-start(bf16[272,128]{1,0:T(8,128)(2,1)S(1)} %slice.52), channel_id=1, source_target_pairs={{0,2},{1,3},{2,0},{3,1},{4,6},{5,7},{6,4},{7,5},{8,10},{9,11},{10,... | collective-permute-start | bytes 208904 | tf_op jit(solution)/shard_map/ppermute | solution.py:115
  43.7 2.0 %copy-start = (bf16[7,512,512]{2,1,0:T(8,128)(2,1)S(1)}, bf16[7,512,512]{2,1,0:T(8,128)(2,1)}, u32[]{:S(2)}) copy-start(bf16[7,512,512]{2,1,0:T(8,128)(2,1)} %refs_1_.1) | copy-start | bytes 11010052
  55.8 4.3 %collective-permute-start.22 = (f32[128,128]{1,0:T(8,128)S(1)}, f32[128,128]{1,0:T(8,128)S(1)}, u32[]{:S(2)}, u32[]{:S(2)}) collective-permute-start(f32[128,128]{1,0:T(8,128)S(1)} %get-tuple-element.6), channel_id=1, source_target_pairs={{0,4},{1,5},{2,6},{3,7},{4,0},{5,1},{6,2},{7,3},{8,12},{9,13},{10,... | collective-permute-start | bytes 196616 | tf_op jit(solution)/shard_map/ppermute | solution.py:115
  57.3 5.2 %collective-permute-start.23 = (f32[128,128]{1,0:T(8,128)S(1)}, f32[128,128]{1,0:T(8,128)S(1)}, u32[]{:S(2)}, u32[]{:S(2)}) collective-permute-start(f32[128,128]{1,0:T(8,128)S(1)} %get-tuple-element.5), channel_id=1, source_target_pairs={{0,6},{1,7},{2,4},{3,5},{4,2},{5,3},{6,0},{7,1},{8,14},{9,15},{10,... | collective-permute-start | bytes 196616 | tf_op jit(solution)/shard_map/ppermute | solution.py:115
  58.9 4.3 %collective-permute-start.21 = (f32[128,128]{1,0:T(8,128)S(1)}, f32[128,128]{1,0:T(8,128)S(1)}, u32[]{:S(2)}, u32[]{:S(2)}) collective-permute-start(f32[128,128]{1,0:T(8,128)S(1)} %get-tuple-element.5), channel_id=1, source_target_pairs={{0,2},{1,3},{2,0},{3,1},{4,6},{5,7},{6,4},{7,5},{8,10},{9,11},{10,... | collective-permute-start | bytes 196616 | tf_op jit(solution)/shard_map/ppermute | solution.py:115
  63.2 6.1 %collective-permute-start.26 = (f32[128,128]{1,0:T(8,128)S(1)}, f32[128,128]{1,0:T(8,128)S(1)}, u32[]{:S(2)}, u32[]{:S(2)}) collective-permute-start(f32[128,128]{1,0:T(8,128)S(1)} %add_add_fusion), channel_id=1, source_target_pairs={{0,24},{1,25},{2,26},{3,27},{4,28},{5,29},{6,30},{7,31},{8,16},{9,... | collective-permute-start | bytes 196616 | tf_op jit(solution)/shard_map/ppermute | solution.py:115
  65.7 5.2 %collective-permute-start.25 = (f32[128,128]{1,0:T(8,128)S(1)}, f32[128,128]{1,0:T(8,128)S(1)}, u32[]{:S(2)}, u32[]{:S(2)}) collective-permute-start(f32[128,128]{1,0:T(8,128)S(1)} %add_add_fusion), channel_id=1, source_target_pairs={{0,16},{1,17},{2,18},{3,19},{4,20},{5,21},{6,22},{7,23},{8,24},{9,... | collective-permute-start | bytes 196616 | tf_op jit(solution)/shard_map/ppermute | solution.py:115
  65.7 5.2 %collective-permute-start.24 = (f32[128,128]{1,0:T(8,128)S(1)}, f32[128,128]{1,0:T(8,128)S(1)}, u32[]{:S(2)}, u32[]{:S(2)}) collective-permute-start(f32[128,128]{1,0:T(8,128)S(1)} %add_add_fusion), channel_id=1, source_target_pairs={{0,8},{1,9},{2,10},{3,11},{4,12},{5,13},{6,14},{7,15},{8,0},{9,1},... | collective-permute-start | bytes 196616 | tf_op jit(solution)/shard_map/ppermute | solution.py:115

commit v2 on v1

v2 whole, which is shorter than its diff:
```python
import jax
import jax.numpy as jnp
from jax import lax
from jax.experimental import pallas as pl
from jax.experimental.pallas import tpu as pltpu
from jax.sharding import PartitionSpec as P

AXES = ("grp", "reg")
CAP = 2
CHUNKS = 4
VMEM_LIMIT = 48 * 1024 * 1024


def in_hbm(array):
    return pltpu.with_memory_space_constraint(array, pltpu.HBM)


def in_vmem(array):
    return pltpu.with_memory_space_constraint(array, pltpu.VMEM)


def pack_kernel(index_hbm, orbitals_hbm, occupied_hbm, packed_ref, index, orbitals, occupied, sems):
    points, orbs = orbitals.shape
    width = index.shape[1]
    step = points // CHUNKS
    copies = [
        pltpu.make_async_copy(index_hbm, index, sems.at[CHUNKS + 1]),
        pltpu.make_async_copy(occupied_hbm, occupied, sems.at[CHUNKS]),
    ]
    for n in range(CHUNKS):
        rows = pl.ds(n * step, step)
        copies.append(pltpu.make_async_copy(orbitals_hbm.at[rows], orbitals.at[rows], sems.at[n]))
    for copy in copies:
        copy.start()
    copies[0].wait()
    numbers = lax.broadcasted_iota(jnp.int32, (orbs, width), 0)
    chosen = jnp.where(numbers == index[...], 1.0, 0.0).astype(jnp.bfloat16)
    copies[1].wait()
    occ = occupied[...].astype(jnp.float32)
    slabs = [occ[:, at : at + width] for at in range(0, points, width)]
    packed_ref[points:, :] = jnp.concatenate(slabs, axis=0).astype(jnp.bfloat16)
    for n in range(CHUNKS):
        copies[2 + n].wait()
        rows = slice(n * step, n * step + step)
        panel = jnp.dot(orbitals[rows, :], chosen, preferred_element_type=jnp.float32)
        packed_ref[rows, :] = panel.astype(jnp.bfloat16)


def pack(panel_index, orbitals, occupied):
    points = orbitals.shape[0]
    width = panel_index.shape[0]
    occ_rows = occupied.shape[0] * points // width
    return pl.pallas_call(
        pack_kernel,
        out_shape=pltpu.VMEM((points + occ_rows, width), jnp.bfloat16),
        out_specs=pl.BlockSpec(memory_space=pltpu.VMEM),
        in_specs=[pl.BlockSpec(memory_space=pltpu.HBM)] * 3,
        scratch_shapes=[
            pltpu.VMEM((1, width), jnp.int32),
            pltpu.VMEM(orbitals.shape, jnp.bfloat16),
            pltpu.VMEM(occupied.shape, jnp.bfloat16),
            pltpu.SemaphoreType.DMA((CHUNKS + 2,)),
        ],
        compiler_params=pltpu.CompilerParams(vmem_limit_bytes=VMEM_LIMIT),
    )(in_hbm(panel_index[None, :]), in_hbm(orbitals), in_hbm(occupied))


def collect_kernel(codes_ref, own_hbm, other_hbm, labels_ref, blocks_ref, sems):
    groups, regions = lax.axis_size("grp"), lax.axis_size("reg")
    reg = lax.axis_index("reg")
    me = lax.axis_index("grp") * regions + reg
    held = own_hbm.shape[0]
    slots = blocks_ref.shape[0]

    def block_copy(source, n, at):
        return pltpu.make_async_copy(source.at[n], blocks_ref.at[at], sems.at[at])

    for at in range(slots):
        labels_ref[at, 0] = -1
        labels_ref[at, 1] = 0
        labels_ref[at, 2] = 0
    used = jnp.int32(0)
    for source, first in ((own_hbm, 0), (other_hbm, held)):
        for n in range(held):
            code = codes_ref[first + n]
            region = code % regions
            row = code // regions % groups
            col = code // (regions * groups)
            wanted = (region ^ reg) % 2 == 0

            @pl.when(wanted)
            def _():
                labels_ref[used, 0] = (region ^ reg) // 2
                labels_ref[used, 1] = ((row * regions + region) ^ me) // 2
                labels_ref[used, 2] = ((col * regions + region) ^ me) // 2
                block_copy(source, n, used).start()

            used = used + wanted.astype(jnp.int32)
    for at in range(slots):

        @pl.when(at < used)
        def _():
            block_copy(own_hbm, 0, at).wait()


def collect(codes, own, other, regions):
    held = own.shape[0]
    slots = min(2 * held, 2 * CAP * regions)
    return pl.pallas_call(
        collect_kernel,
        out_shape=(
            pltpu.SMEM((slots, 3), jnp.int32),
            pltpu.VMEM((slots,) + own.shape[1:], jnp.bfloat16),
        ),
        in_specs=[pl.BlockSpec(memory_space=pltpu.SMEM)]
        + [pl.BlockSpec(memory_space=pltpu.HBM)] * 2,
        out_specs=(
            pl.BlockSpec(memory_space=pltpu.SMEM),
            pl.BlockSpec(memory_space=pltpu.VMEM),
        ),
        scratch_shapes=[pltpu.SemaphoreType.DMA((slots,))],
        compiler_params=pltpu.CompilerParams(vmem_limit_bytes=VMEM_LIMIT),
    )(codes, in_hbm(own), in_hbm(other))


def sigma_kernel(places, points, occ_count, labels_ref, blocks, *refs):
    piece_refs = refs[: len(places)]
    out_ref, packed, dressed, screened = refs[len(places) :]
    slots = blocks.shape[0]
    out_ref[...] = jnp.zeros_like(out_ref)
    for n, place in enumerate(places):
        packed[place] = piece_refs[n][...]

    def occupied_of(slot):
        rows = packed[slot, points:, :].astype(jnp.float32)
        slabs = [rows[at : at + occ_count] for at in range(0, rows.shape[0], occ_count)]
        return jnp.concatenate(slabs, axis=1).astype(jnp.bfloat16)

    transposed = (((0,), (0,)), ((), ()))
    for at in range(slots):
        row, col = labels_ref[at, 1], labels_ref[at, 2]
        overlap = lax.dot_general(
            occupied_of(row), occupied_of(col), transposed, preferred_element_type=jnp.float32
        )
        dressed[at] = (blocks[at].astype(jnp.float32) * overlap).astype(jnp.bfloat16)
    for at in range(slots):
        col = labels_ref[at, 2]
        screened[at] = jnp.dot(
            dressed[at], packed[col, :points, :], preferred_element_type=jnp.float32
        ).astype(jnp.bfloat16)
    for at in range(slots):
        place, row = labels_ref[at, 0], labels_ref[at, 1]
        product = lax.dot_general(
            packed[row, :points, :], screened[at], transposed, preferred_element_type=jnp.float32
        )
        out_ref[jnp.maximum(place, 0)] += jnp.where(place >= 0, product, 0.0)


def partial_sigma(labels, blocks, found, regions, points, occ_count):
    arrays = [array for _, array in found]
    places = [mask // 2 for mask, _ in found]
    rows, width = arrays[0].shape
    slots = blocks.shape[0]
    return pl.pallas_call(
        lambda *refs: sigma_kernel(places, points, occ_count, *refs),
        out_shape=pltpu.VMEM((regions, width, width), jnp.float32),
        in_specs=[pl.BlockSpec(memory_space=pltpu.SMEM)]
        + [pl.BlockSpec(memory_space=pltpu.VMEM)] * (1 + len(arrays)),
        out_specs=pl.BlockSpec(memory_space=pltpu.VMEM),
        scratch_shapes=[
            pltpu.VMEM((len(arrays), rows, width), jnp.bfloat16),
            pltpu.VMEM((slots, points, points), jnp.bfloat16),
            pltpu.VMEM((slots, points, width), jnp.bfloat16),
        ],
        compiler_params=pltpu.CompilerParams(vmem_limit_bytes=VMEM_LIMIT),
    )(
        pltpu.with_memory_space_constraint(labels, pltpu.SMEM),
        in_vmem(blocks),
        *[in_vmem(array) for array in arrays],
    )


def swap(array, mask, count):
    return lax.ppermute(array, AXES, [(i, i ^ mask) for i in range(count)])


def gather(packed, count, first_bit):
    bits = []
    while first_bit < count:
        bits.append(first_bit)
        first_bit *= 2
    y, x = bits[0], bits[1]
    column = [(0, packed)]
    for mask in range(bits[2], count, bits[2]):
        column.append((mask, swap(packed, mask, count)))
    found = []
    earlier = []
    for n, (mask, array) in enumerate(column):
        if n >= 2:
            array, _ = lax.optimization_barrier((array, earlier[n - 2]))
        over_x, over_y = swap(array, x, count), swap(array, y, count)
        corner = swap(over_x, y, count) if n % 2 else swap(over_y, x, count)
        earlier.append(corner)
        found += [(mask, array), (mask ^ x, over_x), (mask ^ y, over_y), (mask ^ x ^ y, corner)]
    return found


def total(values):
    while len(values) > 1:
        values = [values[n] + values[n + 1] for n in range(0, len(values), 2)]
    return values[0]


def shards(orbitals, occupied, panel_index, screening, block_region, block_row, block_col):
    groups, regions = lax.axis_size("grp"), lax.axis_size("reg")
    count = groups * regions
    points, occ_count = screening.shape[1], occupied.shape[2]

    other = swap(screening, 1, count)
    packed = pack(panel_index, orbitals[0, 0], occupied[0, 0])
    found = gather(packed, count, 2)
    codes = (block_col * groups + block_row) * regions + block_region[:, 0]
    codes = jnp.concatenate([codes, swap(codes, 1, count)])
    labels, blocks = collect(codes, screening, other, regions // 2)
    sums = partial_sigma(labels, blocks, found, regions // 2, points, occ_count)
    stage = []
    for low in (0, regions):
        for mask in range(0, regions, 2):
            part = sums[mask // 2]
            stage.append(swap(part, low ^ mask, count) if low ^ mask else part)
    sigma = total(stage)
    bit = 2 * regions
    while bit < count:
        top = min(4 * bit, count)
        sigma = total([sigma] + [swap(sigma, mask, count) for mask in range(bit, top, bit)])
        bit = top
    return sigma[None]


def solution(mesh):
    in_specs = (
        P("reg", "grp", None, None),
        P("reg", "grp", None, None),
        P(),
        P(("grp", "reg"), None, None),
        P(("grp", "reg"), None),
        P(("grp", "reg")),
        P(("grp", "reg")),
    )
    out_specs = P("reg", None, None)
    return jax.shard_map(shards, mesh=mesh, in_specs=in_specs, out_specs=out_specs, check_vma=False)
```

time: 71.8 us -> 59.8 us (0.83)
  starting transfers between devices: 34.4 us -> 27.5 us
  local copies, waits for them, and re-layouts: 4.78 us -> 1.2 us
  Pallas kernels: 10.5 us -> 7.6 us
  waiting for transfers between devices: 19.5 us -> 21.9 us
  other arithmetic: 2.15 us -> 1.43 us
    ppermute x27 -> x23, starting transfers between devices: 34.4 us -> 27.5 us  [swap(): return lax.ppermute(array, AXES, [(i, i ^ mask) for i in range(count)])]
    unnamed x8 -> x2, local copies, waits for them, and re-layouts: 4.61 us -> 1.19 us
    pallas_call x2 -> x3, Pallas kernels: 10.5 us -> 7.6 us  [the longest x1 2.91 us: collect(): pl.pallas_call(collect_kernel, out_shape=(pltpu.SMEM((slots, 3), jnp.int3...]
    ppermute x27 -> x23, waiting for transfers between devices: 19.5 us -> 21.9 us  [swap(): return lax.ppermute(array, AXES, [(i, i ^ mask) for i in range(count)])]
  transfers between devices with their start and end apart: 27 -> 23, of which waited for: 15 -> 11; matrix products, arithmetic and copies ran while one was open for 2% -> 1% of each run, Pallas kernels for 1% -> 8%
where the time goes in v2:
time: 59.8 us; the launch traced here: 59.6 us
  starting transfers between devices  27.5 us (46%)
  waiting for transfers between devices  21.9 us (37%)
  Pallas kernels  7.6 us (13%)
  other arithmetic  1.43 us (2%)
  local copies, waits for them, and re-layouts  1.2 us (2%)
    ppermute x23, starting transfers between devices, swap(): return lax.ppermute(array, AXES, [(i, i ^ mask) for i in range(count)])  27.5 us
    ppermute x23, waiting for transfers between devices, swap(): return lax.ppermute(array, AXES, [(i, i ^ mask) for i in range(count)])  21.9 us
    pallas_call x1, Pallas kernels, collect(): pl.pallas_call(collect_kernel, out_shape=(pltpu.SMEM((slots, 3), jnp.int3...  2.91 us
    pallas_call x1, Pallas kernels, partial_sigma(): pl.pallas_call(lambda *refs: sigma_kernel(places, points, occ_count, *ref...  2.8 us
    pallas_call x1, Pallas kernels, pack(): pl.pallas_call(pack_kernel, out_shape=pltpu.VMEM((points + occ_rows, widt...  1.9 us
  transfers between devices with their start and end apart: 23, of which 11 were waited for; matrix products, arithmetic and copies ran while one was open for 1% of the time, Pallas kernels for 8%

profile of v2, /device:TPU:0, one launch (start us, length us, event | category | flops | bytes accessed | tf_op | source)
XLA Modules:
  0.0 59.6 jit_solution(1121685731108486662)
XLA Ops:
  0.0 0.5 collective-permute-start.1
  0.5 1.9 %shard_map.74.refs_2_ = bf16[544,128]{1,0:T(8,128)(2,1)S(1)} custom-call(s32[1,128]{1,0:T(1,128)} %bitcast.15, bf16[512,1024]{1,0:T(8,128)(2,1)} %bitcast.13, bf16[8,512]{1,0:T(8,128)(2,1)} %bitcast.14), custom_call_target="tpu_custom_call" | custom-call | tf_op jit(solution)/shard_map/pallas_call | solution.py:53
  2.4 2.6 %collective-permute-start.5 = (bf16[544,128]{1,0:T(8,128)(2,1)S(1)}, bf16[544,128]{1,0:T(8,128)(2,1)S(1)}, u32[]{:S(2)}, u32[]{:S(2)}) collective-permute-start(bf16[544,128]{1,0:T(8,128)(2,1)S(1)} %shard_map.74.refs_2_), channel_id=1, source_target_pairs={{0,8},{1,9},{2,10},{3,11},{4,12},{5,13},{6,14},{7,15},{8,0},{9,1},... | collective-permute-start | bytes 417800 | tf_op jit(solution)/shard_map/ppermute | solution.py:184
  5.0 1.5 %collective-permute-start.3 = (bf16[544,128]{1,0:T(8,128)(2,1)S(1)}, bf16[544,128]{1,0:T(8,128)(2,1)S(1)}, u32[]{:S(2)}, u32[]{:S(2)}) collective-permute-start(bf16[544,128]{1,0:T(8,128)(2,1)S(1)} %shard_map.74.refs_2_), channel_id=1, source_target_pairs={{0,2},{1,3},{2,0},{3,1},{4,6},{5,7},{6,4},{7,5},{8,10},{9,11},{10,... | collective-permute-start | bytes 417800 | tf_op jit(solution)/shard_map/ppermute | solution.py:184
  6.5 2.8 %collective-permute-done.5.refs_6_ = bf16[544,128]{1,0:T(8,128)(2,1)S(1)} collective-permute-done((bf16[544,128]{1,0:T(8,128)(2,1)S(1)}, bf16[544,128]{1,0:T(8,128)(2,1)S(1)}, u32[]{:S(2)}, u32[]{:S(2)}) %collective-permute-start.5) | collective-permute-done | bytes 139296 | tf_op jit(solution)/shard_map/ppermute | solution.py:184
  9.3 1.7 %collective-permute-start.6 = (bf16[544,128]{1,0:T(8,128)(2,1)S(1)}, bf16[544,128]{1,0:T(8,128)(2,1)S(1)}, u32[]{:S(2)}, u32[]{:S(2)}) collective-permute-start(bf16[544,128]{1,0:T(8,128)(2,1)S(1)} %collective-permute-done.5.refs_6_), channel_id=1, source_target_pairs={{0,4},{1,5},{2,6},{3,7},{4,0},{5,1},{6,2},{7,3},{8,12},{9,13},{10,... | collective-permute-start | bytes 417800 | tf_op jit(solution)/shard_map/ppermute | solution.py:184
  11.0 2.6 %collective-permute-start.9 = (bf16[544,128]{1,0:T(8,128)(2,1)S(1)}, bf16[544,128]{1,0:T(8,128)(2,1)S(1)}, u32[]{:S(2)}, u32[]{:S(2)}) collective-permute-start(bf16[544,128]{1,0:T(8,128)(2,1)S(1)} %shard_map.74.refs_2_), channel_id=1, source_target_pairs={{0,16},{1,17},{2,18},{3,19},{4,20},{5,21},{6,22},{7,23},{8,24},{9,... | collective-permute-start | bytes 417800 | tf_op jit(solution)/shard_map/ppermute | solution.py:184
  13.6 0.5 collective-permute-start.4
  14.1 1.3 %collective-permute-start.13 = (bf16[544,128]{1,0:T(8,128)(2,1)S(1)}, bf16[544,128]{1,0:T(8,128)(2,1)S(1)}, u32[]{:S(2)}, u32[]{:S(2)}) collective-permute-start(bf16[544,128]{1,0:T(8,128)(2,1)S(1)} %shard_map.74.refs_2_), channel_id=1, source_target_pairs={{0,24},{1,25},{2,26},{3,27},{4,28},{5,29},{6,30},{7,31},{8,16},{9,... | collective-permute-start | bytes 417800 | tf_op jit(solution)/shard_map/ppermute | solution.py:184
  15.5 0.0 collective-permute-done.6.refs_7_
  15.5 1.5 %collective-permute-start.8 = (bf16[544,128]{1,0:T(8,128)(2,1)S(1)}, bf16[544,128]{1,0:T(8,128)(2,1)S(1)}, u32[]{:S(2)}, u32[]{:S(2)}) collective-permute-start(bf16[544,128]{1,0:T(8,128)(2,1)S(1)} %collective-permute-done.6.refs_7_), channel_id=1, source_target_pairs={{0,2},{1,3},{2,0},{3,1},{4,6},{5,7},{6,4},{7,5},{8,10},{9,11},{10,... | collective-permute-start | bytes 417800 | tf_op jit(solution)/shard_map/ppermute | solution.py:184
  17.0 7.1 %collective-permute-done.9.refs_10_ = bf16[544,128]{1,0:T(8,128)(2,1)S(1)} collective-permute-done((bf16[544,128]{1,0:T(8,128)(2,1)S(1)}, bf16[544,128]{1,0:T(8,128)(2,1)S(1)}, u32[]{:S(2)}, u32[]{:S(2)}) %collective-permute-start.9) | collective-permute-done | bytes 139296 | tf_op jit(solution)/shard_map/ppermute | solution.py:184
  24.1 0.5 collective-permute-start.2
  24.6 0.0 collective-permute-done.4.refs_5_
  24.6 1.5 %collective-permute-start.11 = (bf16[544,128]{1,0:T(8,128)(2,1)S(1)}, bf16[544,128]{1,0:T(8,128)(2,1)S(1)}, u32[]{:S(2)}, u32[]{:S(2)}) collective-permute-start(bf16[544,128]{1,0:T(8,128)(2,1)S(1)} %collective-permute-done.9.refs_10_), channel_id=1, source_target_pairs={{0,2},{1,3},{2,0},{3,1},{4,6},{5,7},{6,4},{7,5},{8,10},{9,11},{10,... | collective-permute-start | bytes 417800 | tf_op jit(solution)/shard_map/ppermute | solution.py:184
  26.1 0.0 collective-permute-done.13.refs_14_
  26.1 0.0 collective-permute-done.8.refs_9_
  26.1 1.5 %collective-permute-start.14 = (bf16[544,128]{1,0:T(8,128)(2,1)S(1)}, bf16[544,128]{1,0:T(8,128)(2,1)S(1)}, u32[]{:S(2)}, u32[]{:S(2)}) collective-permute-start(bf16[544,128]{1,0:T(8,128)(2,1)S(1)} %collective-permute-done.13.refs_14_), channel_id=1, source_target_pairs={{0,4},{1,5},{2,6},{3,7},{4,0},{5,1},{6,2},{7,3},{8,12},{9,13},{10,... | collective-permute-start | bytes 417800 | tf_op jit(solution)/shard_map/ppermute | solution.py:184
  27.6 0.7 %bitcast_add_fusion = s32[7]{0:T(128)S(1)} fusion(s32[7,1]{0,1:T(1,128)} %param.11, s32[7]{0:T(128)} %param.12, s32[7]{0:T(128)} %param.13), kind=kLoop, calls=%fused_computation.5 | loop fusion | flops 28 | bytes 112 | tf_op jit(solution)/shard_map/add | solution.py:222
  28.3 0.0 collective-permute-start
  28.3 1.1 %collective-permute-done = s32[7]{0:T(128)S(1)} collective-permute-done((s32[7]{0:T(128)S(1)}, s32[7]{0:T(128)S(1)}, u32[]{:S(2)}, u32[]{:S(2)}) %collective-permute-start) | collective-permute-done | bytes 60 | tf_op jit(solution)/shard_map/ppermute | solution.py:184
  29.4 0.5 collective-permute-start.7
  30.0 0.5 collective-permute-start.10
  30.5 1.5 %collective-permute-start.15 = (bf16[544,128]{1,0:T(8,128)(2,1)S(1)}, bf16[544,128]{1,0:T(8,128)(2,1)S(1)}, u32[]{:S(2)}, u32[]{:S(2)}) collective-permute-start(bf16[544,128]{1,0:T(8,128)(2,1)S(1)} %collective-permute-done.13.refs_14_), channel_id=1, source_target_pairs={{0,2},{1,3},{2,0},{3,1},{4,6},{5,7},{6,4},{7,5},{8,10},{9,11},{10,... | collective-permute-start | bytes 417800 | tf_op jit(solution)/shard_map/ppermute | solution.py:184
  32.0 1.5 %collective-permute-start.12 = (bf16[544,128]{1,0:T(8,128)(2,1)S(1)}, bf16[544,128]{1,0:T(8,128)(2,1)S(1)}, u32[]{:S(2)}, u32[]{:S(2)}) collective-permute-start(bf16[544,128]{1,0:T(8,128)(2,1)S(1)} %collective-permute-done.11.refs_12_), channel_id=1, source_target_pairs={{0,4},{1,5},{2,6},{3,7},{4,0},{5,1},{6,2},{7,3},{8,12},{9,13},{10,... | collective-permute-start | bytes 417800 | tf_op jit(solution)/shard_map/ppermute | solution.py:184
  33.5 0.0 collective-permute-done.1.other_hbm
  33.5 0.5 collective-permute-start.16
  34.0 0.1 pad_add_fusion.codes_ref
  34.1 1.2 %copy-done = bf16[7,512,512]{2,1,0:T(8,128)(2,1)} copy-done((bf16[7,512,512]{2,1,0:T(8,128)(2,1)}, bf16[7,512,512]{2,1,0:T(8,128)(2,1)S(1)}, u32[]{:S(2)}) %copy-start) | copy-done | bytes 3670040
  35.3 2.9 %shard_map.73 = (s32[8,3]{1,0:T(8,128)S(4)}, bf16[8,512,512]{2,1,0:T(8,128)(2,1)S(1)}) custom-call(s32[14]{0:T(128)S(1)} %pad_add_fusion.codes_ref, bf16[7,512,512]{2,1,0:T(8,128)(2,1)} %own_hbm.1, bf16[7,512,512]{2,1,0:T(8,128)(2,1)} %copy-done), custom_call_target="tpu_custom_call" | custom-call | tf_op jit(solution)/shard_map/pallas_call | solution.py:109
  38.2 0.0 collective-permute-done.7.refs_8_
  38.2 0.2 collective-permute-done.12.refs_13_
  38.4 0.5 collective-permute-done.15.refs_16_
  38.9 2.3 %collective-permute-done.16.refs_17_ = bf16[544,128]{1,0:T(8,128)(2,1)S(1)} collective-permute-done((bf16[544,128]{1,0:T(8,128)(2,1)S(1)}, bf16[544,128]{1,0:T(8,128)(2,1)S(1)}, u32[]{:S(2)}, u32[]{:S(2)}) %collective-permute-start.16) | collective-permute-done | bytes 139296 | tf_op jit(solution)/shard_map/ppermute | solution.py:184
  41.2 2.8 %shard_map.75 = f32[2,128,128]{2,1,0:T(8,128)S(1)} custom-call(s32[8,3]{1,0:T(8,128)S(4)} %get-tuple-element.9.refs_0_, bf16[8,512,512]{2,1,0:T(8,128)(2,1)S(1)} %get-tuple-element.10.refs_1_, bf16[544,128]{1,0:T(8,128)(2,1)S(1)} %shard_map.74.refs_2_, bf16[544,128]{1,0:T(8,128)(2,1)S(1)} %collective-permute-done.2.refs_3_, ...), custom_call_target="tpu_custom_call" | custom-call | tf_op jit(solution)/shard_map/pallas_call | solution.py:164
  44.0 0.6 %collective-permute-start.18 = (f32[128,128]{1,0:T(8,128)S(1)}, f32[128,128]{1,0:T(8,128)S(1)}, u32[]{:S(2)}, u32[]{:S(2)}) collective-permute-start(f32[128,128]{1,0:T(8,128)S(1)} %get-tuple-element.14), channel_id=1, source_target_pairs={{0,4},{1,5},{2,6},{3,7},{4,0},{5,1},{6,2},{7,3},{8,12},{9,13},{10,... | collective-permute-start | bytes 196616 | tf_op jit(solution)/shard_map/ppermute | solution.py:184
  44.6 1.4 %collective-permute-start.19 = (f32[128,128]{1,0:T(8,128)S(1)}, f32[128,128]{1,0:T(8,128)S(1)}, u32[]{:S(2)}, u32[]{:S(2)}) collective-permute-start(f32[128,128]{1,0:T(8,128)S(1)} %get-tuple-element.13), channel_id=1, source_target_pairs={{0,6},{1,7},{2,4},{3,5},{4,2},{5,3},{6,0},{7,1},{8,14},{9,15},{10,... | collective-permute-start | bytes 196616 | tf_op jit(solution)/shard_map/ppermute | solution.py:184
  46.1 1.5 %collective-permute-start.17 = (f32[128,128]{1,0:T(8,128)S(1)}, f32[128,128]{1,0:T(8,128)S(1)}, u32[]{:S(2)}, u32[]{:S(2)}) collective-permute-start(f32[128,128]{1,0:T(8,128)S(1)} %get-tuple-element.13), channel_id=1, source_target_pairs={{0,2},{1,3},{2,0},{3,1},{4,6},{5,7},{6,4},{7,5},{8,10},{9,11},{10,... | collective-permute-start | bytes 196616 | tf_op jit(solution)/shard_map/ppermute | solution.py:184
  47.6 0.8 %collective-permute-done.18 = f32[128,128]{1,0:T(8,128)S(1)} collective-permute-done((f32[128,128]{1,0:T(8,128)S(1)}, f32[128,128]{1,0:T(8,128)S(1)}, u32[]{:S(2)}, u32[]{:S(2)}) %collective-permute-start.18) | collective-permute-done | bytes 65568 | tf_op jit(solution)/shard_map/ppermute | solution.py:184
  48.3 1.5 %collective-permute-done.19 = f32[128,128]{1,0:T(8,128)S(1)} collective-permute-done((f32[128,128]{1,0:T(8,128)S(1)}, f32[128,128]{1,0:T(8,128)S(1)}, u32[]{:S(2)}, u32[]{:S(2)}) %collective-permute-start.19) | collective-permute-done | bytes 65568 | tf_op jit(solution)/shard_map/ppermute | solution.py:184
  49.8 0.7 %collective-permute-done.17 = f32[128,128]{1,0:T(8,128)S(1)} collective-permute-done((f32[128,128]{1,0:T(8,128)S(1)}, f32[128,128]{1,0:T(8,128)S(1)}, u32[]{:S(2)}, u32[]{:S(2)}) %collective-permute-start.17) | collective-permute-done | bytes 65568 | tf_op jit(solution)/shard_map/ppermute | solution.py:184
  50.5 2.4 %collective-permute-start.21 = (f32[128,128]{1,0:T(8,128)S(1)}, f32[128,128]{1,0:T(8,128)S(1)}, u32[]{:S(2)}, u32[]{:S(2)}) collective-permute-start(f32[128,128]{1,0:T(8,128)S(1)} %add_add_fusion), channel_id=1, source_target_pairs={{0,16},{1,17},{2,18},{3,19},{4,20},{5,21},{6,22},{7,23},{8,24},{9,... | collective-permute-start | bytes 196616 | tf_op jit(solution)/shard_map/ppermute | solution.py:184
  52.9 0.4 collective-permute-start.22
  53.4 0.7 %collective-permute-start.20 = (f32[128,128]{1,0:T(8,128)S(1)}, f32[128,128]{1,0:T(8,128)S(1)}, u32[]{:S(2)}, u32[]{:S(2)}) collective-permute-start(f32[128,128]{1,0:T(8,128)S(1)} %add_add_fusion), channel_id=1, source_target_pairs={{0,8},{1,9},{2,10},{3,11},{4,12},{5,13},{6,14},{7,15},{8,0},{9,1},... | collective-permute-start | bytes 196616 | tf_op jit(solution)/shard_map/ppermute | solution.py:184
  54.1 2.9 %collective-permute-done.21 = f32[128,128]{1,0:T(8,128)S(1)} collective-permute-done((f32[128,128]{1,0:T(8,128)S(1)}, f32[128,128]{1,0:T(8,128)S(1)}, u32[]{:S(2)}, u32[]{:S(2)}) %collective-permute-start.21) | collective-permute-done | bytes 65568 | tf_op jit(solution)/shard_map/ppermute | solution.py:184
  57.0 2.0 %collective-permute-done.22 = f32[128,128]{1,0:T(8,128)S(1)} collective-permute-done((f32[128,128]{1,0:T(8,128)S(1)}, f32[128,128]{1,0:T(8,128)S(1)}, u32[]{:S(2)}, u32[]{:S(2)}) %collective-permute-start.22) | collective-permute-done | bytes 65568 | tf_op jit(solution)/shard_map/ppermute | solution.py:184
  59.0 0.0 collective-permute-done.20
  59.0 0.6 %add_bitcast_fusion = f32[1,128,128]{2,1,0:T(8,128)} fusion(f32[128,128]{1,0:T(8,128)S(1)} %collective-permute-done.21, f32[128,128]{1,0:T(8,128)S(1)} %collective-permute-done.22, f32[128,128]{1,0:T(8,128)S(1)} %add_add_fusion, f32[128,128]{1,0:T(8,128)S(1)} %collective-permute-done.20), kind=kLoop, calls=%fused_computation.2 | loop fusion | flops 49152 | bytes 327680 | tf_op jit(solution)/shard_map/broadcast_in_dim | solution.py:237
  (8 shorter events, 0.0 us)
Async XLA Ops:
  0.0 33.5 %collective-permute-start.1 = (bf16[7,512,512]{2,1,0:T(8,128)(2,1)}, bf16[7,512,512]{2,1,0:T(8,128)(2,1)S(1)}, u32[]{:S(2)}, u32[]{:S(2)}) collective-permute-start(bf16[7,512,512]{2,1,0:T(8,128)(2,1)} %own_hbm.1), channel_id=1, source_target_pairs={{0,1},{1,0},{2,3},{3,2},{4,5},{5,4},{6,7},{7,6},{8,9},{9,8},{10,11... | collective-permute-start | bytes 11010056 | tf_op jit(solution)/shard_map/ppermute | solution.py:184
  2.4 7.0 %collective-permute-start.5 = (bf16[544,128]{1,0:T(8,128)(2,1)S(1)}, bf16[544,128]{1,0:T(8,128)(2,1)S(1)}, u32[]{:S(2)}, u32[]{:S(2)}) collective-permute-start(bf16[544,128]{1,0:T(8,128)(2,1)S(1)} %shard_map.74.refs_2_), channel_id=1, source_target_pairs={{0,8},{1,9},{2,10},{3,11},{4,12},{5,13},{6,14},{7,15},{8,0},{9,1},... | collective-permute-start | bytes 417800 | tf_op jit(solution)/shard_map/ppermute | solution.py:184
  5.0 8.6 %collective-permute-start.3 = (bf16[544,128]{1,0:T(8,128)(2,1)S(1)}, bf16[544,128]{1,0:T(8,128)(2,1)S(1)}, u32[]{:S(2)}, u32[]{:S(2)}) collective-permute-start(bf16[544,128]{1,0:T(8,128)(2,1)S(1)} %shard_map.74.refs_2_), channel_id=1, source_target_pairs={{0,2},{1,3},{2,0},{3,1},{4,6},{5,7},{6,4},{7,5},{8,10},{9,11},{10,... | collective-permute-start | bytes 417800 | tf_op jit(solution)/shard_map/ppermute | solution.py:184
  9.3 6.1 %collective-permute-start.6 = (bf16[544,128]{1,0:T(8,128)(2,1)S(1)}, bf16[544,128]{1,0:T(8,128)(2,1)S(1)}, u32[]{:S(2)}, u32[]{:S(2)}) collective-permute-start(bf16[544,128]{1,0:T(8,128)(2,1)S(1)} %collective-permute-done.5.refs_6_), channel_id=1, source_target_pairs={{0,4},{1,5},{2,6},{3,7},{4,0},{5,1},{6,2},{7,3},{8,12},{9,13},{10,... | collective-permute-start | bytes 417800 | tf_op jit(solution)/shard_map/ppermute | solution.py:184
  11.0 13.1 %collective-permute-start.9 = (bf16[544,128]{1,0:T(8,128)(2,1)S(1)}, bf16[544,128]{1,0:T(8,128)(2,1)S(1)}, u32[]{:S(2)}, u32[]{:S(2)}) collective-permute-start(bf16[544,128]{1,0:T(8,128)(2,1)S(1)} %shard_map.74.refs_2_), channel_id=1, source_target_pairs={{0,16},{1,17},{2,18},{3,19},{4,20},{5,21},{6,22},{7,23},{8,24},{9,... | collective-permute-start | bytes 417800 | tf_op jit(solution)/shard_map/ppermute | solution.py:184
  13.6 11.0 %collective-permute-start.4 = (bf16[544,128]{1,0:T(8,128)(2,1)S(1)}, bf16[544,128]{1,0:T(8,128)(2,1)S(1)}, u32[]{:S(2)}, u32[]{:S(2)}) collective-permute-start(bf16[544,128]{1,0:T(8,128)(2,1)S(1)} %collective-permute-done.3.refs_4_), channel_id=1, source_target_pairs={{0,4},{1,5},{2,6},{3,7},{4,0},{5,1},{6,2},{7,3},{8,12},{9,13},{10,... | collective-permute-start | bytes 417800 | tf_op jit(solution)/shard_map/ppermute | solution.py:184
  14.1 12.0 %collective-permute-start.13 = (bf16[544,128]{1,0:T(8,128)(2,1)S(1)}, bf16[544,128]{1,0:T(8,128)(2,1)S(1)}, u32[]{:S(2)}, u32[]{:S(2)}) collective-permute-start(bf16[544,128]{1,0:T(8,128)(2,1)S(1)} %shard_map.74.refs_2_), channel_id=1, source_target_pairs={{0,24},{1,25},{2,26},{3,27},{4,28},{5,29},{6,30},{7,31},{8,16},{9,... | collective-permute-start | bytes 417800 | tf_op jit(solution)/shard_map/ppermute | solution.py:184
  15.5 10.7 %collective-permute-start.8 = (bf16[544,128]{1,0:T(8,128)(2,1)S(1)}, bf16[544,128]{1,0:T(8,128)(2,1)S(1)}, u32[]{:S(2)}, u32[]{:S(2)}) collective-permute-start(bf16[544,128]{1,0:T(8,128)(2,1)S(1)} %collective-permute-done.6.refs_7_), channel_id=1, source_target_pairs={{0,2},{1,3},{2,0},{3,1},{4,6},{5,7},{6,4},{7,5},{8,10},{9,11},{10,... | collective-permute-start | bytes 417800 | tf_op jit(solution)/shard_map/ppermute | solution.py:184
  24.1 5.9 %collective-permute-start.2 = (bf16[544,128]{1,0:T(8,128)(2,1)S(1)}, bf16[544,128]{1,0:T(8,128)(2,1)S(1)}, u32[]{:S(2)}, u32[]{:S(2)}) collective-permute-start(bf16[544,128]{1,0:T(8,128)(2,1)S(1)} %shard_map.74.refs_2_), channel_id=1, source_target_pairs={{0,4},{1,5},{2,6},{3,7},{4,0},{5,1},{6,2},{7,3},{8,12},{9,13},{10,... | collective-permute-start | bytes 417800 | tf_op jit(solution)/shard_map/ppermute | solution.py:184
  24.6 5.9 %collective-permute-start.11 = (bf16[544,128]{1,0:T(8,128)(2,1)S(1)}, bf16[544,128]{1,0:T(8,128)(2,1)S(1)}, u32[]{:S(2)}, u32[]{:S(2)}) collective-permute-start(bf16[544,128]{1,0:T(8,128)(2,1)S(1)} %collective-permute-done.9.refs_10_), channel_id=1, source_target_pairs={{0,2},{1,3},{2,0},{3,1},{4,6},{5,7},{6,4},{7,5},{8,10},{9,11},{10,... | collective-permute-start | bytes 417800 | tf_op jit(solution)/shard_map/ppermute | solution.py:184
  26.1 5.9 %collective-permute-start.14 = (bf16[544,128]{1,0:T(8,128)(2,1)S(1)}, bf16[544,128]{1,0:T(8,128)(2,1)S(1)}, u32[]{:S(2)}, u32[]{:S(2)}) collective-permute-start(bf16[544,128]{1,0:T(8,128)(2,1)S(1)} %collective-permute-done.13.refs_14_), channel_id=1, source_target_pairs={{0,4},{1,5},{2,6},{3,7},{4,0},{5,1},{6,2},{7,3},{8,12},{9,13},{10,... | collective-permute-start | bytes 417800 | tf_op jit(solution)/shard_map/ppermute | solution.py:184
  28.3 1.1 %collective-permute-start = (s32[7]{0:T(128)S(1)}, s32[7]{0:T(128)S(1)}, u32[]{:S(2)}, u32[]{:S(2)}) collective-permute-start(s32[7]{0:T(128)S(1)} %bitcast_add_fusion), channel_id=1, source_target_pairs={{0,1},{1,0},{2,3},{3,2},{4,5},{5,4},{6,7},{7,6},{8,9},{9,8},{10,11... | collective-permute-start | bytes 92 | tf_op jit(solution)/shard_map/ppermute | solution.py:184
  29.4 8.8 %collective-permute-start.7 = (bf16[544,128]{1,0:T(8,128)(2,1)S(1)}, bf16[544,128]{1,0:T(8,128)(2,1)S(1)}, u32[]{:S(2)}, u32[]{:S(2)}) collective-permute-start(bf16[544,128]{1,0:T(8,128)(2,1)S(1)} %collective-permute-done.5.refs_6_), channel_id=1, source_target_pairs={{0,2},{1,3},{2,0},{3,1},{4,6},{5,7},{6,4},{7,5},{8,10},{9,11},{10,... | collective-permute-start | bytes 417800 | tf_op jit(solution)/shard_map/ppermute | solution.py:184
  30.0 8.3 %collective-permute-start.10 = (bf16[544,128]{1,0:T(8,128)(2,1)S(1)}, bf16[544,128]{1,0:T(8,128)(2,1)S(1)}, u32[]{:S(2)}, u32[]{:S(2)}) collective-permute-start(bf16[544,128]{1,0:T(8,128)(2,1)S(1)} %collective-permute-done.9.refs_10_), channel_id=1, source_target_pairs={{0,4},{1,5},{2,6},{3,7},{4,0},{5,1},{6,2},{7,3},{8,12},{9,13},{10,... | collective-permute-start | bytes 417800 | tf_op jit(solution)/shard_map/ppermute | solution.py:184
  30.5 8.5 %collective-permute-start.15 = (bf16[544,128]{1,0:T(8,128)(2,1)S(1)}, bf16[544,128]{1,0:T(8,128)(2,1)S(1)}, u32[]{:S(2)}, u32[]{:S(2)}) collective-permute-start(bf16[544,128]{1,0:T(8,128)(2,1)S(1)} %collective-permute-done.13.refs_14_), channel_id=1, source_target_pairs={{0,2},{1,3},{2,0},{3,1},{4,6},{5,7},{6,4},{7,5},{8,10},{9,11},{10,... | collective-permute-start | bytes 417800 | tf_op jit(solution)/shard_map/ppermute | solution.py:184
  32.0 6.4 %collective-permute-start.12 = (bf16[544,128]{1,0:T(8,128)(2,1)S(1)}, bf16[544,128]{1,0:T(8,128)(2,1)S(1)}, u32[]{:S(2)}, u32[]{:S(2)}) collective-permute-start(bf16[544,128]{1,0:T(8,128)(2,1)S(1)} %collective-permute-done.11.refs_12_), channel_id=1, source_target_pairs={{0,4},{1,5},{2,6},{3,7},{4,0},{5,1},{6,2},{7,3},{8,12},{9,13},{10,... | collective-permute-start | bytes 417800 | tf_op jit(solution)/shard_map/ppermute | solution.py:184
  33.5 1.8 %copy-start = (bf16[7,512,512]{2,1,0:T(8,128)(2,1)}, bf16[7,512,512]{2,1,0:T(8,128)(2,1)S(1)}, u32[]{:S(2)}) copy-start(bf16[7,512,512]{2,1,0:T(8,128)(2,1)S(1)} %collective-permute-done.1.other_hbm) | copy-start | bytes 11010052
  33.5 7.7 %collective-permute-start.16 = (bf16[544,128]{1,0:T(8,128)(2,1)S(1)}, bf16[544,128]{1,0:T(8,128)(2,1)S(1)}, u32[]{:S(2)}, u32[]{:S(2)}) collective-permute-start(bf16[544,128]{1,0:T(8,128)(2,1)S(1)} %collective-permute-done.14.refs_15_), channel_id=1, source_target_pairs={{0,2},{1,3},{2,0},{3,1},{4,6},{5,7},{6,4},{7,5},{8,10},{9,11},{10,... | collective-permute-start | bytes 417800 | tf_op jit(solution)/shard_map/ppermute | solution.py:184
  44.0 4.3 %collective-permute-start.18 = (f32[128,128]{1,0:T(8,128)S(1)}, f32[128,128]{1,0:T(8,128)S(1)}, u32[]{:S(2)}, u32[]{:S(2)}) collective-permute-start(f32[128,128]{1,0:T(8,128)S(1)} %get-tuple-element.14), channel_id=1, source_target_pairs={{0,4},{1,5},{2,6},{3,7},{4,0},{5,1},{6,2},{7,3},{8,12},{9,13},{10,... | collective-permute-start | bytes 196616 | tf_op jit(solution)/shard_map/ppermute | solution.py:184
  44.6 5.2 %collective-permute-start.19 = (f32[128,128]{1,0:T(8,128)S(1)}, f32[128,128]{1,0:T(8,128)S(1)}, u32[]{:S(2)}, u32[]{:S(2)}) collective-permute-start(f32[128,128]{1,0:T(8,128)S(1)} %get-tuple-element.13), channel_id=1, source_target_pairs={{0,6},{1,7},{2,4},{3,5},{4,2},{5,3},{6,0},{7,1},{8,14},{9,15},{10,... | collective-permute-start | bytes 196616 | tf_op jit(solution)/shard_map/ppermute | solution.py:184
  46.1 4.4 %collective-permute-start.17 = (f32[128,128]{1,0:T(8,128)S(1)}, f32[128,128]{1,0:T(8,128)S(1)}, u32[]{:S(2)}, u32[]{:S(2)}) collective-permute-start(f32[128,128]{1,0:T(8,128)S(1)} %get-tuple-element.13), channel_id=1, source_target_pairs={{0,2},{1,3},{2,0},{3,1},{4,6},{5,7},{6,4},{7,5},{8,10},{9,11},{10,... | collective-permute-start | bytes 196616 | tf_op jit(solution)/shard_map/ppermute | solution.py:184
  50.5 6.5 %collective-permute-start.21 = (f32[128,128]{1,0:T(8,128)S(1)}, f32[128,128]{1,0:T(8,128)S(1)}, u32[]{:S(2)}, u32[]{:S(2)}) collective-permute-start(f32[128,128]{1,0:T(8,128)S(1)} %add_add_fusion), channel_id=1, source_target_pairs={{0,16},{1,17},{2,18},{3,19},{4,20},{5,21},{6,22},{7,23},{8,24},{9,... | collective-permute-start | bytes 196616 | tf_op jit(solution)/shard_map/ppermute | solution.py:184
  52.9 6.1 %collective-permute-start.22 = (f32[128,128]{1,0:T(8,128)S(1)}, f32[128,128]{1,0:T(8,128)S(1)}, u32[]{:S(2)}, u32[]{:S(2)}) collective-permute-start(f32[128,128]{1,0:T(8,128)S(1)} %add_add_fusion), channel_id=1, source_target_pairs={{0,24},{1,25},{2,26},{3,27},{4,28},{5,29},{6,30},{7,31},{8,16},{9,... | collective-permute-start | bytes 196616 | tf_op jit(solution)/shard_map/ppermute | solution.py:184
  53.4 5.6 %collective-permute-start.20 = (f32[128,128]{1,0:T(8,128)S(1)}, f32[128,128]{1,0:T(8,128)S(1)}, u32[]{:S(2)}, u32[]{:S(2)}) collective-permute-start(f32[128,128]{1,0:T(8,128)S(1)} %add_add_fusion), channel_id=1, source_target_pairs={{0,8},{1,9},{2,10},{3,11},{4,12},{5,13},{6,14},{7,15},{8,0},{9,1},... | collective-permute-start | bytes 196616 | tf_op jit(solution)/shard_map/ppermute | solution.py:184

commit v3 on v2

--- a/solution.py
+++ b/solution.py
@@ -61,28 +61,36 @@
             pltpu.VMEM(occupied.shape, jnp.bfloat16),
             pltpu.SemaphoreType.DMA((CHUNKS + 2,)),
         ],
+        cost_estimate=pl.CostEstimate(flops=4 * 10**10, bytes_accessed=0, transcendentals=0),
         compiler_params=pltpu.CompilerParams(vmem_limit_bytes=VMEM_LIMIT),
     )(in_hbm(panel_index[None, :]), in_hbm(orbitals), in_hbm(occupied))
 
 
-def collect_kernel(codes_ref, own_hbm, other_hbm, labels_ref, blocks_ref, sems):
+def collect_kernel(own_codes, other_codes, own_hbm, labels_ref, blocks_ref, own, other, sems):
     groups, regions = lax.axis_size("grp"), lax.axis_size("reg")
     reg = lax.axis_index("reg")
     me = lax.axis_index("grp") * regions + reg
     held = own_hbm.shape[0]
-    slots = blocks_ref.shape[0]
-
-    def block_copy(source, n, at):
-        return pltpu.make_async_copy(source.at[n], blocks_ref.at[at], sems.at[at])
-
-    for at in range(slots):
+    half = blocks_ref.shape[0]
+    copies = [
+        pltpu.make_async_copy(own_codes, own, sems.at[half]),
+        pltpu.make_async_copy(other_codes, other, sems.at[half + 1]),
+    ]
+
+    def block_copy(n, at):
+        return pltpu.make_async_copy(own_hbm.at[n], blocks_ref.at[at], sems.at[at])
+
+    for copy in copies:
+        copy.start()
+    for at in range(2 * half):
         labels_ref[at, 0] = -1
-        labels_ref[at, 1] = 0
-        labels_ref[at, 2] = 0
-    used = jnp.int32(0)
-    for source, first in ((own_hbm, 0), (other_hbm, held)):
+        for column in range(1, 4):
+            labels_ref[at, column] = 0
+    for copy, codes, first in zip(copies, (own, other), (0, half)):
+        copy.wait()
+        used = jnp.int32(first)
         for n in range(held):
-            code = codes_ref[first + n]
+            code = codes[n]
             region = code % regions
             row = code // regions % groups
             col = code // (regions * groups)
@@ -93,40 +101,45 @@
                 labels_ref[used, 0] = (region ^ reg) // 2
                 labels_ref[used, 1] = ((row * regions + region) ^ me) // 2
                 labels_ref[used, 2] = ((col * regions + region) ^ me) // 2
-                block_copy(source, n, used).start()
+                labels_ref[used, 3] = n
+                if first == 0:
+                    block_copy(n, used).start()
 
             used = used + wanted.astype(jnp.int32)
-    for at in range(slots):
-
-        @pl.when(at < used)
+        if first == 0:
+            used_own = used
+    for at in range(half):
+
+        @pl.when(at < used_own)
         def _():
-            block_copy(own_hbm, 0, at).wait()
-
-
-def collect(codes, own, other, regions):
+            block_copy(0, at).wait()
+
+
+def collect(codes, own, regions):
     held = own.shape[0]
-    slots = min(2 * held, 2 * CAP * regions)
+    half = min(held, CAP * regions)
     return pl.pallas_call(
         collect_kernel,
         out_shape=(
-            pltpu.SMEM((slots, 3), jnp.int32),
-            pltpu.VMEM((slots,) + own.shape[1:], jnp.bfloat16),
+            pltpu.SMEM((2 * half, 4), jnp.int32),
+            pltpu.VMEM((half,) + own.shape[1:], jnp.bfloat16),
         ),
-        in_specs=[pl.BlockSpec(memory_space=pltpu.SMEM)]
-        + [pl.BlockSpec(memory_space=pltpu.HBM)] * 2,
+        in_specs=[pl.BlockSpec(memory_space=pltpu.HBM)] * 3,
         out_specs=(
             pl.BlockSpec(memory_space=pltpu.SMEM),
             pl.BlockSpec(memory_space=pltpu.VMEM),
         ),
-        scratch_shapes=[pltpu.SemaphoreType.DMA((slots,))],
+        scratch_shapes=[pltpu.SMEM((held,), jnp.int32)] * 2
+        + [pltpu.SemaphoreType.DMA((half + 2,))],
         compiler_params=pltpu.CompilerParams(vmem_limit_bytes=VMEM_LIMIT),
-    )(codes, in_hbm(own), in_hbm(other))
-
-
-def sigma_kernel(places, points, occ_count, labels_ref, blocks, *refs):
+    )(*[in_hbm(array) for array in (*codes, own)])
+
+
+def sigma_kernel(places, points, occ_count, labels_ref, blocks, other, *refs):
     piece_refs = refs[: len(places)]
     out_ref, packed, dressed, screened = refs[len(places) :]
-    slots = blocks.shape[0]
+    half = blocks.shape[0]
+    slots = 2 * half
     out_ref[...] = jnp.zeros_like(out_ref)
     for n, place in enumerate(places):
         packed[place] = piece_refs[n][...]
@@ -142,7 +155,8 @@
         overlap = lax.dot_general(
             occupied_of(row), occupied_of(col), transposed, preferred_element_type=jnp.float32
         )
-        dressed[at] = (blocks[at].astype(jnp.float32) * overlap).astype(jnp.bfloat16)
+        block = blocks[at] if at < half else other[labels_ref[at, 3]]
+        dressed[at] = (block.astype(jnp.float32) * overlap).astype(jnp.bfloat16)
     for at in range(slots):
         col = labels_ref[at, 2]
         screened[at] = jnp.dot(
@@ -156,16 +170,16 @@
         out_ref[jnp.maximum(place, 0)] += jnp.where(place >= 0, product, 0.0)
 
 
-def partial_sigma(labels, blocks, found, regions, points, occ_count):
+def partial_sigma(labels, blocks, other, found, regions, points, occ_count):
     arrays = [array for _, array in found]
     places = [mask // 2 for mask, _ in found]
     rows, width = arrays[0].shape
-    slots = blocks.shape[0]
+    slots = 2 * blocks.shape[0]
     return pl.pallas_call(
         lambda *refs: sigma_kernel(places, points, occ_count, *refs),
         out_shape=pltpu.VMEM((regions, width, width), jnp.float32),
         in_specs=[pl.BlockSpec(memory_space=pltpu.SMEM)]
-        + [pl.BlockSpec(memory_space=pltpu.VMEM)] * (1 + len(arrays)),
+        + [pl.BlockSpec(memory_space=pltpu.VMEM)] * (2 + len(arrays)),
         out_specs=pl.BlockSpec(memory_space=pltpu.VMEM),
         scratch_shapes=[
             pltpu.VMEM((len(arrays), rows, width), jnp.bfloat16),
@@ -176,6 +190,7 @@
     )(
         pltpu.with_memory_space_constraint(labels, pltpu.SMEM),
         in_vmem(blocks),
+        in_vmem(other),
         *[in_vmem(array) for array in arrays],
     )
 
@@ -184,25 +199,23 @@
     return lax.ppermute(array, AXES, [(i, i ^ mask) for i in range(count)])
 
 
-def gather(packed, count, first_bit):
-    bits = []
-    while first_bit < count:
-        bits.append(first_bit)
-        first_bit *= 2
-    y, x = bits[0], bits[1]
-    column = [(0, packed)]
-    for mask in range(bits[2], count, bits[2]):
-        column.append((mask, swap(packed, mask, count)))
-    found = []
-    earlier = []
-    for n, (mask, array) in enumerate(column):
-        if n >= 2:
-            array, _ = lax.optimization_barrier((array, earlier[n - 2]))
-        over_x, over_y = swap(array, x, count), swap(array, y, count)
-        corner = swap(over_x, y, count) if n % 2 else swap(over_y, x, count)
-        earlier.append(corner)
-        found += [(mask, array), (mask ^ x, over_x), (mask ^ y, over_y), (mask ^ x ^ y, corner)]
-    return found
+def gather(packed, count, tied):
+    y, x, near = 2, 4, 8
+    far = [1 << n for n in range(3, count.bit_length() - 1)]
+    column = {0: packed, far[-1]: swap(packed, far[-1], count)}
+    column[far[-1]], tied = lax.optimization_barrier((column[far[-1]], tied))
+    for bit in reversed(far[:-1]):
+        for mask in list(column):
+            column[mask ^ bit] = swap(column[mask], bit, count)
+    found = dict(column)
+    for mask in sorted(column):
+        if mask & near and mask != near:
+            over_x, over_y = (swap(found[mask ^ near ^ bit], near, count) for bit in (x, y))
+        else:
+            over_x, over_y = (swap(column[mask], bit, count) for bit in (x, y))
+        corner = swap(over_x, y, count) if mask & near else swap(over_y, x, count)
+        found.update({mask ^ x: over_x, mask ^ y: over_y, mask ^ x ^ y: corner})
+    return sorted(found.items()), tied
 
 
 def total(values):
@@ -217,12 +230,13 @@
     points, occ_count = screening.shape[1], occupied.shape[2]
 
     other = swap(screening, 1, count)
+    codes = (block_col * groups + block_row) * regions + block_region[:, 0]
+    codes = (codes, swap(codes, 1, count))
     packed = pack(panel_index, orbitals[0, 0], occupied[0, 0])
-    found = gather(packed, count, 2)
-    codes = (block_col * groups + block_row) * regions + block_region[:, 0]
-    codes = jnp.concatenate([codes, swap(codes, 1, count)])
-    labels, blocks = collect(codes, screening, other, regions // 2)
-    sums = partial_sigma(labels, blocks, found, regions // 2, points, occ_count)
+    packed, codes = lax.optimization_barrier((packed, codes))
+    found, (codes, other) = gather(packed, count, (codes, other))
+    labels, blocks = collect(codes, screening, regions // 2)
+    sums = partial_sigma(labels, blocks, other, found, regions // 2, points, occ_count)
     stage = []
     for low in (0, regions):
         for mask in range(0, regions, 2):

time: 59.8 us -> 52.7 us (0.88)
  waiting for transfers between devices: 21.9 us -> 15.6 us
  local copies, waits for them, and re-layouts: 1.2 us -> 0.02 us
  starting transfers between devices: 27.5 us -> 28.6 us
  Pallas kernels: 7.6 us -> 6.84 us
    ppermute x23, waiting for transfers between devices: 21.9 us -> 15.6 us  [swap(): return lax.ppermute(array, AXES, [(i, i ^ mask) for i in range(count)])]
    unnamed x2 -> x4, local copies, waits for them, and re-layouts: 1.19 us -> 0.01 us
    ppermute x23, starting transfers between devices: 27.5 us -> 28.6 us  [swap(): return lax.ppermute(array, AXES, [(i, i ^ mask) for i in range(count)])]
    pallas_call x1, Pallas kernels: 2.91 us -> 2.15 us  [collect(): pl.pallas_call(collect_kernel, out_shape=(pltpu.SMEM((2 * half, 4), jnp.i...]
  transfers between devices with their start and end apart: 23 -> 23, of which waited for: 11 -> 11; matrix products, arithmetic and copies ran while one was open for 1% -> 0% of each run, Pallas kernels for 8% -> 8%
where the time goes in v3:
time: 52.7 us; the launch traced here: 52.5 us
  starting transfers between devices  28.6 us (54%)
  waiting for transfers between devices  15.6 us (30%)
  Pallas kernels  6.84 us (13%)
  other arithmetic  1.36 us (3%)
    ppermute x23, starting transfers between devices, swap(): return lax.ppermute(array, AXES, [(i, i ^ mask) for i in range(count)])  28.6 us
    ppermute x23, waiting for transfers between devices, swap(): return lax.ppermute(array, AXES, [(i, i ^ mask) for i in range(count)])  15.6 us
    pallas_call x1, Pallas kernels, partial_sigma(): pl.pallas_call(lambda *refs: sigma_kernel(places, points, occ_count, *ref...  2.79 us
    pallas_call x1, Pallas kernels, collect(): pl.pallas_call(collect_kernel, out_shape=(pltpu.SMEM((2 * half, 4), jnp.i...  2.15 us
    pallas_call x1, Pallas kernels, pack(): pl.pallas_call(pack_kernel, out_shape=pltpu.VMEM((points + occ_rows, widt...  1.9 us
  transfers between devices with their start and end apart: 23, of which 11 were waited for; matrix products, arithmetic and copies ran while one was open for 0% of the time, Pallas kernels for 8%

profile of v3, /device:TPU:0, one launch (start us, length us, event | category | flops | bytes accessed | tf_op | source)
XLA Modules:
  0.0 52.5 jit_solution(5177908921327788846)
XLA Ops:
  0.0 0.7 %bitcast_add_fusion.own_codes = s32[7]{0:T(128)S(1)} fusion(s32[7,1]{0,1:T(1,128)} %param.11, s32[7]{0:T(128)} %param.12, s32[7]{0:T(128)} %param.13), kind=kLoop, calls=%fused_computation.4 | loop fusion | flops 28 | bytes 112 | tf_op jit(solution)/shard_map/add | solution.py:233
  0.7 0.5 collective-permute-start
  1.1 0.1 collective-permute-start.2
  1.2 1.9 %shard_map.73.refs_3_ = bf16[544,128]{1,0:T(8,128)(2,1)S(1)} custom-call(s32[1,128]{1,0:T(1,128)} %bitcast.15, bf16[512,1024]{1,0:T(8,128)(2,1)} %bitcast.13, bf16[8,512]{1,0:T(8,128)(2,1)} %bitcast.14), custom_call_target="tpu_custom_call" | custom-call | flops 40000000000 | tf_op jit(solution)/shard_map/pallas_call | solution.py:53
  3.1 0.0 collective-permute-done.other_codes
  3.2 4.1 %collective-permute-start.1 = (bf16[544,128]{1,0:T(8,128)(2,1)S(1)}, bf16[544,128]{1,0:T(8,128)(2,1)S(1)}, u32[]{:S(2)}, u32[]{:S(2)}) collective-permute-start(bf16[544,128]{1,0:T(8,128)(2,1)S(1)} %shard_map.73.refs_3_), channel_id=1, source_target_pairs={{0,16},{1,17},{2,18},{3,19},{4,20},{5,21},{6,22},{7,23},{8,24},{9,... | collective-permute-start | bytes 417800 | tf_op jit(solution)/shard_map/ppermute | solution.py:199
  7.2 1.6 %collective-permute-start.6 = (bf16[544,128]{1,0:T(8,128)(2,1)S(1)}, bf16[544,128]{1,0:T(8,128)(2,1)S(1)}, u32[]{:S(2)}, u32[]{:S(2)}) collective-permute-start(bf16[544,128]{1,0:T(8,128)(2,1)S(1)} %shard_map.73.refs_3_), channel_id=1, source_target_pairs={{0,8},{1,9},{2,10},{3,11},{4,12},{5,13},{6,14},{7,15},{8,0},{9,1},... | collective-permute-start | bytes 417800 | tf_op jit(solution)/shard_map/ppermute | solution.py:199
  8.8 1.5 %collective-permute-start.4 = (bf16[544,128]{1,0:T(8,128)(2,1)S(1)}, bf16[544,128]{1,0:T(8,128)(2,1)S(1)}, u32[]{:S(2)}, u32[]{:S(2)}) collective-permute-start(bf16[544,128]{1,0:T(8,128)(2,1)S(1)} %shard_map.73.refs_3_), channel_id=1, source_target_pairs={{0,4},{1,5},{2,6},{3,7},{4,0},{5,1},{6,2},{7,3},{8,12},{9,13},{10,... | collective-permute-start | bytes 417800 | tf_op jit(solution)/shard_map/ppermute | solution.py:199
  10.3 1.5 %collective-permute-start.3 = (bf16[544,128]{1,0:T(8,128)(2,1)S(1)}, bf16[544,128]{1,0:T(8,128)(2,1)S(1)}, u32[]{:S(2)}, u32[]{:S(2)}) collective-permute-start(bf16[544,128]{1,0:T(8,128)(2,1)S(1)} %shard_map.73.refs_3_), channel_id=1, source_target_pairs={{0,2},{1,3},{2,0},{3,1},{4,6},{5,7},{6,4},{7,5},{8,10},{9,11},{10,... | collective-permute-start | bytes 417800 | tf_op jit(solution)/shard_map/ppermute | solution.py:199
  11.8 2.4 %collective-permute-done.1.refs_11_ = bf16[544,128]{1,0:T(8,128)(2,1)S(1)} collective-permute-done((bf16[544,128]{1,0:T(8,128)(2,1)S(1)}, bf16[544,128]{1,0:T(8,128)(2,1)S(1)}, u32[]{:S(2)}, u32[]{:S(2)}) %collective-permute-start.1) | collective-permute-done | bytes 139296 | tf_op jit(solution)/shard_map/ppermute | solution.py:199
  14.2 0.0 collective-permute-done.2.refs_2_
  14.2 1.5 %collective-permute-start.11 = (bf16[544,128]{1,0:T(8,128)(2,1)S(1)}, bf16[544,128]{1,0:T(8,128)(2,1)S(1)}, u32[]{:S(2)}, u32[]{:S(2)}) collective-permute-start(bf16[544,128]{1,0:T(8,128)(2,1)S(1)} %collective-permute-done.1.refs_11_), channel_id=1, source_target_pairs={{0,4},{1,5},{2,6},{3,7},{4,0},{5,1},{6,2},{7,3},{8,12},{9,13},{10,... | collective-permute-start | bytes 417800 | tf_op jit(solution)/shard_map/ppermute | solution.py:199
  15.8 0.0 collective-permute-done.6.refs_7_
  15.8 0.5 collective-permute-start.8
  16.3 1.6 %collective-permute-start.7 = (bf16[544,128]{1,0:T(8,128)(2,1)S(1)}, bf16[544,128]{1,0:T(8,128)(2,1)S(1)}, u32[]{:S(2)}, u32[]{:S(2)}) collective-permute-start(bf16[544,128]{1,0:T(8,128)(2,1)S(1)} %collective-permute-done.6.refs_7_), channel_id=1, source_target_pairs={{0,2},{1,3},{2,0},{3,1},{4,6},{5,7},{6,4},{7,5},{8,10},{9,11},{10,... | collective-permute-start | bytes 417800 | tf_op jit(solution)/shard_map/ppermute | solution.py:199
  17.9 0.5 collective-permute-start.10
  18.3 0.0 collective-permute-done.3.refs_4_
  18.3 1.5 %collective-permute-start.5 = (bf16[544,128]{1,0:T(8,128)(2,1)S(1)}, bf16[544,128]{1,0:T(8,128)(2,1)S(1)}, u32[]{:S(2)}, u32[]{:S(2)}) collective-permute-start(bf16[544,128]{1,0:T(8,128)(2,1)S(1)} %collective-permute-done.3.refs_4_), channel_id=1, source_target_pairs={{0,4},{1,5},{2,6},{3,7},{4,0},{5,1},{6,2},{7,3},{8,12},{9,13},{10,... | collective-permute-start | bytes 417800 | tf_op jit(solution)/shard_map/ppermute | solution.py:199
  19.9 1.0 %collective-permute-done.11.refs_13_ = bf16[544,128]{1,0:T(8,128)(2,1)S(1)} collective-permute-done((bf16[544,128]{1,0:T(8,128)(2,1)S(1)}, bf16[544,128]{1,0:T(8,128)(2,1)S(1)}, u32[]{:S(2)}, u32[]{:S(2)}) %collective-permute-start.11) | collective-permute-done | bytes 139296 | tf_op jit(solution)/shard_map/ppermute | solution.py:199
  20.9 0.5 %collective-permute-start.15 = (bf16[544,128]{1,0:T(8,128)(2,1)S(1)}, bf16[544,128]{1,0:T(8,128)(2,1)S(1)}, u32[]{:S(2)}, u32[]{:S(2)}) collective-permute-start(bf16[544,128]{1,0:T(8,128)(2,1)S(1)} %collective-permute-done.11.refs_13_), channel_id=1, source_target_pairs={{0,8},{1,9},{2,10},{3,11},{4,12},{5,13},{6,14},{7,15},{8,0},{9,1},... | collective-permute-start | bytes 417800 | tf_op jit(solution)/shard_map/ppermute | solution.py:199
  21.4 2.3 %collective-permute-done.8.refs_9_ = bf16[544,128]{1,0:T(8,128)(2,1)S(1)} collective-permute-done((bf16[544,128]{1,0:T(8,128)(2,1)S(1)}, bf16[544,128]{1,0:T(8,128)(2,1)S(1)}, u32[]{:S(2)}, u32[]{:S(2)}) %collective-permute-start.8) | collective-permute-done | bytes 139296 | tf_op jit(solution)/shard_map/ppermute | solution.py:199
  23.7 1.3 %collective-permute-start.9 = (bf16[544,128]{1,0:T(8,128)(2,1)S(1)}, bf16[544,128]{1,0:T(8,128)(2,1)S(1)}, u32[]{:S(2)}, u32[]{:S(2)}) collective-permute-start(bf16[544,128]{1,0:T(8,128)(2,1)S(1)} %collective-permute-done.8.refs_9_), channel_id=1, source_target_pairs={{0,2},{1,3},{2,0},{3,1},{4,6},{5,7},{6,4},{7,5},{8,10},{9,11},{10,... | collective-permute-start | bytes 417800 | tf_op jit(solution)/shard_map/ppermute | solution.py:199
  25.0 0.9 %collective-permute-start.13 = (bf16[544,128]{1,0:T(8,128)(2,1)S(1)}, bf16[544,128]{1,0:T(8,128)(2,1)S(1)}, u32[]{:S(2)}, u32[]{:S(2)}) collective-permute-start(bf16[544,128]{1,0:T(8,128)(2,1)S(1)} %collective-permute-done.1.refs_11_), channel_id=1, source_target_pairs={{0,8},{1,9},{2,10},{3,11},{4,12},{5,13},{6,14},{7,15},{8,0},{9,1},... | collective-permute-start | bytes 417800 | tf_op jit(solution)/shard_map/ppermute | solution.py:199
  25.9 0.0 collective-permute-done.10.refs_12_
  25.9 1.1 %collective-permute-start.14 = (bf16[544,128]{1,0:T(8,128)(2,1)S(1)}, bf16[544,128]{1,0:T(8,128)(2,1)S(1)}, u32[]{:S(2)}, u32[]{:S(2)}) collective-permute-start(bf16[544,128]{1,0:T(8,128)(2,1)S(1)} %collective-permute-done.10.refs_12_), channel_id=1, source_target_pairs={{0,8},{1,9},{2,10},{3,11},{4,12},{5,13},{6,14},{7,15},{8,0},{9,1},... | collective-permute-start | bytes 417800 | tf_op jit(solution)/shard_map/ppermute | solution.py:199
  27.0 0.0 collective-permute-done.5.refs_6_
  27.0 1.5 %collective-permute-start.12 = (bf16[544,128]{1,0:T(8,128)(2,1)S(1)}, bf16[544,128]{1,0:T(8,128)(2,1)S(1)}, u32[]{:S(2)}, u32[]{:S(2)}) collective-permute-start(bf16[544,128]{1,0:T(8,128)(2,1)S(1)} %collective-permute-done.10.refs_12_), channel_id=1, source_target_pairs={{0,4},{1,5},{2,6},{3,7},{4,0},{5,1},{6,2},{7,3},{8,12},{9,13},{10,... | collective-permute-start | bytes 417800 | tf_op jit(solution)/shard_map/ppermute | solution.py:199
  28.5 0.0 collective-permute-done.15.refs_17_
  28.5 0.5 collective-permute-start.16
  29.0 2.1 %shard_map.74 = (s32[8,4]{1,0:T(8,128)S(4)}, bf16[4,512,512]{2,1,0:T(8,128)(2,1)S(1)}) custom-call(s32[7]{0:T(128)} %copy-done, s32[7]{0:T(128)} %copy-done.1, bf16[7,512,512]{2,1,0:T(8,128)(2,1)} %own_hbm.1), custom_call_target="tpu_custom_call" | custom-call | tf_op jit(solution)/shard_map/pallas_call | solution.py:121
  31.2 0.0 collective-permute-done.13.refs_15_
  31.2 0.7 %collective-permute-done.14.refs_16_ = bf16[544,128]{1,0:T(8,128)(2,1)S(1)} collective-permute-done((bf16[544,128]{1,0:T(8,128)(2,1)S(1)}, bf16[544,128]{1,0:T(8,128)(2,1)S(1)}, u32[]{:S(2)}, u32[]{:S(2)}) %collective-permute-start.14) | collective-permute-done | bytes 139296 | tf_op jit(solution)/shard_map/ppermute | solution.py:199
  31.9 0.2 collective-permute-done.12.refs_14_
  32.1 1.5 %collective-permute-done.16.refs_18_ = bf16[544,128]{1,0:T(8,128)(2,1)S(1)} collective-permute-done((bf16[544,128]{1,0:T(8,128)(2,1)S(1)}, bf16[544,128]{1,0:T(8,128)(2,1)S(1)}, u32[]{:S(2)}, u32[]{:S(2)}) %collective-permute-start.16) | collective-permute-done | bytes 139296 | tf_op jit(solution)/shard_map/ppermute | solution.py:199
  33.6 2.8 %shard_map.75 = f32[2,128,128]{2,1,0:T(8,128)S(1)} custom-call(s32[8,4]{1,0:T(8,128)S(4)} %get-tuple-element.19.refs_0_, bf16[4,512,512]{2,1,0:T(8,128)(2,1)S(1)} %get-tuple-element.20.refs_1_, bf16[7,512,512]{2,1,0:T(8,128)(2,1)S(1)} %collective-permute-done.2.refs_2_, bf16[544,128]{1,0:T(8,128)(2,1)S(1)} %shard_map.73.refs_3_, ...), custom_call_target="tpu_custom_call" | custom-call | tf_op jit(solution)/shard_map/pallas_call | solution.py:178
  36.4 0.6 %collective-permute-start.18 = (f32[128,128]{1,0:T(8,128)S(1)}, f32[128,128]{1,0:T(8,128)S(1)}, u32[]{:S(2)}, u32[]{:S(2)}) collective-permute-start(f32[128,128]{1,0:T(8,128)S(1)} %get-tuple-element.24), channel_id=1, source_target_pairs={{0,4},{1,5},{2,6},{3,7},{4,0},{5,1},{6,2},{7,3},{8,12},{9,13},{10,... | collective-permute-start | bytes 196616 | tf_op jit(solution)/shard_map/ppermute | solution.py:199
  37.0 1.4 %collective-permute-start.19 = (f32[128,128]{1,0:T(8,128)S(1)}, f32[128,128]{1,0:T(8,128)S(1)}, u32[]{:S(2)}, u32[]{:S(2)}) collective-permute-start(f32[128,128]{1,0:T(8,128)S(1)} %get-tuple-element.23), channel_id=1, source_target_pairs={{0,6},{1,7},{2,4},{3,5},{4,2},{5,3},{6,0},{7,1},{8,14},{9,15},{10,... | collective-permute-start | bytes 196616 | tf_op jit(solution)/shard_map/ppermute | solution.py:199
  38.4 1.5 %collective-permute-start.17 = (f32[128,128]{1,0:T(8,128)S(1)}, f32[128,128]{1,0:T(8,128)S(1)}, u32[]{:S(2)}, u32[]{:S(2)}) collective-permute-start(f32[128,128]{1,0:T(8,128)S(1)} %get-tuple-element.23), channel_id=1, source_target_pairs={{0,2},{1,3},{2,0},{3,1},{4,6},{5,7},{6,4},{7,5},{8,10},{9,11},{10,... | collective-permute-start | bytes 196616 | tf_op jit(solution)/shard_map/ppermute | solution.py:199
  40.0 0.8 %collective-permute-done.18 = f32[128,128]{1,0:T(8,128)S(1)} collective-permute-done((f32[128,128]{1,0:T(8,128)S(1)}, f32[128,128]{1,0:T(8,128)S(1)}, u32[]{:S(2)}, u32[]{:S(2)}) %collective-permute-start.18) | collective-permute-done | bytes 65568 | tf_op jit(solution)/shard_map/ppermute | solution.py:199
  40.7 1.5 %collective-permute-done.19 = f32[128,128]{1,0:T(8,128)S(1)} collective-permute-done((f32[128,128]{1,0:T(8,128)S(1)}, f32[128,128]{1,0:T(8,128)S(1)}, u32[]{:S(2)}, u32[]{:S(2)}) %collective-permute-start.19) | collective-permute-done | bytes 65568 | tf_op jit(solution)/shard_map/ppermute | solution.py:199
  42.2 0.7 %collective-permute-done.17 = f32[128,128]{1,0:T(8,128)S(1)} collective-permute-done((f32[128,128]{1,0:T(8,128)S(1)}, f32[128,128]{1,0:T(8,128)S(1)}, u32[]{:S(2)}, u32[]{:S(2)}) %collective-permute-start.17) | collective-permute-done | bytes 65568 | tf_op jit(solution)/shard_map/ppermute | solution.py:199
  42.9 3.8 %collective-permute-start.22 = (f32[128,128]{1,0:T(8,128)S(1)}, f32[128,128]{1,0:T(8,128)S(1)}, u32[]{:S(2)}, u32[]{:S(2)}) collective-permute-start(f32[128,128]{1,0:T(8,128)S(1)} %add_add_fusion), channel_id=1, source_target_pairs={{0,24},{1,25},{2,26},{3,27},{4,28},{5,29},{6,30},{7,31},{8,16},{9,... | collective-permute-start | bytes 196616 | tf_op jit(solution)/shard_map/ppermute | solution.py:199
  46.7 0.0 collective-permute-start.21
  46.7 0.7 %collective-permute-start.20 = (f32[128,128]{1,0:T(8,128)S(1)}, f32[128,128]{1,0:T(8,128)S(1)}, u32[]{:S(2)}, u32[]{:S(2)}) collective-permute-start(f32[128,128]{1,0:T(8,128)S(1)} %add_add_fusion), channel_id=1, source_target_pairs={{0,8},{1,9},{2,10},{3,11},{4,12},{5,13},{6,14},{7,15},{8,0},{9,1},... | collective-permute-start | bytes 196616 | tf_op jit(solution)/shard_map/ppermute | solution.py:199
  47.3 1.7 %collective-permute-done.22 = f32[128,128]{1,0:T(8,128)S(1)} collective-permute-done((f32[128,128]{1,0:T(8,128)S(1)}, f32[128,128]{1,0:T(8,128)S(1)}, u32[]{:S(2)}, u32[]{:S(2)}) %collective-permute-start.22) | collective-permute-done | bytes 65568 | tf_op jit(solution)/shard_map/ppermute | solution.py:199
  49.0 2.8 %collective-permute-done.21 = f32[128,128]{1,0:T(8,128)S(1)} collective-permute-done((f32[128,128]{1,0:T(8,128)S(1)}, f32[128,128]{1,0:T(8,128)S(1)}, u32[]{:S(2)}, u32[]{:S(2)}) %collective-permute-start.21) | collective-permute-done | bytes 65568 | tf_op jit(solution)/shard_map/ppermute | solution.py:199
  51.8 0.0 collective-permute-done.20
  51.8 0.6 %add_bitcast_fusion = f32[1,128,128]{2,1,0:T(8,128)} fusion(f32[128,128]{1,0:T(8,128)S(1)} %collective-permute-done.21, f32[128,128]{1,0:T(8,128)S(1)} %collective-permute-done.22, f32[128,128]{1,0:T(8,128)S(1)} %add_add_fusion, f32[128,128]{1,0:T(8,128)S(1)} %collective-permute-done.20), kind=kLoop, calls=%fused_computation.2 | loop fusion | flops 49152 | bytes 327680 | tf_op jit(solution)/shard_map/broadcast_in_dim | solution.py:251
  (9 shorter events, 0.0 us)
Async XLA Ops:
  0.7 2.4 %copy-start = (s32[7]{0:T(128)}, s32[7]{0:T(128)S(1)}, u32[]{:S(2)}) copy-start(s32[7]{0:T(128)S(1)} %bitcast_add_fusion.own_codes) | copy-start | bytes 88
  0.7 2.4 %collective-permute-start = (s32[7]{0:T(128)S(1)}, s32[7]{0:T(128)S(1)}, u32[]{:S(2)}, u32[]{:S(2)}) collective-permute-start(s32[7]{0:T(128)S(1)} %bitcast_add_fusion.own_codes), channel_id=1, source_target_pairs={{0,1},{1,0},{2,3},{3,2},{4,5},{5,4},{6,7},{7,6},{8,9},{9,8},{10,11... | collective-permute-start | bytes 92 | tf_op jit(solution)/shard_map/ppermute | solution.py:199
  1.1 13.1 %collective-permute-start.2 = (bf16[7,512,512]{2,1,0:T(8,128)(2,1)}, bf16[7,512,512]{2,1,0:T(8,128)(2,1)S(1)}, u32[]{:S(2)}, u32[]{:S(2)}) collective-permute-start(bf16[7,512,512]{2,1,0:T(8,128)(2,1)} %own_hbm.1), channel_id=1, source_target_pairs={{0,1},{1,0},{2,3},{3,2},{4,5},{5,4},{6,7},{7,6},{8,9},{9,8},{10,11... | collective-permute-start | bytes 11010056 | tf_op jit(solution)/shard_map/ppermute | solution.py:199
  3.1 25.9 %copy-start.1 = (s32[7]{0:T(128)}, s32[7]{0:T(128)S(1)}, u32[]{:S(2)}) copy-start(s32[7]{0:T(128)S(1)} %collective-permute-done.other_codes) | copy-start | bytes 88
  3.2 11.1 %collective-permute-start.1 = (bf16[544,128]{1,0:T(8,128)(2,1)S(1)}, bf16[544,128]{1,0:T(8,128)(2,1)S(1)}, u32[]{:S(2)}, u32[]{:S(2)}) collective-permute-start(bf16[544,128]{1,0:T(8,128)(2,1)S(1)} %shard_map.73.refs_3_), channel_id=1, source_target_pairs={{0,16},{1,17},{2,18},{3,19},{4,20},{5,21},{6,22},{7,23},{8,24},{9,... | collective-permute-start | bytes 417800 | tf_op jit(solution)/shard_map/ppermute | solution.py:199
  7.2 8.5 %collective-permute-start.6 = (bf16[544,128]{1,0:T(8,128)(2,1)S(1)}, bf16[544,128]{1,0:T(8,128)(2,1)S(1)}, u32[]{:S(2)}, u32[]{:S(2)}) collective-permute-start(bf16[544,128]{1,0:T(8,128)(2,1)S(1)} %shard_map.73.refs_3_), channel_id=1, source_target_pairs={{0,8},{1,9},{2,10},{3,11},{4,12},{5,13},{6,14},{7,15},{8,0},{9,1},... | collective-permute-start | bytes 417800 | tf_op jit(solution)/shard_map/ppermute | solution.py:199
  8.8 9.0 %collective-permute-start.4 = (bf16[544,128]{1,0:T(8,128)(2,1)S(1)}, bf16[544,128]{1,0:T(8,128)(2,1)S(1)}, u32[]{:S(2)}, u32[]{:S(2)}) collective-permute-start(bf16[544,128]{1,0:T(8,128)(2,1)S(1)} %shard_map.73.refs_3_), channel_id=1, source_target_pairs={{0,4},{1,5},{2,6},{3,7},{4,0},{5,1},{6,2},{7,3},{8,12},{9,13},{10,... | collective-permute-start | bytes 417800 | tf_op jit(solution)/shard_map/ppermute | solution.py:199
  10.3 8.0 %collective-permute-start.3 = (bf16[544,128]{1,0:T(8,128)(2,1)S(1)}, bf16[544,128]{1,0:T(8,128)(2,1)S(1)}, u32[]{:S(2)}, u32[]{:S(2)}) collective-permute-start(bf16[544,128]{1,0:T(8,128)(2,1)S(1)} %shard_map.73.refs_3_), channel_id=1, source_target_pairs={{0,2},{1,3},{2,0},{3,1},{4,6},{5,7},{6,4},{7,5},{8,10},{9,11},{10,... | collective-permute-start | bytes 417800 | tf_op jit(solution)/shard_map/ppermute | solution.py:199
  14.2 6.6 %collective-permute-start.11 = (bf16[544,128]{1,0:T(8,128)(2,1)S(1)}, bf16[544,128]{1,0:T(8,128)(2,1)S(1)}, u32[]{:S(2)}, u32[]{:S(2)}) collective-permute-start(bf16[544,128]{1,0:T(8,128)(2,1)S(1)} %collective-permute-done.1.refs_11_), channel_id=1, source_target_pairs={{0,4},{1,5},{2,6},{3,7},{4,0},{5,1},{6,2},{7,3},{8,12},{9,13},{10,... | collective-permute-start | bytes 417800 | tf_op jit(solution)/shard_map/ppermute | solution.py:199
  15.8 7.9 %collective-permute-start.8 = (bf16[544,128]{1,0:T(8,128)(2,1)S(1)}, bf16[544,128]{1,0:T(8,128)(2,1)S(1)}, u32[]{:S(2)}, u32[]{:S(2)}) collective-permute-start(bf16[544,128]{1,0:T(8,128)(2,1)S(1)} %collective-permute-done.6.refs_7_), channel_id=1, source_target_pairs={{0,4},{1,5},{2,6},{3,7},{4,0},{5,1},{6,2},{7,3},{8,12},{9,13},{10,... | collective-permute-start | bytes 417800 | tf_op jit(solution)/shard_map/ppermute | solution.py:199
  16.3 8.7 %collective-permute-start.7 = (bf16[544,128]{1,0:T(8,128)(2,1)S(1)}, bf16[544,128]{1,0:T(8,128)(2,1)S(1)}, u32[]{:S(2)}, u32[]{:S(2)}) collective-permute-start(bf16[544,128]{1,0:T(8,128)(2,1)S(1)} %collective-permute-done.6.refs_7_), channel_id=1, source_target_pairs={{0,2},{1,3},{2,0},{3,1},{4,6},{5,7},{6,4},{7,5},{8,10},{9,11},{10,... | collective-permute-start | bytes 417800 | tf_op jit(solution)/shard_map/ppermute | solution.py:199
  17.9 8.1 %collective-permute-start.10 = (bf16[544,128]{1,0:T(8,128)(2,1)S(1)}, bf16[544,128]{1,0:T(8,128)(2,1)S(1)}, u32[]{:S(2)}, u32[]{:S(2)}) collective-permute-start(bf16[544,128]{1,0:T(8,128)(2,1)S(1)} %collective-permute-done.1.refs_11_), channel_id=1, source_target_pairs={{0,2},{1,3},{2,0},{3,1},{4,6},{5,7},{6,4},{7,5},{8,10},{9,11},{10,... | collective-permute-start | bytes 417800 | tf_op jit(solution)/shard_map/ppermute | solution.py:199
  18.3 8.7 %collective-permute-start.5 = (bf16[544,128]{1,0:T(8,128)(2,1)S(1)}, bf16[544,128]{1,0:T(8,128)(2,1)S(1)}, u32[]{:S(2)}, u32[]{:S(2)}) collective-permute-start(bf16[544,128]{1,0:T(8,128)(2,1)S(1)} %collective-permute-done.3.refs_4_), channel_id=1, source_target_pairs={{0,4},{1,5},{2,6},{3,7},{4,0},{5,1},{6,2},{7,3},{8,12},{9,13},{10,... | collective-permute-start | bytes 417800 | tf_op jit(solution)/shard_map/ppermute | solution.py:199
  20.9 7.7 %collective-permute-start.15 = (bf16[544,128]{1,0:T(8,128)(2,1)S(1)}, bf16[544,128]{1,0:T(8,128)(2,1)S(1)}, u32[]{:S(2)}, u32[]{:S(2)}) collective-permute-start(bf16[544,128]{1,0:T(8,128)(2,1)S(1)} %collective-permute-done.11.refs_13_), channel_id=1, source_target_pairs={{0,8},{1,9},{2,10},{3,11},{4,12},{5,13},{6,14},{7,15},{8,0},{9,1},... | collective-permute-start | bytes 417800 | tf_op jit(solution)/shard_map/ppermute | solution.py:199
  23.7 7.5 %collective-permute-start.9 = (bf16[544,128]{1,0:T(8,128)(2,1)S(1)}, bf16[544,128]{1,0:T(8,128)(2,1)S(1)}, u32[]{:S(2)}, u32[]{:S(2)}) collective-permute-start(bf16[544,128]{1,0:T(8,128)(2,1)S(1)} %collective-permute-done.8.refs_9_), channel_id=1, source_target_pairs={{0,2},{1,3},{2,0},{3,1},{4,6},{5,7},{6,4},{7,5},{8,10},{9,11},{10,... | collective-permute-start | bytes 417800 | tf_op jit(solution)/shard_map/ppermute | solution.py:199
  25.0 6.2 %collective-permute-start.13 = (bf16[544,128]{1,0:T(8,128)(2,1)S(1)}, bf16[544,128]{1,0:T(8,128)(2,1)S(1)}, u32[]{:S(2)}, u32[]{:S(2)}) collective-permute-start(bf16[544,128]{1,0:T(8,128)(2,1)S(1)} %collective-permute-done.1.refs_11_), channel_id=1, source_target_pairs={{0,8},{1,9},{2,10},{3,11},{4,12},{5,13},{6,14},{7,15},{8,0},{9,1},... | collective-permute-start | bytes 417800 | tf_op jit(solution)/shard_map/ppermute | solution.py:199
  25.9 6.0 %collective-permute-start.14 = (bf16[544,128]{1,0:T(8,128)(2,1)S(1)}, bf16[544,128]{1,0:T(8,128)(2,1)S(1)}, u32[]{:S(2)}, u32[]{:S(2)}) collective-permute-start(bf16[544,128]{1,0:T(8,128)(2,1)S(1)} %collective-permute-done.10.refs_12_), channel_id=1, source_target_pairs={{0,8},{1,9},{2,10},{3,11},{4,12},{5,13},{6,14},{7,15},{8,0},{9,1},... | collective-permute-start | bytes 417800 | tf_op jit(solution)/shard_map/ppermute | solution.py:199
  27.0 5.1 %collective-permute-start.12 = (bf16[544,128]{1,0:T(8,128)(2,1)S(1)}, bf16[544,128]{1,0:T(8,128)(2,1)S(1)}, u32[]{:S(2)}, u32[]{:S(2)}) collective-permute-start(bf16[544,128]{1,0:T(8,128)(2,1)S(1)} %collective-permute-done.10.refs_12_), channel_id=1, source_target_pairs={{0,4},{1,5},{2,6},{3,7},{4,0},{5,1},{6,2},{7,3},{8,12},{9,13},{10,... | collective-permute-start | bytes 417800 | tf_op jit(solution)/shard_map/ppermute | solution.py:199
  28.5 5.1 %collective-permute-start.16 = (bf16[544,128]{1,0:T(8,128)(2,1)S(1)}, bf16[544,128]{1,0:T(8,128)(2,1)S(1)}, u32[]{:S(2)}, u32[]{:S(2)}) collective-permute-start(bf16[544,128]{1,0:T(8,128)(2,1)S(1)} %collective-permute-done.15.refs_17_), channel_id=1, source_target_pairs={{0,2},{1,3},{2,0},{3,1},{4,6},{5,7},{6,4},{7,5},{8,10},{9,11},{10,... | collective-permute-start | bytes 417800 | tf_op jit(solution)/shard_map/ppermute | solution.py:199
  36.4 4.3 %collective-permute-start.18 = (f32[128,128]{1,0:T(8,128)S(1)}, f32[128,128]{1,0:T(8,128)S(1)}, u32[]{:S(2)}, u32[]{:S(2)}) collective-permute-start(f32[128,128]{1,0:T(8,128)S(1)} %get-tuple-element.24), channel_id=1, source_target_pairs={{0,4},{1,5},{2,6},{3,7},{4,0},{5,1},{6,2},{7,3},{8,12},{9,13},{10,... | collective-permute-start | bytes 196616 | tf_op jit(solution)/shard_map/ppermute | solution.py:199
  37.0 5.2 %collective-permute-start.19 = (f32[128,128]{1,0:T(8,128)S(1)}, f32[128,128]{1,0:T(8,128)S(1)}, u32[]{:S(2)}, u32[]{:S(2)}) collective-permute-start(f32[128,128]{1,0:T(8,128)S(1)} %get-tuple-element.23), channel_id=1, source_target_pairs={{0,6},{1,7},{2,4},{3,5},{4,2},{5,3},{6,0},{7,1},{8,14},{9,15},{10,... | collective-permute-start | bytes 196616 | tf_op jit(solution)/shard_map/ppermute | solution.py:199
  38.4 4.4 %collective-permute-start.17 = (f32[128,128]{1,0:T(8,128)S(1)}, f32[128,128]{1,0:T(8,128)S(1)}, u32[]{:S(2)}, u32[]{:S(2)}) collective-permute-start(f32[128,128]{1,0:T(8,128)S(1)} %get-tuple-element.23), channel_id=1, source_target_pairs={{0,2},{1,3},{2,0},{3,1},{4,6},{5,7},{6,4},{7,5},{8,10},{9,11},{10,... | collective-permute-start | bytes 196616 | tf_op jit(solution)/shard_map/ppermute | solution.py:199
  42.9 6.1 %collective-permute-start.22 = (f32[128,128]{1,0:T(8,128)S(1)}, f32[128,128]{1,0:T(8,128)S(1)}, u32[]{:S(2)}, u32[]{:S(2)}) collective-permute-start(f32[128,128]{1,0:T(8,128)S(1)} %add_add_fusion), channel_id=1, source_target_pairs={{0,24},{1,25},{2,26},{3,27},{4,28},{5,29},{6,30},{7,31},{8,16},{9,... | collective-permute-start | bytes 196616 | tf_op jit(solution)/shard_map/ppermute | solution.py:199
  46.7 5.2 %collective-permute-start.21 = (f32[128,128]{1,0:T(8,128)S(1)}, f32[128,128]{1,0:T(8,128)S(1)}, u32[]{:S(2)}, u32[]{:S(2)}) collective-permute-start(f32[128,128]{1,0:T(8,128)S(1)} %add_add_fusion), channel_id=1, source_target_pairs={{0,16},{1,17},{2,18},{3,19},{4,20},{5,21},{6,22},{7,23},{8,24},{9,... | collective-permute-start | bytes 196616 | tf_op jit(solution)/shard_map/ppermute | solution.py:199
  46.7 5.2 %collective-permute-start.20 = (f32[128,128]{1,0:T(8,128)S(1)}, f32[128,128]{1,0:T(8,128)S(1)}, u32[]{:S(2)}, u32[]{:S(2)}) collective-permute-start(f32[128,128]{1,0:T(8,128)S(1)} %add_add_fusion), channel_id=1, source_target_pairs={{0,8},{1,9},{2,10},{3,11},{4,12},{5,13},{6,14},{7,15},{8,0},{9,1},... | collective-permute-start | bytes 196616 | tf_op jit(solution)/shard_map/ppermute | solution.py:199

commit v4 on v3

--- a/solution.py
+++ b/solution.py
@@ -7,7 +7,7 @@
 
 AXES = ("grp", "reg")
 CAP = 2
-CHUNKS = 4
+CHUNKS = 2
 VMEM_LIMIT = 48 * 1024 * 1024
 
 
@@ -199,23 +199,27 @@
     return lax.ppermute(array, AXES, [(i, i ^ mask) for i in range(count)])
 
 
-def gather(packed, count, tied):
+def gather(packed, count, blocks, codes):
     y, x, near = 2, 4, 8
     far = [1 << n for n in range(3, count.bit_length() - 1)]
-    column = {0: packed, far[-1]: swap(packed, far[-1], count)}
-    column[far[-1]], tied = lax.optimization_barrier((column[far[-1]], tied))
-    for bit in reversed(far[:-1]):
-        for mask in list(column):
-            column[mask ^ bit] = swap(column[mask], bit, count)
+    column = {0: packed}
+    for bit in reversed(far):
+        for mask, array in list(column.items()):
+            if bit == near and mask == far[-1]:
+                array, blocks = lax.optimization_barrier((array, blocks))
+            column[mask ^ bit] = swap(array, bit, count)
     found = dict(column)
     for mask in sorted(column):
         if mask & near and mask != near:
             over_x, over_y = (swap(found[mask ^ near ^ bit], near, count) for bit in (x, y))
         else:
             over_x, over_y = (swap(column[mask], bit, count) for bit in (x, y))
-        corner = swap(over_x, y, count) if mask & near else swap(over_y, x, count)
+        sent = over_x if mask & near else over_y
+        if mask == 0:
+            sent, codes = lax.optimization_barrier((sent, codes))
+        corner = swap(sent, y if mask & near else x, count)
         found.update({mask ^ x: over_x, mask ^ y: over_y, mask ^ x ^ y: corner})
-    return sorted(found.items()), tied
+    return sorted(found.items()), blocks, codes
 
 
 def total(values):
@@ -233,8 +237,7 @@
     codes = (block_col * groups + block_row) * regions + block_region[:, 0]
     codes = (codes, swap(codes, 1, count))
     packed = pack(panel_index, orbitals[0, 0], occupied[0, 0])
-    packed, codes = lax.optimization_barrier((packed, codes))
-    found, (codes, other) = gather(packed, count, (codes, other))
+    found, other, codes = gather(packed, count, other, codes)
     labels, blocks = collect(codes, screening, regions // 2)
     sums = partial_sigma(labels, blocks, other, found, regions // 2, points, occ_count)
     stage = []

time: 52.7 us -> 51.6 us (0.979)
  other arithmetic: 1.36 us -> 0.67 us
    add x1, other arithmetic: 0.69 us -> 0.01 us  [shards(): codes = (block_col * groups + block_row) * regions + block_region[:, 0]]
  transfers between devices with their start and end apart: 23 -> 23, of which waited for: 11 -> 12; matrix products, arithmetic and copies ran while one was open for 0% -> 0% of each run, Pallas kernels for 8% -> 8%
where the time goes in v4:
time: 51.6 us; the launch traced here: 51.4 us
  starting transfers between devices  28.2 us (55%)
  waiting for transfers between devices  15.6 us (30%)
  Pallas kernels  6.79 us (13%)
  other arithmetic  0.67 us (1%)
    ppermute x23, starting transfers between devices, swap(): return lax.ppermute(array, AXES, [(i, i ^ mask) for i in range(count)])  28.2 us
    ppermute x23, waiting for transfers between devices, swap(): return lax.ppermute(array, AXES, [(i, i ^ mask) for i in range(count)])  15.6 us
    pallas_call x1, Pallas kernels, partial_sigma(): pl.pallas_call(lambda *refs: sigma_kernel(places, points, occ_count, *ref...  2.8 us
    pallas_call x1, Pallas kernels, collect(): pl.pallas_call(collect_kernel, out_shape=(pltpu.SMEM((2 * half, 4), jnp.i...  2.27 us
    pallas_call x1, Pallas kernels, pack(): pl.pallas_call(pack_kernel, out_shape=pltpu.VMEM((points + occ_rows, widt...  1.71 us
  transfers between devices with their start and end apart: 23, of which 12 were waited for; matrix products, arithmetic and copies ran while one was open for 0% of the time, Pallas kernels for 8%

profile of v4, /device:TPU:0, one launch (start us, length us, event | category | flops | bytes accessed | tf_op | source)
XLA Modules:
  0.0 51.4 jit_solution(3038779215259120087)
XLA Ops:
  0.0 0.5 collective-permute-start.3
  0.5 1.7 %shard_map.73.refs_3_ = bf16[544,128]{1,0:T(8,128)(2,1)S(1)} custom-call(s32[1,128]{1,0:T(1,128)} %bitcast.15, bf16[512,1024]{1,0:T(8,128)(2,1)} %bitcast.13, bf16[8,512]{1,0:T(8,128)(2,1)} %bitcast.14), custom_call_target="tpu_custom_call" | custom-call | flops 40000000000 | tf_op jit(solution)/shard_map/pallas_call | solution.py:53
  2.2 2.6 %collective-permute-start.6 = (bf16[544,128]{1,0:T(8,128)(2,1)S(1)}, bf16[544,128]{1,0:T(8,128)(2,1)S(1)}, u32[]{:S(2)}, u32[]{:S(2)}) collective-permute-start(bf16[544,128]{1,0:T(8,128)(2,1)S(1)} %shard_map.73.refs_3_), channel_id=1, source_target_pairs={{0,8},{1,9},{2,10},{3,11},{4,12},{5,13},{6,14},{7,15},{8,0},{9,1},... | collective-permute-start | bytes 417800 | tf_op jit(solution)/shard_map/ppermute | solution.py:199
  4.8 2.6 %collective-permute-start.2 = (bf16[544,128]{1,0:T(8,128)(2,1)S(1)}, bf16[544,128]{1,0:T(8,128)(2,1)S(1)}, u32[]{:S(2)}, u32[]{:S(2)}) collective-permute-start(bf16[544,128]{1,0:T(8,128)(2,1)S(1)} %shard_map.73.refs_3_), channel_id=1, source_target_pairs={{0,16},{1,17},{2,18},{3,19},{4,20},{5,21},{6,22},{7,23},{8,24},{9,... | collective-permute-start | bytes 417800 | tf_op jit(solution)/shard_map/ppermute | solution.py:199
  7.4 1.5 %collective-permute-start = (bf16[544,128]{1,0:T(8,128)(2,1)S(1)}, bf16[544,128]{1,0:T(8,128)(2,1)S(1)}, u32[]{:S(2)}, u32[]{:S(2)}) collective-permute-start(bf16[544,128]{1,0:T(8,128)(2,1)S(1)} %shard_map.73.refs_3_), channel_id=1, source_target_pairs={{0,2},{1,3},{2,0},{3,1},{4,6},{5,7},{6,4},{7,5},{8,10},{9,11},{10,... | collective-permute-start | bytes 417800 | tf_op jit(solution)/shard_map/ppermute | solution.py:199
  8.9 0.0 copy-start
  9.0 0.1 collective-permute-start.1
  9.0 1.1 %collective-permute-done.1.other_codes = s32[7]{0:T(128)S(1)} collective-permute-done((s32[7]{0:T(128)S(1)}, s32[7]{0:T(128)S(1)}, u32[]{:S(2)}, u32[]{:S(2)}) %collective-permute-start.1) | collective-permute-done | bytes 60 | tf_op jit(solution)/shard_map/ppermute | solution.py:199
  10.1 1.5 %collective-permute-start.4 = (bf16[544,128]{1,0:T(8,128)(2,1)S(1)}, bf16[544,128]{1,0:T(8,128)(2,1)S(1)}, u32[]{:S(2)}, u32[]{:S(2)}) collective-permute-start(bf16[544,128]{1,0:T(8,128)(2,1)S(1)} %shard_map.73.refs_3_), channel_id=1, source_target_pairs={{0,4},{1,5},{2,6},{3,7},{4,0},{5,1},{6,2},{7,3},{8,12},{9,13},{10,... | collective-permute-start | bytes 417800 | tf_op jit(solution)/shard_map/ppermute | solution.py:199
  11.6 2.9 %collective-permute-done.2.refs_11_ = bf16[544,128]{1,0:T(8,128)(2,1)S(1)} collective-permute-done((bf16[544,128]{1,0:T(8,128)(2,1)S(1)}, bf16[544,128]{1,0:T(8,128)(2,1)S(1)}, u32[]{:S(2)}, u32[]{:S(2)}) %collective-permute-start.2) | collective-permute-done | bytes 139296 | tf_op jit(solution)/shard_map/ppermute | solution.py:199
  14.6 1.5 %collective-permute-start.11 = (bf16[544,128]{1,0:T(8,128)(2,1)S(1)}, bf16[544,128]{1,0:T(8,128)(2,1)S(1)}, u32[]{:S(2)}, u32[]{:S(2)}) collective-permute-start(bf16[544,128]{1,0:T(8,128)(2,1)S(1)} %collective-permute-done.2.refs_11_), channel_id=1, source_target_pairs={{0,4},{1,5},{2,6},{3,7},{4,0},{5,1},{6,2},{7,3},{8,12},{9,13},{10,... | collective-permute-start | bytes 417800 | tf_op jit(solution)/shard_map/ppermute | solution.py:199
  16.0 0.0 collective-permute-done.refs_4_
  16.1 1.5 %collective-permute-start.10 = (bf16[544,128]{1,0:T(8,128)(2,1)S(1)}, bf16[544,128]{1,0:T(8,128)(2,1)S(1)}, u32[]{:S(2)}, u32[]{:S(2)}) collective-permute-start(bf16[544,128]{1,0:T(8,128)(2,1)S(1)} %collective-permute-done.2.refs_11_), channel_id=1, source_target_pairs={{0,2},{1,3},{2,0},{3,1},{4,6},{5,7},{6,4},{7,5},{8,10},{9,11},{10,... | collective-permute-start | bytes 417800 | tf_op jit(solution)/shard_map/ppermute | solution.py:199
  17.6 0.0 collective-permute-done.6.refs_7_
  17.6 0.5 %collective-permute-start.8 = (bf16[544,128]{1,0:T(8,128)(2,1)S(1)}, bf16[544,128]{1,0:T(8,128)(2,1)S(1)}, u32[]{:S(2)}, u32[]{:S(2)}) collective-permute-start(bf16[544,128]{1,0:T(8,128)(2,1)S(1)} %collective-permute-done.6.refs_7_), channel_id=1, source_target_pairs={{0,4},{1,5},{2,6},{3,7},{4,0},{5,1},{6,2},{7,3},{8,12},{9,13},{10,... | collective-permute-start | bytes 417800 | tf_op jit(solution)/shard_map/ppermute | solution.py:199
  18.1 0.0 collective-permute-done.4.refs_5_
  18.1 0.5 collective-permute-start.7
  18.6 1.8 %collective-permute-done.11.refs_13_ = bf16[544,128]{1,0:T(8,128)(2,1)S(1)} collective-permute-done((bf16[544,128]{1,0:T(8,128)(2,1)S(1)}, bf16[544,128]{1,0:T(8,128)(2,1)S(1)}, u32[]{:S(2)}, u32[]{:S(2)}) %collective-permute-start.11) | collective-permute-done | bytes 139296 | tf_op jit(solution)/shard_map/ppermute | solution.py:199
  20.4 0.4 collective-permute-start.15
  20.8 0.0 collective-permute-done.3.refs_2_
  20.8 2.3 %collective-permute-start.5 = (bf16[544,128]{1,0:T(8,128)(2,1)S(1)}, bf16[544,128]{1,0:T(8,128)(2,1)S(1)}, u32[]{:S(2)}, u32[]{:S(2)}) collective-permute-start(bf16[544,128]{1,0:T(8,128)(2,1)S(1)} %collective-permute-done.refs_4_), channel_id=1, source_target_pairs={{0,4},{1,5},{2,6},{3,7},{4,0},{5,1},{6,2},{7,3},{8,12},{9,13},{10,... | collective-permute-start | bytes 417800 | tf_op jit(solution)/shard_map/ppermute | solution.py:199
  23.1 0.9 %collective-permute-start.14 = (bf16[544,128]{1,0:T(8,128)(2,1)S(1)}, bf16[544,128]{1,0:T(8,128)(2,1)S(1)}, u32[]{:S(2)}, u32[]{:S(2)}) collective-permute-start(bf16[544,128]{1,0:T(8,128)(2,1)S(1)} %collective-permute-done.10.refs_12_), channel_id=1, source_target_pairs={{0,8},{1,9},{2,10},{3,11},{4,12},{5,13},{6,14},{7,15},{8,0},{9,1},... | collective-permute-start | bytes 417800 | tf_op jit(solution)/shard_map/ppermute | solution.py:199
  23.9 0.0 collective-permute-done.8.refs_9_
  23.9 0.5 %collective-permute-start.12 = (bf16[544,128]{1,0:T(8,128)(2,1)S(1)}, bf16[544,128]{1,0:T(8,128)(2,1)S(1)}, u32[]{:S(2)}, u32[]{:S(2)}) collective-permute-start(bf16[544,128]{1,0:T(8,128)(2,1)S(1)} %collective-permute-done.10.refs_12_), channel_id=1, source_target_pairs={{0,4},{1,5},{2,6},{3,7},{4,0},{5,1},{6,2},{7,3},{8,12},{9,13},{10,... | collective-permute-start | bytes 417800 | tf_op jit(solution)/shard_map/ppermute | solution.py:199
  24.5 0.7 %collective-permute-start.9 = (bf16[544,128]{1,0:T(8,128)(2,1)S(1)}, bf16[544,128]{1,0:T(8,128)(2,1)S(1)}, u32[]{:S(2)}, u32[]{:S(2)}) collective-permute-start(bf16[544,128]{1,0:T(8,128)(2,1)S(1)} %collective-permute-done.8.refs_9_), channel_id=1, source_target_pairs={{0,2},{1,3},{2,0},{3,1},{4,6},{5,7},{6,4},{7,5},{8,10},{9,11},{10,... | collective-permute-start | bytes 417800 | tf_op jit(solution)/shard_map/ppermute | solution.py:199
  25.2 0.3 collective-permute-done.15.refs_17_
  25.5 1.5 %collective-permute-start.16 = (bf16[544,128]{1,0:T(8,128)(2,1)S(1)}, bf16[544,128]{1,0:T(8,128)(2,1)S(1)}, u32[]{:S(2)}, u32[]{:S(2)}) collective-permute-start(bf16[544,128]{1,0:T(8,128)(2,1)S(1)} %collective-permute-done.15.refs_17_), channel_id=1, source_target_pairs={{0,2},{1,3},{2,0},{3,1},{4,6},{5,7},{6,4},{7,5},{8,10},{9,11},{10,... | collective-permute-start | bytes 417800 | tf_op jit(solution)/shard_map/ppermute | solution.py:199
  27.1 0.1 collective-permute-done.5.refs_6_
  27.1 1.1 %collective-permute-start.13 = (bf16[544,128]{1,0:T(8,128)(2,1)S(1)}, bf16[544,128]{1,0:T(8,128)(2,1)S(1)}, u32[]{:S(2)}, u32[]{:S(2)}) collective-permute-start(bf16[544,128]{1,0:T(8,128)(2,1)S(1)} %collective-permute-done.2.refs_11_), channel_id=1, source_target_pairs={{0,8},{1,9},{2,10},{3,11},{4,12},{5,13},{6,14},{7,15},{8,0},{9,1},... | collective-permute-start | bytes 417800 | tf_op jit(solution)/shard_map/ppermute | solution.py:199
  28.2 2.3 %shard_map.74 = (s32[8,4]{1,0:T(8,128)S(4)}, bf16[4,512,512]{2,1,0:T(8,128)(2,1)S(1)}) custom-call(s32[7]{0:T(128)} %copy-done, s32[7]{0:T(128)} %copy-done.1, bf16[7,512,512]{2,1,0:T(8,128)(2,1)} %own_hbm.1), custom_call_target="tpu_custom_call" | custom-call | tf_op jit(solution)/shard_map/pallas_call | solution.py:121
  30.5 0.0 collective-permute-done.14.refs_16_
  30.5 0.0 collective-permute-done.12.refs_14_
  30.5 0.5 %collective-permute-done.16.refs_18_ = bf16[544,128]{1,0:T(8,128)(2,1)S(1)} collective-permute-done((bf16[544,128]{1,0:T(8,128)(2,1)S(1)}, bf16[544,128]{1,0:T(8,128)(2,1)S(1)}, u32[]{:S(2)}, u32[]{:S(2)}) %collective-permute-start.16) | collective-permute-done | bytes 139296 | tf_op jit(solution)/shard_map/ppermute | solution.py:199
  31.0 1.1 %collective-permute-done.13.refs_15_ = bf16[544,128]{1,0:T(8,128)(2,1)S(1)} collective-permute-done((bf16[544,128]{1,0:T(8,128)(2,1)S(1)}, bf16[544,128]{1,0:T(8,128)(2,1)S(1)}, u32[]{:S(2)}, u32[]{:S(2)}) %collective-permute-start.13) | collective-permute-done | bytes 139296 | tf_op jit(solution)/shard_map/ppermute | solution.py:199
  32.2 2.8 %shard_map.75 = f32[2,128,128]{2,1,0:T(8,128)S(1)} custom-call(s32[8,4]{1,0:T(8,128)S(4)} %get-tuple-element.14.refs_0_, bf16[4,512,512]{2,1,0:T(8,128)(2,1)S(1)} %get-tuple-element.15.refs_1_, bf16[7,512,512]{2,1,0:T(8,128)(2,1)S(1)} %collective-permute-done.3.refs_2_, bf16[544,128]{1,0:T(8,128)(2,1)S(1)} %shard_map.73.refs_3_, ...), custom_call_target="tpu_custom_call" | custom-call | tf_op jit(solution)/shard_map/pallas_call | solution.py:178
  35.0 1.1 %collective-permute-start.18 = (f32[128,128]{1,0:T(8,128)S(1)}, f32[128,128]{1,0:T(8,128)S(1)}, u32[]{:S(2)}, u32[]{:S(2)}) collective-permute-start(f32[128,128]{1,0:T(8,128)S(1)} %get-tuple-element.20), channel_id=1, source_target_pairs={{0,4},{1,5},{2,6},{3,7},{4,0},{5,1},{6,2},{7,3},{8,12},{9,13},{10,... | collective-permute-start | bytes 196616 | tf_op jit(solution)/shard_map/ppermute | solution.py:199
  36.1 1.5 %collective-permute-start.19 = (f32[128,128]{1,0:T(8,128)S(1)}, f32[128,128]{1,0:T(8,128)S(1)}, u32[]{:S(2)}, u32[]{:S(2)}) collective-permute-start(f32[128,128]{1,0:T(8,128)S(1)} %get-tuple-element.19), channel_id=1, source_target_pairs={{0,6},{1,7},{2,4},{3,5},{4,2},{5,3},{6,0},{7,1},{8,14},{9,15},{10,... | collective-permute-start | bytes 196616 | tf_op jit(solution)/shard_map/ppermute | solution.py:199
  37.6 1.0 %collective-permute-start.17 = (f32[128,128]{1,0:T(8,128)S(1)}, f32[128,128]{1,0:T(8,128)S(1)}, u32[]{:S(2)}, u32[]{:S(2)}) collective-permute-start(f32[128,128]{1,0:T(8,128)S(1)} %get-tuple-element.19), channel_id=1, source_target_pairs={{0,2},{1,3},{2,0},{3,1},{4,6},{5,7},{6,4},{7,5},{8,10},{9,11},{10,... | collective-permute-start | bytes 196616 | tf_op jit(solution)/shard_map/ppermute | solution.py:199
  38.5 0.8 %collective-permute-done.18 = f32[128,128]{1,0:T(8,128)S(1)} collective-permute-done((f32[128,128]{1,0:T(8,128)S(1)}, f32[128,128]{1,0:T(8,128)S(1)}, u32[]{:S(2)}, u32[]{:S(2)}) %collective-permute-start.18) | collective-permute-done | bytes 65568 | tf_op jit(solution)/shard_map/ppermute | solution.py:199
  39.3 1.9 %collective-permute-done.19 = f32[128,128]{1,0:T(8,128)S(1)} collective-permute-done((f32[128,128]{1,0:T(8,128)S(1)}, f32[128,128]{1,0:T(8,128)S(1)}, u32[]{:S(2)}, u32[]{:S(2)}) %collective-permute-start.19) | collective-permute-done | bytes 65568 | tf_op jit(solution)/shard_map/ppermute | solution.py:199
  41.2 0.7 %collective-permute-done.17 = f32[128,128]{1,0:T(8,128)S(1)} collective-permute-done((f32[128,128]{1,0:T(8,128)S(1)}, f32[128,128]{1,0:T(8,128)S(1)}, u32[]{:S(2)}, u32[]{:S(2)}) %collective-permute-start.17) | collective-permute-done | bytes 65568 | tf_op jit(solution)/shard_map/ppermute | solution.py:199
  42.0 3.6 %collective-permute-start.22 = (f32[128,128]{1,0:T(8,128)S(1)}, f32[128,128]{1,0:T(8,128)S(1)}, u32[]{:S(2)}, u32[]{:S(2)}) collective-permute-start(f32[128,128]{1,0:T(8,128)S(1)} %add_add_fusion), channel_id=1, source_target_pairs={{0,24},{1,25},{2,26},{3,27},{4,28},{5,29},{6,30},{7,31},{8,16},{9,... | collective-permute-start | bytes 196616 | tf_op jit(solution)/shard_map/ppermute | solution.py:199
  45.6 0.0 collective-permute-start.21
  45.6 0.8 %collective-permute-start.20 = (f32[128,128]{1,0:T(8,128)S(1)}, f32[128,128]{1,0:T(8,128)S(1)}, u32[]{:S(2)}, u32[]{:S(2)}) collective-permute-start(f32[128,128]{1,0:T(8,128)S(1)} %add_add_fusion), channel_id=1, source_target_pairs={{0,8},{1,9},{2,10},{3,11},{4,12},{5,13},{6,14},{7,15},{8,0},{9,1},... | collective-permute-start | bytes 196616 | tf_op jit(solution)/shard_map/ppermute | solution.py:199
  46.4 1.7 %collective-permute-done.22 = f32[128,128]{1,0:T(8,128)S(1)} collective-permute-done((f32[128,128]{1,0:T(8,128)S(1)}, f32[128,128]{1,0:T(8,128)S(1)}, u32[]{:S(2)}, u32[]{:S(2)}) %collective-permute-start.22) | collective-permute-done | bytes 65568 | tf_op jit(solution)/shard_map/ppermute | solution.py:199
  48.1 2.7 %collective-permute-done.21 = f32[128,128]{1,0:T(8,128)S(1)} collective-permute-done((f32[128,128]{1,0:T(8,128)S(1)}, f32[128,128]{1,0:T(8,128)S(1)}, u32[]{:S(2)}, u32[]{:S(2)}) %collective-permute-start.21) | collective-permute-done | bytes 65568 | tf_op jit(solution)/shard_map/ppermute | solution.py:199
  50.8 0.0 collective-permute-done.20
  50.8 0.6 %add_bitcast_fusion = f32[1,128,128]{2,1,0:T(8,128)} fusion(f32[128,128]{1,0:T(8,128)S(1)} %collective-permute-done.21, f32[128,128]{1,0:T(8,128)S(1)} %collective-permute-done.22, f32[128,128]{1,0:T(8,128)S(1)} %add_add_fusion, f32[128,128]{1,0:T(8,128)S(1)} %collective-permute-done.20), kind=kLoop, calls=%fused_computation.2 | loop fusion | flops 49152 | bytes 327680 | tf_op jit(solution)/shard_map/broadcast_in_dim | solution.py:254
  (15 shorter events, 0.1 us)
Async XLA Ops:
  0.0 20.8 %collective-permute-start.3 = (bf16[7,512,512]{2,1,0:T(8,128)(2,1)}, bf16[7,512,512]{2,1,0:T(8,128)(2,1)S(1)}, u32[]{:S(2)}, u32[]{:S(2)}) collective-permute-start(bf16[7,512,512]{2,1,0:T(8,128)(2,1)} %own_hbm.1), channel_id=1, source_target_pairs={{0,1},{1,0},{2,3},{3,2},{4,5},{5,4},{6,7},{7,6},{8,9},{9,8},{10,11... | collective-permute-start | bytes 11010056 | tf_op jit(solution)/shard_map/ppermute | solution.py:199
  0.5 8.5 %copy-start.2 = (s32[7,1]{0,1:T(1,128)S(1)}, s32[7,1]{0,1:T(1,128)}, u32[]{:S(2)}) copy-start(s32[7,1]{0,1:T(1,128)} %param.11) | copy-start | bytes 88
  0.5 8.5 %copy-start.3 = (s32[7]{0:T(128)S(1)}, s32[7]{0:T(128)}, u32[]{:S(2)}) copy-start(s32[7]{0:T(128)} %param.12) | copy-start | bytes 88
  0.5 8.5 %copy-start.4 = (s32[7]{0:T(128)S(1)}, s32[7]{0:T(128)}, u32[]{:S(2)}) copy-start(s32[7]{0:T(128)} %param.13) | copy-start | bytes 88
  2.2 15.4 %collective-permute-start.6 = (bf16[544,128]{1,0:T(8,128)(2,1)S(1)}, bf16[544,128]{1,0:T(8,128)(2,1)S(1)}, u32[]{:S(2)}, u32[]{:S(2)}) collective-permute-start(bf16[544,128]{1,0:T(8,128)(2,1)S(1)} %shard_map.73.refs_3_), channel_id=1, source_target_pairs={{0,8},{1,9},{2,10},{3,11},{4,12},{5,13},{6,14},{7,15},{8,0},{9,1},... | collective-permute-start | bytes 417800 | tf_op jit(solution)/shard_map/ppermute | solution.py:199
  4.8 9.7 %collective-permute-start.2 = (bf16[544,128]{1,0:T(8,128)(2,1)S(1)}, bf16[544,128]{1,0:T(8,128)(2,1)S(1)}, u32[]{:S(2)}, u32[]{:S(2)}) collective-permute-start(bf16[544,128]{1,0:T(8,128)(2,1)S(1)} %shard_map.73.refs_3_), channel_id=1, source_target_pairs={{0,16},{1,17},{2,18},{3,19},{4,20},{5,21},{6,22},{7,23},{8,24},{9,... | collective-permute-start | bytes 417800 | tf_op jit(solution)/shard_map/ppermute | solution.py:199
  7.4 8.6 %collective-permute-start = (bf16[544,128]{1,0:T(8,128)(2,1)S(1)}, bf16[544,128]{1,0:T(8,128)(2,1)S(1)}, u32[]{:S(2)}, u32[]{:S(2)}) collective-permute-start(bf16[544,128]{1,0:T(8,128)(2,1)S(1)} %shard_map.73.refs_3_), channel_id=1, source_target_pairs={{0,2},{1,3},{2,0},{3,1},{4,6},{5,7},{6,4},{7,5},{8,10},{9,11},{10,... | collective-permute-start | bytes 417800 | tf_op jit(solution)/shard_map/ppermute | solution.py:199
  8.9 19.2 %copy-start = (s32[7]{0:T(128)}, s32[7]{0:T(128)S(1)}, u32[]{:S(2)}) copy-start(s32[7]{0:T(128)S(1)} %bitcast_add_fusion.own_codes) | copy-start | bytes 88
  9.0 1.2 %collective-permute-start.1 = (s32[7]{0:T(128)S(1)}, s32[7]{0:T(128)S(1)}, u32[]{:S(2)}, u32[]{:S(2)}) collective-permute-start(s32[7]{0:T(128)S(1)} %bitcast_add_fusion.own_codes), channel_id=1, source_target_pairs={{0,1},{1,0},{2,3},{3,2},{4,5},{5,4},{6,7},{7,6},{8,9},{9,8},{10,11... | collective-permute-start | bytes 92 | tf_op jit(solution)/shard_map/ppermute | solution.py:199
  10.1 18.0 %copy-start.1 = (s32[7]{0:T(128)}, s32[7]{0:T(128)S(1)}, u32[]{:S(2)}) copy-start(s32[7]{0:T(128)S(1)} %collective-permute-done.1.other_codes) | copy-start | bytes 88
  10.1 8.0 %collective-permute-start.4 = (bf16[544,128]{1,0:T(8,128)(2,1)S(1)}, bf16[544,128]{1,0:T(8,128)(2,1)S(1)}, u32[]{:S(2)}, u32[]{:S(2)}) collective-permute-start(bf16[544,128]{1,0:T(8,128)(2,1)S(1)} %shard_map.73.refs_3_), channel_id=1, source_target_pairs={{0,4},{1,5},{2,6},{3,7},{4,0},{5,1},{6,2},{7,3},{8,12},{9,13},{10,... | collective-permute-start | bytes 417800 | tf_op jit(solution)/shard_map/ppermute | solution.py:199
  14.6 5.9 %collective-permute-start.11 = (bf16[544,128]{1,0:T(8,128)(2,1)S(1)}, bf16[544,128]{1,0:T(8,128)(2,1)S(1)}, u32[]{:S(2)}, u32[]{:S(2)}) collective-permute-start(bf16[544,128]{1,0:T(8,128)(2,1)S(1)} %collective-permute-done.2.refs_11_), channel_id=1, source_target_pairs={{0,4},{1,5},{2,6},{3,7},{4,0},{5,1},{6,2},{7,3},{8,12},{9,13},{10,... | collective-permute-start | bytes 417800 | tf_op jit(solution)/shard_map/ppermute | solution.py:199
  16.1 7.0 %collective-permute-start.10 = (bf16[544,128]{1,0:T(8,128)(2,1)S(1)}, bf16[544,128]{1,0:T(8,128)(2,1)S(1)}, u32[]{:S(2)}, u32[]{:S(2)}) collective-permute-start(bf16[544,128]{1,0:T(8,128)(2,1)S(1)} %collective-permute-done.2.refs_11_), channel_id=1, source_target_pairs={{0,2},{1,3},{2,0},{3,1},{4,6},{5,7},{6,4},{7,5},{8,10},{9,11},{10,... | collective-permute-start | bytes 417800 | tf_op jit(solution)/shard_map/ppermute | solution.py:199
  17.6 6.4 %collective-permute-start.8 = (bf16[544,128]{1,0:T(8,128)(2,1)S(1)}, bf16[544,128]{1,0:T(8,128)(2,1)S(1)}, u32[]{:S(2)}, u32[]{:S(2)}) collective-permute-start(bf16[544,128]{1,0:T(8,128)(2,1)S(1)} %collective-permute-done.6.refs_7_), channel_id=1, source_target_pairs={{0,4},{1,5},{2,6},{3,7},{4,0},{5,1},{6,2},{7,3},{8,12},{9,13},{10,... | collective-permute-start | bytes 417800 | tf_op jit(solution)/shard_map/ppermute | solution.py:199
  18.1 6.4 %collective-permute-start.7 = (bf16[544,128]{1,0:T(8,128)(2,1)S(1)}, bf16[544,128]{1,0:T(8,128)(2,1)S(1)}, u32[]{:S(2)}, u32[]{:S(2)}) collective-permute-start(bf16[544,128]{1,0:T(8,128)(2,1)S(1)} %collective-permute-done.6.refs_7_), channel_id=1, source_target_pairs={{0,2},{1,3},{2,0},{3,1},{4,6},{5,7},{6,4},{7,5},{8,10},{9,11},{10,... | collective-permute-start | bytes 417800 | tf_op jit(solution)/shard_map/ppermute | solution.py:199
  20.4 5.1 %collective-permute-start.15 = (bf16[544,128]{1,0:T(8,128)(2,1)S(1)}, bf16[544,128]{1,0:T(8,128)(2,1)S(1)}, u32[]{:S(2)}, u32[]{:S(2)}) collective-permute-start(bf16[544,128]{1,0:T(8,128)(2,1)S(1)} %collective-permute-done.11.refs_13_), channel_id=1, source_target_pairs={{0,8},{1,9},{2,10},{3,11},{4,12},{5,13},{6,14},{7,15},{8,0},{9,1},... | collective-permute-start | bytes 417800 | tf_op jit(solution)/shard_map/ppermute | solution.py:199
  20.8 6.3 %collective-permute-start.5 = (bf16[544,128]{1,0:T(8,128)(2,1)S(1)}, bf16[544,128]{1,0:T(8,128)(2,1)S(1)}, u32[]{:S(2)}, u32[]{:S(2)}) collective-permute-start(bf16[544,128]{1,0:T(8,128)(2,1)S(1)} %collective-permute-done.refs_4_), channel_id=1, source_target_pairs={{0,4},{1,5},{2,6},{3,7},{4,0},{5,1},{6,2},{7,3},{8,12},{9,13},{10,... | collective-permute-start | bytes 417800 | tf_op jit(solution)/shard_map/ppermute | solution.py:199
  23.1 7.4 %collective-permute-start.14 = (bf16[544,128]{1,0:T(8,128)(2,1)S(1)}, bf16[544,128]{1,0:T(8,128)(2,1)S(1)}, u32[]{:S(2)}, u32[]{:S(2)}) collective-permute-start(bf16[544,128]{1,0:T(8,128)(2,1)S(1)} %collective-permute-done.10.refs_12_), channel_id=1, source_target_pairs={{0,8},{1,9},{2,10},{3,11},{4,12},{5,13},{6,14},{7,15},{8,0},{9,1},... | collective-permute-start | bytes 417800 | tf_op jit(solution)/shard_map/ppermute | solution.py:199
  23.9 6.5 %collective-permute-start.12 = (bf16[544,128]{1,0:T(8,128)(2,1)S(1)}, bf16[544,128]{1,0:T(8,128)(2,1)S(1)}, u32[]{:S(2)}, u32[]{:S(2)}) collective-permute-start(bf16[544,128]{1,0:T(8,128)(2,1)S(1)} %collective-permute-done.10.refs_12_), channel_id=1, source_target_pairs={{0,4},{1,5},{2,6},{3,7},{4,0},{5,1},{6,2},{7,3},{8,12},{9,13},{10,... | collective-permute-start | bytes 417800 | tf_op jit(solution)/shard_map/ppermute | solution.py:199
  24.5 6.0 %collective-permute-start.9 = (bf16[544,128]{1,0:T(8,128)(2,1)S(1)}, bf16[544,128]{1,0:T(8,128)(2,1)S(1)}, u32[]{:S(2)}, u32[]{:S(2)}) collective-permute-start(bf16[544,128]{1,0:T(8,128)(2,1)S(1)} %collective-permute-done.8.refs_9_), channel_id=1, source_target_pairs={{0,2},{1,3},{2,0},{3,1},{4,6},{5,7},{6,4},{7,5},{8,10},{9,11},{10,... | collective-permute-start | bytes 417800 | tf_op jit(solution)/shard_map/ppermute | solution.py:199
  25.5 5.5 %collective-permute-start.16 = (bf16[544,128]{1,0:T(8,128)(2,1)S(1)}, bf16[544,128]{1,0:T(8,128)(2,1)S(1)}, u32[]{:S(2)}, u32[]{:S(2)}) collective-permute-start(bf16[544,128]{1,0:T(8,128)(2,1)S(1)} %collective-permute-done.15.refs_17_), channel_id=1, source_target_pairs={{0,2},{1,3},{2,0},{3,1},{4,6},{5,7},{6,4},{7,5},{8,10},{9,11},{10,... | collective-permute-start | bytes 417800 | tf_op jit(solution)/shard_map/ppermute | solution.py:199
  27.1 5.1 %collective-permute-start.13 = (bf16[544,128]{1,0:T(8,128)(2,1)S(1)}, bf16[544,128]{1,0:T(8,128)(2,1)S(1)}, u32[]{:S(2)}, u32[]{:S(2)}) collective-permute-start(bf16[544,128]{1,0:T(8,128)(2,1)S(1)} %collective-permute-done.2.refs_11_), channel_id=1, source_target_pairs={{0,8},{1,9},{2,10},{3,11},{4,12},{5,13},{6,14},{7,15},{8,0},{9,1},... | collective-permute-start | bytes 417800 | tf_op jit(solution)/shard_map/ppermute | solution.py:199
  35.0 4.3 %collective-permute-start.18 = (f32[128,128]{1,0:T(8,128)S(1)}, f32[128,128]{1,0:T(8,128)S(1)}, u32[]{:S(2)}, u32[]{:S(2)}) collective-permute-start(f32[128,128]{1,0:T(8,128)S(1)} %get-tuple-element.20), channel_id=1, source_target_pairs={{0,4},{1,5},{2,6},{3,7},{4,0},{5,1},{6,2},{7,3},{8,12},{9,13},{10,... | collective-permute-start | bytes 196616 | tf_op jit(solution)/shard_map/ppermute | solution.py:199
  36.1 5.2 %collective-permute-start.19 = (f32[128,128]{1,0:T(8,128)S(1)}, f32[128,128]{1,0:T(8,128)S(1)}, u32[]{:S(2)}, u32[]{:S(2)}) collective-permute-start(f32[128,128]{1,0:T(8,128)S(1)} %get-tuple-element.19), channel_id=1, source_target_pairs={{0,6},{1,7},{2,4},{3,5},{4,2},{5,3},{6,0},{7,1},{8,14},{9,15},{10,... | collective-permute-start | bytes 196616 | tf_op jit(solution)/shard_map/ppermute | solution.py:199
  37.6 4.4 %collective-permute-start.17 = (f32[128,128]{1,0:T(8,128)S(1)}, f32[128,128]{1,0:T(8,128)S(1)}, u32[]{:S(2)}, u32[]{:S(2)}) collective-permute-start(f32[128,128]{1,0:T(8,128)S(1)} %get-tuple-element.19), channel_id=1, source_target_pairs={{0,2},{1,3},{2,0},{3,1},{4,6},{5,7},{6,4},{7,5},{8,10},{9,11},{10,... | collective-permute-start | bytes 196616 | tf_op jit(solution)/shard_map/ppermute | solution.py:199
  42.0 6.1 %collective-permute-start.22 = (f32[128,128]{1,0:T(8,128)S(1)}, f32[128,128]{1,0:T(8,128)S(1)}, u32[]{:S(2)}, u32[]{:S(2)}) collective-permute-start(f32[128,128]{1,0:T(8,128)S(1)} %add_add_fusion), channel_id=1, source_target_pairs={{0,24},{1,25},{2,26},{3,27},{4,28},{5,29},{6,30},{7,31},{8,16},{9,... | collective-permute-start | bytes 196616 | tf_op jit(solution)/shard_map/ppermute | solution.py:199
  45.6 5.2 %collective-permute-start.21 = (f32[128,128]{1,0:T(8,128)S(1)}, f32[128,128]{1,0:T(8,128)S(1)}, u32[]{:S(2)}, u32[]{:S(2)}) collective-permute-start(f32[128,128]{1,0:T(8,128)S(1)} %add_add_fusion), channel_id=1, source_target_pairs={{0,16},{1,17},{2,18},{3,19},{4,20},{5,21},{6,22},{7,23},{8,24},{9,... | collective-permute-start | bytes 196616 | tf_op jit(solution)/shard_map/ppermute | solution.py:199
  45.6 5.2 %collective-permute-start.20 = (f32[128,128]{1,0:T(8,128)S(1)}, f32[128,128]{1,0:T(8,128)S(1)}, u32[]{:S(2)}, u32[]{:S(2)}) collective-permute-start(f32[128,128]{1,0:T(8,128)S(1)} %add_add_fusion), channel_id=1, source_target_pairs={{0,8},{1,9},{2,10},{3,11},{4,12},{5,13},{6,14},{7,15},{8,0},{9,1},... | collective-permute-start | bytes 196616 | tf_op jit(solution)/shard_map/ppermute | solution.py:199

commit v5 on v4

--- a/solution.py
+++ b/solution.py
@@ -61,7 +61,6 @@
             pltpu.VMEM(occupied.shape, jnp.bfloat16),
             pltpu.SemaphoreType.DMA((CHUNKS + 2,)),
         ],
-        cost_estimate=pl.CostEstimate(flops=4 * 10**10, bytes_accessed=0, transcendentals=0),
         compiler_params=pltpu.CompilerParams(vmem_limit_bytes=VMEM_LIMIT),
     )(in_hbm(panel_index[None, :]), in_hbm(orbitals), in_hbm(occupied))
 
@@ -240,17 +239,18 @@
     found, other, codes = gather(packed, count, other, codes)
     labels, blocks = collect(codes, screening, regions // 2)
     sums = partial_sigma(labels, blocks, other, found, regions // 2, points, occ_count)
+    top = count // 2
     stage = []
-    for low in (0, regions):
+    for far in (0, top):
         for mask in range(0, regions, 2):
             part = sums[mask // 2]
-            stage.append(swap(part, low ^ mask, count) if low ^ mask else part)
+            stage.append(swap(part, far ^ mask, count) if far ^ mask else part)
     sigma = total(stage)
-    bit = 2 * regions
-    while bit < count:
-        top = min(4 * bit, count)
-        sigma = total([sigma] + [swap(sigma, mask, count) for mask in range(bit, top, bit)])
-        bit = top
+    bit = regions
+    while bit < top:
+        end = min(4 * bit, top)
+        sigma = total([sigma] + [swap(sigma, mask, count) for mask in range(bit, end, bit)])
+        bit = end
     return sigma[None]
 
 

time: 51.6 us -> 51.5 us (level)
  starting transfers between devices: 28.2 us -> 27.4 us
  other arithmetic: 0.67 us -> 1.36 us
    ppermute x23, starting transfers between devices: 28.2 us -> 27.4 us  [swap(): return lax.ppermute(array, AXES, [(i, i ^ mask) for i in range(count)])]
    add x1, other arithmetic: 0.01 us -> 0.69 us  [shards(): codes = (block_col * groups + block_row) * regions + block_region[:, 0]]
  transfers between devices with their start and end apart: 23 -> 23, of which waited for: 12 -> 12; matrix products, arithmetic and copies ran while one was open for 0% -> 1% of each run, Pallas kernels for 8% -> 8%
where the time goes in v5:
time: 51.5 us; the launch traced here: 51.3 us
  starting transfers between devices  27.4 us (53%)
  waiting for transfers between devices  15.7 us (30%)
  Pallas kernels  6.77 us (13%)
  other arithmetic  1.36 us (3%)
    ppermute x23, starting transfers between devices, swap(): return lax.ppermute(array, AXES, [(i, i ^ mask) for i in range(count)])  27.4 us
    ppermute x23, waiting for transfers between devices, swap(): return lax.ppermute(array, AXES, [(i, i ^ mask) for i in range(count)])  15.7 us
    pallas_call x1, Pallas kernels, partial_sigma(): pl.pallas_call(lambda *refs: sigma_kernel(places, points, occ_count, *ref...  2.8 us
    pallas_call x1, Pallas kernels, collect(): pl.pallas_call(collect_kernel, out_shape=(pltpu.SMEM((2 * half, 4), jnp.i...  2.3 us
    pallas_call x1, Pallas kernels, pack(): pl.pallas_call(pack_kernel, out_shape=pltpu.VMEM((points + occ_rows, widt...  1.67 us
  transfers between devices with their start and end apart: 23, of which 12 were waited for; matrix products, arithmetic and copies ran while one was open for 1% of the time, Pallas kernels for 8%

profile of v5, /device:TPU:0, one launch (start us, length us, event | category | flops | bytes accessed | tf_op | source)
XLA Modules:
  0.0 51.3 jit_solution(1262397477230214370)
XLA Ops:
  0.0 0.5 collective-permute-start.3
  0.5 1.7 %shard_map.73.refs_3_ = bf16[544,128]{1,0:T(8,128)(2,1)S(1)} custom-call(s32[1,128]{1,0:T(1,128)} %bitcast.15, bf16[512,1024]{1,0:T(8,128)(2,1)} %bitcast.13, bf16[8,512]{1,0:T(8,128)(2,1)} %bitcast.14), custom_call_target="tpu_custom_call" | custom-call | tf_op jit(solution)/shard_map/pallas_call | solution.py:53
  2.1 2.6 %collective-permute-start.6 = (bf16[544,128]{1,0:T(8,128)(2,1)S(1)}, bf16[544,128]{1,0:T(8,128)(2,1)S(1)}, u32[]{:S(2)}, u32[]{:S(2)}) collective-permute-start(bf16[544,128]{1,0:T(8,128)(2,1)S(1)} %shard_map.73.refs_3_), channel_id=1, source_target_pairs={{0,8},{1,9},{2,10},{3,11},{4,12},{5,13},{6,14},{7,15},{8,0},{9,1},... | collective-permute-start | bytes 417800 | tf_op jit(solution)/shard_map/ppermute | solution.py:198
  4.8 2.6 %collective-permute-start.2 = (bf16[544,128]{1,0:T(8,128)(2,1)S(1)}, bf16[544,128]{1,0:T(8,128)(2,1)S(1)}, u32[]{:S(2)}, u32[]{:S(2)}) collective-permute-start(bf16[544,128]{1,0:T(8,128)(2,1)S(1)} %shard_map.73.refs_3_), channel_id=1, source_target_pairs={{0,16},{1,17},{2,18},{3,19},{4,20},{5,21},{6,22},{7,23},{8,24},{9,... | collective-permute-start | bytes 417800 | tf_op jit(solution)/shard_map/ppermute | solution.py:198
  7.4 1.5 %collective-permute-start = (bf16[544,128]{1,0:T(8,128)(2,1)S(1)}, bf16[544,128]{1,0:T(8,128)(2,1)S(1)}, u32[]{:S(2)}, u32[]{:S(2)}) collective-permute-start(bf16[544,128]{1,0:T(8,128)(2,1)S(1)} %shard_map.73.refs_3_), channel_id=1, source_target_pairs={{0,2},{1,3},{2,0},{3,1},{4,6},{5,7},{6,4},{7,5},{8,10},{9,11},{10,... | collective-permute-start | bytes 417800 | tf_op jit(solution)/shard_map/ppermute | solution.py:198
  8.9 0.7 %bitcast_add_fusion.own_codes = s32[7]{0:T(128)S(1)} fusion(s32[7,1]{0,1:T(1,128)} %param.11, s32[7]{0:T(128)} %param.12, s32[7]{0:T(128)} %param.13), kind=kLoop, calls=%fused_computation.4 | loop fusion | flops 28 | bytes 112 | tf_op jit(solution)/shard_map/add | solution.py:236
  9.6 0.0 collective-permute-start.1
  9.6 1.1 %collective-permute-done.1.other_codes = s32[7]{0:T(128)S(1)} collective-permute-done((s32[7]{0:T(128)S(1)}, s32[7]{0:T(128)S(1)}, u32[]{:S(2)}, u32[]{:S(2)}) %collective-permute-start.1) | collective-permute-done | bytes 60 | tf_op jit(solution)/shard_map/ppermute | solution.py:198
  10.7 1.5 %collective-permute-start.4 = (bf16[544,128]{1,0:T(8,128)(2,1)S(1)}, bf16[544,128]{1,0:T(8,128)(2,1)S(1)}, u32[]{:S(2)}, u32[]{:S(2)}) collective-permute-start(bf16[544,128]{1,0:T(8,128)(2,1)S(1)} %shard_map.73.refs_3_), channel_id=1, source_target_pairs={{0,4},{1,5},{2,6},{3,7},{4,0},{5,1},{6,2},{7,3},{8,12},{9,13},{10,... | collective-permute-start | bytes 417800 | tf_op jit(solution)/shard_map/ppermute | solution.py:198
  12.2 2.3 %collective-permute-done.2.refs_11_ = bf16[544,128]{1,0:T(8,128)(2,1)S(1)} collective-permute-done((bf16[544,128]{1,0:T(8,128)(2,1)S(1)}, bf16[544,128]{1,0:T(8,128)(2,1)S(1)}, u32[]{:S(2)}, u32[]{:S(2)}) %collective-permute-start.2) | collective-permute-done | bytes 139296 | tf_op jit(solution)/shard_map/ppermute | solution.py:198
  14.5 1.5 %collective-permute-start.11 = (bf16[544,128]{1,0:T(8,128)(2,1)S(1)}, bf16[544,128]{1,0:T(8,128)(2,1)S(1)}, u32[]{:S(2)}, u32[]{:S(2)}) collective-permute-start(bf16[544,128]{1,0:T(8,128)(2,1)S(1)} %collective-permute-done.2.refs_11_), channel_id=1, source_target_pairs={{0,4},{1,5},{2,6},{3,7},{4,0},{5,1},{6,2},{7,3},{8,12},{9,13},{10,... | collective-permute-start | bytes 417800 | tf_op jit(solution)/shard_map/ppermute | solution.py:198
  16.0 0.0 collective-permute-done.refs_4_
  16.0 1.5 %collective-permute-start.10 = (bf16[544,128]{1,0:T(8,128)(2,1)S(1)}, bf16[544,128]{1,0:T(8,128)(2,1)S(1)}, u32[]{:S(2)}, u32[]{:S(2)}) collective-permute-start(bf16[544,128]{1,0:T(8,128)(2,1)S(1)} %collective-permute-done.2.refs_11_), channel_id=1, source_target_pairs={{0,2},{1,3},{2,0},{3,1},{4,6},{5,7},{6,4},{7,5},{8,10},{9,11},{10,... | collective-permute-start | bytes 417800 | tf_op jit(solution)/shard_map/ppermute | solution.py:198
  17.5 0.0 collective-permute-done.6.refs_7_
  17.5 0.5 %collective-permute-start.8 = (bf16[544,128]{1,0:T(8,128)(2,1)S(1)}, bf16[544,128]{1,0:T(8,128)(2,1)S(1)}, u32[]{:S(2)}, u32[]{:S(2)}) collective-permute-start(bf16[544,128]{1,0:T(8,128)(2,1)S(1)} %collective-permute-done.6.refs_7_), channel_id=1, source_target_pairs={{0,4},{1,5},{2,6},{3,7},{4,0},{5,1},{6,2},{7,3},{8,12},{9,13},{10,... | collective-permute-start | bytes 417800 | tf_op jit(solution)/shard_map/ppermute | solution.py:198
  18.1 0.0 collective-permute-done.4.refs_5_
  18.1 0.5 collective-permute-start.7
  18.6 2.4 %collective-permute-done.11.refs_13_ = bf16[544,128]{1,0:T(8,128)(2,1)S(1)} collective-permute-done((bf16[544,128]{1,0:T(8,128)(2,1)S(1)}, bf16[544,128]{1,0:T(8,128)(2,1)S(1)}, u32[]{:S(2)}, u32[]{:S(2)}) %collective-permute-start.11) | collective-permute-done | bytes 139296 | tf_op jit(solution)/shard_map/ppermute | solution.py:198
  21.0 0.0 collective-permute-start.15
  21.0 0.0 collective-permute-done.3.refs_2_
  21.0 2.1 %collective-permute-start.5 = (bf16[544,128]{1,0:T(8,128)(2,1)S(1)}, bf16[544,128]{1,0:T(8,128)(2,1)S(1)}, u32[]{:S(2)}, u32[]{:S(2)}) collective-permute-start(bf16[544,128]{1,0:T(8,128)(2,1)S(1)} %collective-permute-done.refs_4_), channel_id=1, source_target_pairs={{0,4},{1,5},{2,6},{3,7},{4,0},{5,1},{6,2},{7,3},{8,12},{9,13},{10,... | collective-permute-start | bytes 417800 | tf_op jit(solution)/shard_map/ppermute | solution.py:198
  23.0 0.0 collective-permute-done.10.refs_12_
  23.0 1.5 %collective-permute-start.14 = (bf16[544,128]{1,0:T(8,128)(2,1)S(1)}, bf16[544,128]{1,0:T(8,128)(2,1)S(1)}, u32[]{:S(2)}, u32[]{:S(2)}) collective-permute-start(bf16[544,128]{1,0:T(8,128)(2,1)S(1)} %collective-permute-done.10.refs_12_), channel_id=1, source_target_pairs={{0,8},{1,9},{2,10},{3,11},{4,12},{5,13},{6,14},{7,15},{8,0},{9,1},... | collective-permute-start | bytes 417800 | tf_op jit(solution)/shard_map/ppermute | solution.py:198
  24.5 0.0 collective-permute-done.8.refs_9_
  24.5 0.6 %collective-permute-start.12 = (bf16[544,128]{1,0:T(8,128)(2,1)S(1)}, bf16[544,128]{1,0:T(8,128)(2,1)S(1)}, u32[]{:S(2)}, u32[]{:S(2)}) collective-permute-start(bf16[544,128]{1,0:T(8,128)(2,1)S(1)} %collective-permute-done.10.refs_12_), channel_id=1, source_target_pairs={{0,4},{1,5},{2,6},{3,7},{4,0},{5,1},{6,2},{7,3},{8,12},{9,13},{10,... | collective-permute-start | bytes 417800 | tf_op jit(solution)/shard_map/ppermute | solution.py:198
  25.1 0.5 collective-permute-start.9
  25.5 0.5 collective-permute-done.15.refs_17_
  26.0 1.1 %collective-permute-start.16 = (bf16[544,128]{1,0:T(8,128)(2,1)S(1)}, bf16[544,128]{1,0:T(8,128)(2,1)S(1)}, u32[]{:S(2)}, u32[]{:S(2)}) collective-permute-start(bf16[544,128]{1,0:T(8,128)(2,1)S(1)} %collective-permute-done.15.refs_17_), channel_id=1, source_target_pairs={{0,2},{1,3},{2,0},{3,1},{4,6},{5,7},{6,4},{7,5},{8,10},{9,11},{10,... | collective-permute-start | bytes 417800 | tf_op jit(solution)/shard_map/ppermute | solution.py:198
  27.1 0.0 collective-permute-done.5.refs_6_
  27.1 1.0 %collective-permute-start.13 = (bf16[544,128]{1,0:T(8,128)(2,1)S(1)}, bf16[544,128]{1,0:T(8,128)(2,1)S(1)}, u32[]{:S(2)}, u32[]{:S(2)}) collective-permute-start(bf16[544,128]{1,0:T(8,128)(2,1)S(1)} %collective-permute-done.2.refs_11_), channel_id=1, source_target_pairs={{0,8},{1,9},{2,10},{3,11},{4,12},{5,13},{6,14},{7,15},{8,0},{9,1},... | collective-permute-start | bytes 417800 | tf_op jit(solution)/shard_map/ppermute | solution.py:198
  28.1 2.3 %shard_map.74 = (s32[8,4]{1,0:T(8,128)S(4)}, bf16[4,512,512]{2,1,0:T(8,128)(2,1)S(1)}) custom-call(s32[7]{0:T(128)} %copy-done, s32[7]{0:T(128)} %copy-done.1, bf16[7,512,512]{2,1,0:T(8,128)(2,1)} %own_hbm.1), custom_call_target="tpu_custom_call" | custom-call | tf_op jit(solution)/shard_map/pallas_call | solution.py:120
  30.4 0.0 collective-permute-done.14.refs_16_
  30.5 1.1 %collective-permute-done.16.refs_18_ = bf16[544,128]{1,0:T(8,128)(2,1)S(1)} collective-permute-done((bf16[544,128]{1,0:T(8,128)(2,1)S(1)}, bf16[544,128]{1,0:T(8,128)(2,1)S(1)}, u32[]{:S(2)}, u32[]{:S(2)}) %collective-permute-start.16) | collective-permute-done | bytes 139296 | tf_op jit(solution)/shard_map/ppermute | solution.py:198
  31.6 0.5 %collective-permute-done.13.refs_15_ = bf16[544,128]{1,0:T(8,128)(2,1)S(1)} collective-permute-done((bf16[544,128]{1,0:T(8,128)(2,1)S(1)}, bf16[544,128]{1,0:T(8,128)(2,1)S(1)}, u32[]{:S(2)}, u32[]{:S(2)}) %collective-permute-start.13) | collective-permute-done | bytes 139296 | tf_op jit(solution)/shard_map/ppermute | solution.py:198
  32.2 2.8 %shard_map.75 = f32[2,128,128]{2,1,0:T(8,128)S(1)} custom-call(s32[8,4]{1,0:T(8,128)S(4)} %get-tuple-element.14.refs_0_, bf16[4,512,512]{2,1,0:T(8,128)(2,1)S(1)} %get-tuple-element.15.refs_1_, bf16[7,512,512]{2,1,0:T(8,128)(2,1)S(1)} %collective-permute-done.3.refs_2_, bf16[544,128]{1,0:T(8,128)(2,1)S(1)} %shard_map.73.refs_3_, ...), custom_call_target="tpu_custom_call" | custom-call | tf_op jit(solution)/shard_map/pallas_call | solution.py:177
  35.0 1.9 %collective-permute-start.18 = (f32[128,128]{1,0:T(8,128)S(1)}, f32[128,128]{1,0:T(8,128)S(1)}, u32[]{:S(2)}, u32[]{:S(2)}) collective-permute-start(f32[128,128]{1,0:T(8,128)S(1)} %get-tuple-element.20), channel_id=1, source_target_pairs={{0,16},{1,17},{2,18},{3,19},{4,20},{5,21},{6,22},{7,23},{8,24},{9,... | collective-permute-start | bytes 196616 | tf_op jit(solution)/shard_map/ppermute | solution.py:198
  36.8 1.6 %collective-permute-start.19 = (f32[128,128]{1,0:T(8,128)S(1)}, f32[128,128]{1,0:T(8,128)S(1)}, u32[]{:S(2)}, u32[]{:S(2)}) collective-permute-start(f32[128,128]{1,0:T(8,128)S(1)} %get-tuple-element.19), channel_id=1, source_target_pairs={{0,18},{1,19},{2,16},{3,17},{4,22},{5,23},{6,20},{7,21},{8,26},{9,... | collective-permute-start | bytes 196616 | tf_op jit(solution)/shard_map/ppermute | solution.py:198
  38.4 1.0 %collective-permute-start.17 = (f32[128,128]{1,0:T(8,128)S(1)}, f32[128,128]{1,0:T(8,128)S(1)}, u32[]{:S(2)}, u32[]{:S(2)}) collective-permute-start(f32[128,128]{1,0:T(8,128)S(1)} %get-tuple-element.19), channel_id=1, source_target_pairs={{0,2},{1,3},{2,0},{3,1},{4,6},{5,7},{6,4},{7,5},{8,10},{9,11},{10,... | collective-permute-start | bytes 196616 | tf_op jit(solution)/shard_map/ppermute | solution.py:198
  39.4 1.5 %collective-permute-done.18 = f32[128,128]{1,0:T(8,128)S(1)} collective-permute-done((f32[128,128]{1,0:T(8,128)S(1)}, f32[128,128]{1,0:T(8,128)S(1)}, u32[]{:S(2)}, u32[]{:S(2)}) %collective-permute-start.18) | collective-permute-done | bytes 65568 | tf_op jit(solution)/shard_map/ppermute | solution.py:198
  40.9 2.1 %collective-permute-done.19 = f32[128,128]{1,0:T(8,128)S(1)} collective-permute-done((f32[128,128]{1,0:T(8,128)S(1)}, f32[128,128]{1,0:T(8,128)S(1)}, u32[]{:S(2)}, u32[]{:S(2)}) %collective-permute-start.19) | collective-permute-done | bytes 65568 | tf_op jit(solution)/shard_map/ppermute | solution.py:198
  43.0 0.4 collective-permute-done.17
  43.4 2.6 %collective-permute-start.22 = (f32[128,128]{1,0:T(8,128)S(1)}, f32[128,128]{1,0:T(8,128)S(1)}, u32[]{:S(2)}, u32[]{:S(2)}) collective-permute-start(f32[128,128]{1,0:T(8,128)S(1)} %add_add_fusion), channel_id=1, source_target_pairs={{0,12},{1,13},{2,14},{3,15},{4,8},{5,9},{6,10},{7,11},{8,4},{9,5},... | collective-permute-start | bytes 196616 | tf_op jit(solution)/shard_map/ppermute | solution.py:198
  46.0 0.5 collective-permute-start.21
  46.4 0.5 %collective-permute-start.20 = (f32[128,128]{1,0:T(8,128)S(1)}, f32[128,128]{1,0:T(8,128)S(1)}, u32[]{:S(2)}, u32[]{:S(2)}) collective-permute-start(f32[128,128]{1,0:T(8,128)S(1)} %add_add_fusion), channel_id=1, source_target_pairs={{0,4},{1,5},{2,6},{3,7},{4,0},{5,1},{6,2},{7,3},{8,12},{9,13},{10,... | collective-permute-start | bytes 196616 | tf_op jit(solution)/shard_map/ppermute | solution.py:198
  47.0 1.7 %collective-permute-done.22 = f32[128,128]{1,0:T(8,128)S(1)} collective-permute-done((f32[128,128]{1,0:T(8,128)S(1)}, f32[128,128]{1,0:T(8,128)S(1)}, u32[]{:S(2)}, u32[]{:S(2)}) %collective-permute-start.22) | collective-permute-done | bytes 65568 | tf_op jit(solution)/shard_map/ppermute | solution.py:198
  48.6 1.6 %collective-permute-done.21 = f32[128,128]{1,0:T(8,128)S(1)} collective-permute-done((f32[128,128]{1,0:T(8,128)S(1)}, f32[128,128]{1,0:T(8,128)S(1)}, u32[]{:S(2)}, u32[]{:S(2)}) %collective-permute-start.21) | collective-permute-done | bytes 65568 | tf_op jit(solution)/shard_map/ppermute | solution.py:198
  50.2 0.5 collective-permute-done.20
  50.7 0.6 %add_bitcast_fusion = f32[1,128,128]{2,1,0:T(8,128)} fusion(f32[128,128]{1,0:T(8,128)S(1)} %collective-permute-done.21, f32[128,128]{1,0:T(8,128)S(1)} %collective-permute-done.22, f32[128,128]{1,0:T(8,128)S(1)} %add_add_fusion, f32[128,128]{1,0:T(8,128)S(1)} %collective-permute-done.20), kind=kLoop, calls=%fused_computation.2 | loop fusion | flops 49152 | bytes 327680 | tf_op jit(solution)/shard_map/broadcast_in_dim | solution.py:254
  (9 shorter events, 0.0 us)
Async XLA Ops:
  0.0 21.0 %collective-permute-start.3 = (bf16[7,512,512]{2,1,0:T(8,128)(2,1)}, bf16[7,512,512]{2,1,0:T(8,128)(2,1)S(1)}, u32[]{:S(2)}, u32[]{:S(2)}) collective-permute-start(bf16[7,512,512]{2,1,0:T(8,128)(2,1)} %own_hbm.1), channel_id=1, source_target_pairs={{0,1},{1,0},{2,3},{3,2},{4,5},{5,4},{6,7},{7,6},{8,9},{9,8},{10,11... | collective-permute-start | bytes 11010056 | tf_op jit(solution)/shard_map/ppermute | solution.py:198
  2.1 15.4 %collective-permute-start.6 = (bf16[544,128]{1,0:T(8,128)(2,1)S(1)}, bf16[544,128]{1,0:T(8,128)(2,1)S(1)}, u32[]{:S(2)}, u32[]{:S(2)}) collective-permute-start(bf16[544,128]{1,0:T(8,128)(2,1)S(1)} %shard_map.73.refs_3_), channel_id=1, source_target_pairs={{0,8},{1,9},{2,10},{3,11},{4,12},{5,13},{6,14},{7,15},{8,0},{9,1},... | collective-permute-start | bytes 417800 | tf_op jit(solution)/shard_map/ppermute | solution.py:198
  4.8 9.7 %collective-permute-start.2 = (bf16[544,128]{1,0:T(8,128)(2,1)S(1)}, bf16[544,128]{1,0:T(8,128)(2,1)S(1)}, u32[]{:S(2)}, u32[]{:S(2)}) collective-permute-start(bf16[544,128]{1,0:T(8,128)(2,1)S(1)} %shard_map.73.refs_3_), channel_id=1, source_target_pairs={{0,16},{1,17},{2,18},{3,19},{4,20},{5,21},{6,22},{7,23},{8,24},{9,... | collective-permute-start | bytes 417800 | tf_op jit(solution)/shard_map/ppermute | solution.py:198
  7.4 8.6 %collective-permute-start = (bf16[544,128]{1,0:T(8,128)(2,1)S(1)}, bf16[544,128]{1,0:T(8,128)(2,1)S(1)}, u32[]{:S(2)}, u32[]{:S(2)}) collective-permute-start(bf16[544,128]{1,0:T(8,128)(2,1)S(1)} %shard_map.73.refs_3_), channel_id=1, source_target_pairs={{0,2},{1,3},{2,0},{3,1},{4,6},{5,7},{6,4},{7,5},{8,10},{9,11},{10,... | collective-permute-start | bytes 417800 | tf_op jit(solution)/shard_map/ppermute | solution.py:198
  9.6 18.5 %copy-start = (s32[7]{0:T(128)}, s32[7]{0:T(128)S(1)}, u32[]{:S(2)}) copy-start(s32[7]{0:T(128)S(1)} %bitcast_add_fusion.own_codes) | copy-start | bytes 88
  9.6 1.1 %collective-permute-start.1 = (s32[7]{0:T(128)S(1)}, s32[7]{0:T(128)S(1)}, u32[]{:S(2)}, u32[]{:S(2)}) collective-permute-start(s32[7]{0:T(128)S(1)} %bitcast_add_fusion.own_codes), channel_id=1, source_target_pairs={{0,1},{1,0},{2,3},{3,2},{4,5},{5,4},{6,7},{7,6},{8,9},{9,8},{10,11... | collective-permute-start | bytes 92 | tf_op jit(solution)/shard_map/ppermute | solution.py:198
  10.7 17.4 %copy-start.1 = (s32[7]{0:T(128)}, s32[7]{0:T(128)S(1)}, u32[]{:S(2)}) copy-start(s32[7]{0:T(128)S(1)} %collective-permute-done.1.other_codes) | copy-start | bytes 88
  10.7 7.4 %collective-permute-start.4 = (bf16[544,128]{1,0:T(8,128)(2,1)S(1)}, bf16[544,128]{1,0:T(8,128)(2,1)S(1)}, u32[]{:S(2)}, u32[]{:S(2)}) collective-permute-start(bf16[544,128]{1,0:T(8,128)(2,1)S(1)} %shard_map.73.refs_3_), channel_id=1, source_target_pairs={{0,4},{1,5},{2,6},{3,7},{4,0},{5,1},{6,2},{7,3},{8,12},{9,13},{10,... | collective-permute-start | bytes 417800 | tf_op jit(solution)/shard_map/ppermute | solution.py:198
  14.5 6.5 %collective-permute-start.11 = (bf16[544,128]{1,0:T(8,128)(2,1)S(1)}, bf16[544,128]{1,0:T(8,128)(2,1)S(1)}, u32[]{:S(2)}, u32[]{:S(2)}) collective-permute-start(bf16[544,128]{1,0:T(8,128)(2,1)S(1)} %collective-permute-done.2.refs_11_), channel_id=1, source_target_pairs={{0,4},{1,5},{2,6},{3,7},{4,0},{5,1},{6,2},{7,3},{8,12},{9,13},{10,... | collective-permute-start | bytes 417800 | tf_op jit(solution)/shard_map/ppermute | solution.py:198
  16.0 7.0 %collective-permute-start.10 = (bf16[544,128]{1,0:T(8,128)(2,1)S(1)}, bf16[544,128]{1,0:T(8,128)(2,1)S(1)}, u32[]{:S(2)}, u32[]{:S(2)}) collective-permute-start(bf16[544,128]{1,0:T(8,128)(2,1)S(1)} %collective-permute-done.2.refs_11_), channel_id=1, source_target_pairs={{0,2},{1,3},{2,0},{3,1},{4,6},{5,7},{6,4},{7,5},{8,10},{9,11},{10,... | collective-permute-start | bytes 417800 | tf_op jit(solution)/shard_map/ppermute | solution.py:198
  17.5 7.0 %collective-permute-start.8 = (bf16[544,128]{1,0:T(8,128)(2,1)S(1)}, bf16[544,128]{1,0:T(8,128)(2,1)S(1)}, u32[]{:S(2)}, u32[]{:S(2)}) collective-permute-start(bf16[544,128]{1,0:T(8,128)(2,1)S(1)} %collective-permute-done.6.refs_7_), channel_id=1, source_target_pairs={{0,4},{1,5},{2,6},{3,7},{4,0},{5,1},{6,2},{7,3},{8,12},{9,13},{10,... | collective-permute-start | bytes 417800 | tf_op jit(solution)/shard_map/ppermute | solution.py:198
  18.1 7.0 %collective-permute-start.7 = (bf16[544,128]{1,0:T(8,128)(2,1)S(1)}, bf16[544,128]{1,0:T(8,128)(2,1)S(1)}, u32[]{:S(2)}, u32[]{:S(2)}) collective-permute-start(bf16[544,128]{1,0:T(8,128)(2,1)S(1)} %collective-permute-done.6.refs_7_), channel_id=1, source_target_pairs={{0,2},{1,3},{2,0},{3,1},{4,6},{5,7},{6,4},{7,5},{8,10},{9,11},{10,... | collective-permute-start | bytes 417800 | tf_op jit(solution)/shard_map/ppermute | solution.py:198
  21.0 5.1 %collective-permute-start.15 = (bf16[544,128]{1,0:T(8,128)(2,1)S(1)}, bf16[544,128]{1,0:T(8,128)(2,1)S(1)}, u32[]{:S(2)}, u32[]{:S(2)}) collective-permute-start(bf16[544,128]{1,0:T(8,128)(2,1)S(1)} %collective-permute-done.11.refs_13_), channel_id=1, source_target_pairs={{0,8},{1,9},{2,10},{3,11},{4,12},{5,13},{6,14},{7,15},{8,0},{9,1},... | collective-permute-start | bytes 417800 | tf_op jit(solution)/shard_map/ppermute | solution.py:198
  21.0 6.1 %collective-permute-start.5 = (bf16[544,128]{1,0:T(8,128)(2,1)S(1)}, bf16[544,128]{1,0:T(8,128)(2,1)S(1)}, u32[]{:S(2)}, u32[]{:S(2)}) collective-permute-start(bf16[544,128]{1,0:T(8,128)(2,1)S(1)} %collective-permute-done.refs_4_), channel_id=1, source_target_pairs={{0,4},{1,5},{2,6},{3,7},{4,0},{5,1},{6,2},{7,3},{8,12},{9,13},{10,... | collective-permute-start | bytes 417800 | tf_op jit(solution)/shard_map/ppermute | solution.py:198
  23.0 7.4 %collective-permute-start.14 = (bf16[544,128]{1,0:T(8,128)(2,1)S(1)}, bf16[544,128]{1,0:T(8,128)(2,1)S(1)}, u32[]{:S(2)}, u32[]{:S(2)}) collective-permute-start(bf16[544,128]{1,0:T(8,128)(2,1)S(1)} %collective-permute-done.10.refs_12_), channel_id=1, source_target_pairs={{0,8},{1,9},{2,10},{3,11},{4,12},{5,13},{6,14},{7,15},{8,0},{9,1},... | collective-permute-start | bytes 417800 | tf_op jit(solution)/shard_map/ppermute | solution.py:198
  24.5 6.0 %collective-permute-start.12 = (bf16[544,128]{1,0:T(8,128)(2,1)S(1)}, bf16[544,128]{1,0:T(8,128)(2,1)S(1)}, u32[]{:S(2)}, u32[]{:S(2)}) collective-permute-start(bf16[544,128]{1,0:T(8,128)(2,1)S(1)} %collective-permute-done.10.refs_12_), channel_id=1, source_target_pairs={{0,4},{1,5},{2,6},{3,7},{4,0},{5,1},{6,2},{7,3},{8,12},{9,13},{10,... | collective-permute-start | bytes 417800 | tf_op jit(solution)/shard_map/ppermute | solution.py:198
  25.1 5.4 %collective-permute-start.9 = (bf16[544,128]{1,0:T(8,128)(2,1)S(1)}, bf16[544,128]{1,0:T(8,128)(2,1)S(1)}, u32[]{:S(2)}, u32[]{:S(2)}) collective-permute-start(bf16[544,128]{1,0:T(8,128)(2,1)S(1)} %collective-permute-done.8.refs_9_), channel_id=1, source_target_pairs={{0,2},{1,3},{2,0},{3,1},{4,6},{5,7},{6,4},{7,5},{8,10},{9,11},{10,... | collective-permute-start | bytes 417800 | tf_op jit(solution)/shard_map/ppermute | solution.py:198
  26.0 5.6 %collective-permute-start.16 = (bf16[544,128]{1,0:T(8,128)(2,1)S(1)}, bf16[544,128]{1,0:T(8,128)(2,1)S(1)}, u32[]{:S(2)}, u32[]{:S(2)}) collective-permute-start(bf16[544,128]{1,0:T(8,128)(2,1)S(1)} %collective-permute-done.15.refs_17_), channel_id=1, source_target_pairs={{0,2},{1,3},{2,0},{3,1},{4,6},{5,7},{6,4},{7,5},{8,10},{9,11},{10,... | collective-permute-start | bytes 417800 | tf_op jit(solution)/shard_map/ppermute | solution.py:198
  27.1 5.1 %collective-permute-start.13 = (bf16[544,128]{1,0:T(8,128)(2,1)S(1)}, bf16[544,128]{1,0:T(8,128)(2,1)S(1)}, u32[]{:S(2)}, u32[]{:S(2)}) collective-permute-start(bf16[544,128]{1,0:T(8,128)(2,1)S(1)} %collective-permute-done.2.refs_11_), channel_id=1, source_target_pairs={{0,8},{1,9},{2,10},{3,11},{4,12},{5,13},{6,14},{7,15},{8,0},{9,1},... | collective-permute-start | bytes 417800 | tf_op jit(solution)/shard_map/ppermute | solution.py:198
  35.0 5.9 %collective-permute-start.18 = (f32[128,128]{1,0:T(8,128)S(1)}, f32[128,128]{1,0:T(8,128)S(1)}, u32[]{:S(2)}, u32[]{:S(2)}) collective-permute-start(f32[128,128]{1,0:T(8,128)S(1)} %get-tuple-element.20), channel_id=1, source_target_pairs={{0,16},{1,17},{2,18},{3,19},{4,20},{5,21},{6,22},{7,23},{8,24},{9,... | collective-permute-start | bytes 196616 | tf_op jit(solution)/shard_map/ppermute | solution.py:198
  36.8 6.2 %collective-permute-start.19 = (f32[128,128]{1,0:T(8,128)S(1)}, f32[128,128]{1,0:T(8,128)S(1)}, u32[]{:S(2)}, u32[]{:S(2)}) collective-permute-start(f32[128,128]{1,0:T(8,128)S(1)} %get-tuple-element.19), channel_id=1, source_target_pairs={{0,18},{1,19},{2,16},{3,17},{4,22},{5,23},{6,20},{7,21},{8,26},{9,... | collective-permute-start | bytes 196616 | tf_op jit(solution)/shard_map/ppermute | solution.py:198
  38.4 5.0 %collective-permute-start.17 = (f32[128,128]{1,0:T(8,128)S(1)}, f32[128,128]{1,0:T(8,128)S(1)}, u32[]{:S(2)}, u32[]{:S(2)}) collective-permute-start(f32[128,128]{1,0:T(8,128)S(1)} %get-tuple-element.19), channel_id=1, source_target_pairs={{0,2},{1,3},{2,0},{3,1},{4,6},{5,7},{6,4},{7,5},{8,10},{9,11},{10,... | collective-permute-start | bytes 196616 | tf_op jit(solution)/shard_map/ppermute | solution.py:198
  43.4 5.2 %collective-permute-start.22 = (f32[128,128]{1,0:T(8,128)S(1)}, f32[128,128]{1,0:T(8,128)S(1)}, u32[]{:S(2)}, u32[]{:S(2)}) collective-permute-start(f32[128,128]{1,0:T(8,128)S(1)} %add_add_fusion), channel_id=1, source_target_pairs={{0,12},{1,13},{2,14},{3,15},{4,8},{5,9},{6,10},{7,11},{8,4},{9,5},... | collective-permute-start | bytes 196616 | tf_op jit(solution)/shard_map/ppermute | solution.py:198
  46.0 4.3 %collective-permute-start.21 = (f32[128,128]{1,0:T(8,128)S(1)}, f32[128,128]{1,0:T(8,128)S(1)}, u32[]{:S(2)}, u32[]{:S(2)}) collective-permute-start(f32[128,128]{1,0:T(8,128)S(1)} %add_add_fusion), channel_id=1, source_target_pairs={{0,8},{1,9},{2,10},{3,11},{4,12},{5,13},{6,14},{7,15},{8,0},{9,1},... | collective-permute-start | bytes 196616 | tf_op jit(solution)/shard_map/ppermute | solution.py:198
  46.4 4.3 %collective-permute-start.20 = (f32[128,128]{1,0:T(8,128)S(1)}, f32[128,128]{1,0:T(8,128)S(1)}, u32[]{:S(2)}, u32[]{:S(2)}) collective-permute-start(f32[128,128]{1,0:T(8,128)S(1)} %add_add_fusion), channel_id=1, source_target_pairs={{0,4},{1,5},{2,6},{3,7},{4,0},{5,1},{6,2},{7,3},{8,12},{9,13},{10,... | collective-permute-start | bytes 196616 | tf_op jit(solution)/shard_map/ppermute | solution.py:198

commit v6 on v5

--- a/solution.py
+++ b/solution.py
@@ -19,14 +19,11 @@
     return pltpu.with_memory_space_constraint(array, pltpu.VMEM)
 
 
-def pack_kernel(index_hbm, orbitals_hbm, occupied_hbm, packed_ref, index, orbitals, occupied, sems):
+def pack_kernel(index_hbm, orbitals_hbm, occupied, packed_ref, index, orbitals, sems):
     points, orbs = orbitals.shape
     width = index.shape[1]
     step = points // CHUNKS
-    copies = [
-        pltpu.make_async_copy(index_hbm, index, sems.at[CHUNKS + 1]),
-        pltpu.make_async_copy(occupied_hbm, occupied, sems.at[CHUNKS]),
-    ]
+    copies = [pltpu.make_async_copy(index_hbm, index, sems.at[CHUNKS])]
     for n in range(CHUNKS):
         rows = pl.ds(n * step, step)
         copies.append(pltpu.make_async_copy(orbitals_hbm.at[rows], orbitals.at[rows], sems.at[n]))
@@ -35,12 +32,11 @@
     copies[0].wait()
     numbers = lax.broadcasted_iota(jnp.int32, (orbs, width), 0)
     chosen = jnp.where(numbers == index[...], 1.0, 0.0).astype(jnp.bfloat16)
-    copies[1].wait()
     occ = occupied[...].astype(jnp.float32)
     slabs = [occ[:, at : at + width] for at in range(0, points, width)]
     packed_ref[points:, :] = jnp.concatenate(slabs, axis=0).astype(jnp.bfloat16)
     for n in range(CHUNKS):
-        copies[2 + n].wait()
+        copies[1 + n].wait()
         rows = slice(n * step, n * step + step)
         panel = jnp.dot(orbitals[rows, :], chosen, preferred_element_type=jnp.float32)
         packed_ref[rows, :] = panel.astype(jnp.bfloat16)
@@ -53,16 +49,16 @@
     return pl.pallas_call(
         pack_kernel,
         out_shape=pltpu.VMEM((points + occ_rows, width), jnp.bfloat16),
+        in_specs=[pl.BlockSpec(memory_space=pltpu.HBM)] * 2
+        + [pl.BlockSpec(memory_space=pltpu.VMEM)],
         out_specs=pl.BlockSpec(memory_space=pltpu.VMEM),
-        in_specs=[pl.BlockSpec(memory_space=pltpu.HBM)] * 3,
         scratch_shapes=[
             pltpu.VMEM((1, width), jnp.int32),
             pltpu.VMEM(orbitals.shape, jnp.bfloat16),
-            pltpu.VMEM(occupied.shape, jnp.bfloat16),
-            pltpu.SemaphoreType.DMA((CHUNKS + 2,)),
+            pltpu.SemaphoreType.DMA((CHUNKS + 1,)),
         ],
         compiler_params=pltpu.CompilerParams(vmem_limit_bytes=VMEM_LIMIT),
-    )(in_hbm(panel_index[None, :]), in_hbm(orbitals), in_hbm(occupied))
+    )(in_hbm(panel_index[None, :]), in_hbm(orbitals), occupied)
 
 
 def collect_kernel(own_codes, other_codes, own_hbm, labels_ref, blocks_ref, own, other, sems):

time: 51.5 us -> 52.2 us (1.014)
  local copies, waits for them, and re-layouts: 0.02 us -> 0.71 us
    unnamed x4 -> x6, local copies, waits for them, and re-layouts: 0.01 us -> 0.7 us
  transfers between devices with their start and end apart: 23 -> 23, of which waited for: 12 -> 12; matrix products, arithmetic and copies ran while one was open for 1% -> 1% of each run, Pallas kernels for 8% -> 7%
where the time goes in v6:
time: 52.2 us; the launch traced here: 52 us
  starting transfers between devices  27.4 us (52%)
  waiting for transfers between devices  15.9 us (30%)
  Pallas kernels  6.58 us (13%)
  other arithmetic  1.36 us (3%)
  local copies, waits for them, and re-layouts  0.71 us (1%)
    ppermute x23, starting transfers between devices, swap(): return lax.ppermute(array, AXES, [(i, i ^ mask) for i in range(count)])  27.4 us
    ppermute x23, waiting for transfers between devices, swap(): return lax.ppermute(array, AXES, [(i, i ^ mask) for i in range(count)])  15.9 us
    pallas_call x1, Pallas kernels, partial_sigma(): pl.pallas_call(lambda *refs: sigma_kernel(places, points, occ_count, *ref...  2.79 us
    pallas_call x1, Pallas kernels, collect(): pl.pallas_call(collect_kernel, out_shape=(pltpu.SMEM((2 * half, 4), jnp.i...  2.14 us
    pallas_call x1, Pallas kernels, pack(): pl.pallas_call(pack_kernel, out_shape=pltpu.VMEM((points + occ_rows, widt...  1.66 us
  transfers between devices with their start and end apart: 23, of which 12 were waited for; matrix products, arithmetic and copies ran while one was open for 1% of the time, Pallas kernels for 7%

profile of v6, /device:TPU:0, one launch (start us, length us, event | category | flops | bytes accessed | tf_op | source)
XLA Modules:
  0.0 52.0 jit_solution(4483766634755243986)
XLA Ops:
  0.0 0.5 collective-permute-start.3
  0.5 0.7 %copy-done = bf16[1,1,8,512]{3,2,1,0:T(8,128)(2,1)S(1)} copy-done((bf16[1,1,8,512]{3,2,1,0:T(8,128)(2,1)S(1)}, bf16[1,1,8,512]{3,2,1,0:T(8,128)(2,1)}, u32[]{:S(2)}) %copy-start) | copy-done | bytes 8216
  1.2 1.7 %shard_map.73.refs_3_ = bf16[544,128]{1,0:T(8,128)(2,1)S(1)} custom-call(s32[1,128]{1,0:T(1,128)} %bitcast.15, bf16[512,1024]{1,0:T(8,128)(2,1)} %bitcast.14, bf16[8,512]{1,0:T(8,128)(2,1)S(1)} %bitcast.13), custom_call_target="tpu_custom_call" | custom-call | tf_op jit(solution)/shard_map/pallas_call | solution.py:49
  2.8 2.6 %collective-permute-start.6 = (bf16[544,128]{1,0:T(8,128)(2,1)S(1)}, bf16[544,128]{1,0:T(8,128)(2,1)S(1)}, u32[]{:S(2)}, u32[]{:S(2)}) collective-permute-start(bf16[544,128]{1,0:T(8,128)(2,1)S(1)} %shard_map.73.refs_3_), channel_id=1, source_target_pairs={{0,8},{1,9},{2,10},{3,11},{4,12},{5,13},{6,14},{7,15},{8,0},{9,1},... | collective-permute-start | bytes 417800 | tf_op jit(solution)/shard_map/ppermute | solution.py:194
  5.5 2.6 %collective-permute-start.2 = (bf16[544,128]{1,0:T(8,128)(2,1)S(1)}, bf16[544,128]{1,0:T(8,128)(2,1)S(1)}, u32[]{:S(2)}, u32[]{:S(2)}) collective-permute-start(bf16[544,128]{1,0:T(8,128)(2,1)S(1)} %shard_map.73.refs_3_), channel_id=1, source_target_pairs={{0,16},{1,17},{2,18},{3,19},{4,20},{5,21},{6,22},{7,23},{8,24},{9,... | collective-permute-start | bytes 417800 | tf_op jit(solution)/shard_map/ppermute | solution.py:194
  8.0 1.5 %collective-permute-start = (bf16[544,128]{1,0:T(8,128)(2,1)S(1)}, bf16[544,128]{1,0:T(8,128)(2,1)S(1)}, u32[]{:S(2)}, u32[]{:S(2)}) collective-permute-start(bf16[544,128]{1,0:T(8,128)(2,1)S(1)} %shard_map.73.refs_3_), channel_id=1, source_target_pairs={{0,2},{1,3},{2,0},{3,1},{4,6},{5,7},{6,4},{7,5},{8,10},{9,11},{10,... | collective-permute-start | bytes 417800 | tf_op jit(solution)/shard_map/ppermute | solution.py:194
  9.6 0.7 %bitcast_add_fusion.own_codes = s32[7]{0:T(128)S(1)} fusion(s32[7,1]{0,1:T(1,128)} %param.11, s32[7]{0:T(128)} %param.12, s32[7]{0:T(128)} %param.13), kind=kLoop, calls=%fused_computation.4 | loop fusion | flops 28 | bytes 112 | tf_op jit(solution)/shard_map/add | solution.py:232
  10.2 0.0 collective-permute-start.1
  10.3 1.1 %collective-permute-done.1.other_codes = s32[7]{0:T(128)S(1)} collective-permute-done((s32[7]{0:T(128)S(1)}, s32[7]{0:T(128)S(1)}, u32[]{:S(2)}, u32[]{:S(2)}) %collective-permute-start.1) | collective-permute-done | bytes 60 | tf_op jit(solution)/shard_map/ppermute | solution.py:194
  11.4 1.5 %collective-permute-start.4 = (bf16[544,128]{1,0:T(8,128)(2,1)S(1)}, bf16[544,128]{1,0:T(8,128)(2,1)S(1)}, u32[]{:S(2)}, u32[]{:S(2)}) collective-permute-start(bf16[544,128]{1,0:T(8,128)(2,1)S(1)} %shard_map.73.refs_3_), channel_id=1, source_target_pairs={{0,4},{1,5},{2,6},{3,7},{4,0},{5,1},{6,2},{7,3},{8,12},{9,13},{10,... | collective-permute-start | bytes 417800 | tf_op jit(solution)/shard_map/ppermute | solution.py:194
  12.9 2.3 %collective-permute-done.2.refs_11_ = bf16[544,128]{1,0:T(8,128)(2,1)S(1)} collective-permute-done((bf16[544,128]{1,0:T(8,128)(2,1)S(1)}, bf16[544,128]{1,0:T(8,128)(2,1)S(1)}, u32[]{:S(2)}, u32[]{:S(2)}) %collective-permute-start.2) | collective-permute-done | bytes 139296 | tf_op jit(solution)/shard_map/ppermute | solution.py:194
  15.2 1.5 %collective-permute-start.11 = (bf16[544,128]{1,0:T(8,128)(2,1)S(1)}, bf16[544,128]{1,0:T(8,128)(2,1)S(1)}, u32[]{:S(2)}, u32[]{:S(2)}) collective-permute-start(bf16[544,128]{1,0:T(8,128)(2,1)S(1)} %collective-permute-done.2.refs_11_), channel_id=1, source_target_pairs={{0,4},{1,5},{2,6},{3,7},{4,0},{5,1},{6,2},{7,3},{8,12},{9,13},{10,... | collective-permute-start | bytes 417800 | tf_op jit(solution)/shard_map/ppermute | solution.py:194
  16.7 0.0 collective-permute-done.refs_4_
  16.7 1.5 %collective-permute-start.10 = (bf16[544,128]{1,0:T(8,128)(2,1)S(1)}, bf16[544,128]{1,0:T(8,128)(2,1)S(1)}, u32[]{:S(2)}, u32[]{:S(2)}) collective-permute-start(bf16[544,128]{1,0:T(8,128)(2,1)S(1)} %collective-permute-done.2.refs_11_), channel_id=1, source_target_pairs={{0,2},{1,3},{2,0},{3,1},{4,6},{5,7},{6,4},{7,5},{8,10},{9,11},{10,... | collective-permute-start | bytes 417800 | tf_op jit(solution)/shard_map/ppermute | solution.py:194
  18.2 0.0 collective-permute-done.6.refs_7_
  18.2 0.5 %collective-permute-start.8 = (bf16[544,128]{1,0:T(8,128)(2,1)S(1)}, bf16[544,128]{1,0:T(8,128)(2,1)S(1)}, u32[]{:S(2)}, u32[]{:S(2)}) collective-permute-start(bf16[544,128]{1,0:T(8,128)(2,1)S(1)} %collective-permute-done.6.refs_7_), channel_id=1, source_target_pairs={{0,4},{1,5},{2,6},{3,7},{4,0},{5,1},{6,2},{7,3},{8,12},{9,13},{10,... | collective-permute-start | bytes 417800 | tf_op jit(solution)/shard_map/ppermute | solution.py:194
  18.7 0.0 collective-permute-done.4.refs_5_
  18.7 0.5 collective-permute-start.7
  19.3 2.4 %collective-permute-done.11.refs_13_ = bf16[544,128]{1,0:T(8,128)(2,1)S(1)} collective-permute-done((bf16[544,128]{1,0:T(8,128)(2,1)S(1)}, bf16[544,128]{1,0:T(8,128)(2,1)S(1)}, u32[]{:S(2)}, u32[]{:S(2)}) %collective-permute-start.11) | collective-permute-done | bytes 139296 | tf_op jit(solution)/shard_map/ppermute | solution.py:194
  21.6 0.0 collective-permute-start.15
  21.6 0.0 collective-permute-done.3.refs_2_
  21.6 2.1 %collective-permute-start.5 = (bf16[544,128]{1,0:T(8,128)(2,1)S(1)}, bf16[544,128]{1,0:T(8,128)(2,1)S(1)}, u32[]{:S(2)}, u32[]{:S(2)}) collective-permute-start(bf16[544,128]{1,0:T(8,128)(2,1)S(1)} %collective-permute-done.refs_4_), channel_id=1, source_target_pairs={{0,4},{1,5},{2,6},{3,7},{4,0},{5,1},{6,2},{7,3},{8,12},{9,13},{10,... | collective-permute-start | bytes 417800 | tf_op jit(solution)/shard_map/ppermute | solution.py:194
  23.7 1.5 %collective-permute-start.14 = (bf16[544,128]{1,0:T(8,128)(2,1)S(1)}, bf16[544,128]{1,0:T(8,128)(2,1)S(1)}, u32[]{:S(2)}, u32[]{:S(2)}) collective-permute-start(bf16[544,128]{1,0:T(8,128)(2,1)S(1)} %collective-permute-done.10.refs_12_), channel_id=1, source_target_pairs={{0,8},{1,9},{2,10},{3,11},{4,12},{5,13},{6,14},{7,15},{8,0},{9,1},... | collective-permute-start | bytes 417800 | tf_op jit(solution)/shard_map/ppermute | solution.py:194
  25.2 0.0 collective-permute-done.8.refs_9_
  25.2 0.6 %collective-permute-start.12 = (bf16[544,128]{1,0:T(8,128)(2,1)S(1)}, bf16[544,128]{1,0:T(8,128)(2,1)S(1)}, u32[]{:S(2)}, u32[]{:S(2)}) collective-permute-start(bf16[544,128]{1,0:T(8,128)(2,1)S(1)} %collective-permute-done.10.refs_12_), channel_id=1, source_target_pairs={{0,4},{1,5},{2,6},{3,7},{4,0},{5,1},{6,2},{7,3},{8,12},{9,13},{10,... | collective-permute-start | bytes 417800 | tf_op jit(solution)/shard_map/ppermute | solution.py:194
  25.7 0.5 collective-permute-start.9
  26.2 0.5 collective-permute-done.15.refs_17_
  26.7 1.1 %collective-permute-start.16 = (bf16[544,128]{1,0:T(8,128)(2,1)S(1)}, bf16[544,128]{1,0:T(8,128)(2,1)S(1)}, u32[]{:S(2)}, u32[]{:S(2)}) collective-permute-start(bf16[544,128]{1,0:T(8,128)(2,1)S(1)} %collective-permute-done.15.refs_17_), channel_id=1, source_target_pairs={{0,2},{1,3},{2,0},{3,1},{4,6},{5,7},{6,4},{7,5},{8,10},{9,11},{10,... | collective-permute-start | bytes 417800 | tf_op jit(solution)/shard_map/ppermute | solution.py:194
  27.8 0.0 collective-permute-done.5.refs_6_
  27.8 1.0 %collective-permute-start.13 = (bf16[544,128]{1,0:T(8,128)(2,1)S(1)}, bf16[544,128]{1,0:T(8,128)(2,1)S(1)}, u32[]{:S(2)}, u32[]{:S(2)}) collective-permute-start(bf16[544,128]{1,0:T(8,128)(2,1)S(1)} %collective-permute-done.2.refs_11_), channel_id=1, source_target_pairs={{0,8},{1,9},{2,10},{3,11},{4,12},{5,13},{6,14},{7,15},{8,0},{9,1},... | collective-permute-start | bytes 417800 | tf_op jit(solution)/shard_map/ppermute | solution.py:194
  28.8 2.1 %shard_map.74 = (s32[8,4]{1,0:T(8,128)S(4)}, bf16[4,512,512]{2,1,0:T(8,128)(2,1)S(1)}) custom-call(s32[7]{0:T(128)} %copy-done.1, s32[7]{0:T(128)} %copy-done.2, bf16[7,512,512]{2,1,0:T(8,128)(2,1)} %own_hbm.1), custom_call_target="tpu_custom_call" | custom-call | tf_op jit(solution)/shard_map/pallas_call | solution.py:116
  31.0 0.0 collective-permute-done.9.refs_10_
  31.0 1.3 %collective-permute-done.16.refs_18_ = bf16[544,128]{1,0:T(8,128)(2,1)S(1)} collective-permute-done((bf16[544,128]{1,0:T(8,128)(2,1)S(1)}, bf16[544,128]{1,0:T(8,128)(2,1)S(1)}, u32[]{:S(2)}, u32[]{:S(2)}) %collective-permute-start.16) | collective-permute-done | bytes 139296 | tf_op jit(solution)/shard_map/ppermute | solution.py:194
  32.3 0.5 %collective-permute-done.13.refs_15_ = bf16[544,128]{1,0:T(8,128)(2,1)S(1)} collective-permute-done((bf16[544,128]{1,0:T(8,128)(2,1)S(1)}, bf16[544,128]{1,0:T(8,128)(2,1)S(1)}, u32[]{:S(2)}, u32[]{:S(2)}) %collective-permute-start.13) | collective-permute-done | bytes 139296 | tf_op jit(solution)/shard_map/ppermute | solution.py:194
  32.8 2.8 %shard_map.75 = f32[2,128,128]{2,1,0:T(8,128)S(1)} custom-call(s32[8,4]{1,0:T(8,128)S(4)} %get-tuple-element.14.refs_0_, bf16[4,512,512]{2,1,0:T(8,128)(2,1)S(1)} %get-tuple-element.15.refs_1_, bf16[7,512,512]{2,1,0:T(8,128)(2,1)S(1)} %collective-permute-done.3.refs_2_, bf16[544,128]{1,0:T(8,128)(2,1)S(1)} %shard_map.73.refs_3_, ...), custom_call_target="tpu_custom_call" | custom-call | tf_op jit(solution)/shard_map/pallas_call | solution.py:173
  35.6 1.9 %collective-permute-start.18 = (f32[128,128]{1,0:T(8,128)S(1)}, f32[128,128]{1,0:T(8,128)S(1)}, u32[]{:S(2)}, u32[]{:S(2)}) collective-permute-start(f32[128,128]{1,0:T(8,128)S(1)} %get-tuple-element.20), channel_id=1, source_target_pairs={{0,16},{1,17},{2,18},{3,19},{4,20},{5,21},{6,22},{7,23},{8,24},{9,... | collective-permute-start | bytes 196616 | tf_op jit(solution)/shard_map/ppermute | solution.py:194
  37.5 1.6 %collective-permute-start.19 = (f32[128,128]{1,0:T(8,128)S(1)}, f32[128,128]{1,0:T(8,128)S(1)}, u32[]{:S(2)}, u32[]{:S(2)}) collective-permute-start(f32[128,128]{1,0:T(8,128)S(1)} %get-tuple-element.19), channel_id=1, source_target_pairs={{0,18},{1,19},{2,16},{3,17},{4,22},{5,23},{6,20},{7,21},{8,26},{9,... | collective-permute-start | bytes 196616 | tf_op jit(solution)/shard_map/ppermute | solution.py:194
  39.1 1.0 %collective-permute-start.17 = (f32[128,128]{1,0:T(8,128)S(1)}, f32[128,128]{1,0:T(8,128)S(1)}, u32[]{:S(2)}, u32[]{:S(2)}) collective-permute-start(f32[128,128]{1,0:T(8,128)S(1)} %get-tuple-element.19), channel_id=1, source_target_pairs={{0,2},{1,3},{2,0},{3,1},{4,6},{5,7},{6,4},{7,5},{8,10},{9,11},{10,... | collective-permute-start | bytes 196616 | tf_op jit(solution)/shard_map/ppermute | solution.py:194
  40.1 1.5 %collective-permute-done.18 = f32[128,128]{1,0:T(8,128)S(1)} collective-permute-done((f32[128,128]{1,0:T(8,128)S(1)}, f32[128,128]{1,0:T(8,128)S(1)}, u32[]{:S(2)}, u32[]{:S(2)}) %collective-permute-start.18) | collective-permute-done | bytes 65568 | tf_op jit(solution)/shard_map/ppermute | solution.py:194
  41.6 2.1 %collective-permute-done.19 = f32[128,128]{1,0:T(8,128)S(1)} collective-permute-done((f32[128,128]{1,0:T(8,128)S(1)}, f32[128,128]{1,0:T(8,128)S(1)}, u32[]{:S(2)}, u32[]{:S(2)}) %collective-permute-start.19) | collective-permute-done | bytes 65568 | tf_op jit(solution)/shard_map/ppermute | solution.py:194
  43.7 0.4 collective-permute-done.17
  44.1 2.5 %collective-permute-start.22 = (f32[128,128]{1,0:T(8,128)S(1)}, f32[128,128]{1,0:T(8,128)S(1)}, u32[]{:S(2)}, u32[]{:S(2)}) collective-permute-start(f32[128,128]{1,0:T(8,128)S(1)} %add_add_fusion), channel_id=1, source_target_pairs={{0,12},{1,13},{2,14},{3,15},{4,8},{5,9},{6,10},{7,11},{8,4},{9,5},... | collective-permute-start | bytes 196616 | tf_op jit(solution)/shard_map/ppermute | solution.py:194
  46.6 0.5 collective-permute-start.21
  47.1 0.5 %collective-permute-start.20 = (f32[128,128]{1,0:T(8,128)S(1)}, f32[128,128]{1,0:T(8,128)S(1)}, u32[]{:S(2)}, u32[]{:S(2)}) collective-permute-start(f32[128,128]{1,0:T(8,128)S(1)} %add_add_fusion), channel_id=1, source_target_pairs={{0,4},{1,5},{2,6},{3,7},{4,0},{5,1},{6,2},{7,3},{8,12},{9,13},{10,... | collective-permute-start | bytes 196616 | tf_op jit(solution)/shard_map/ppermute | solution.py:194
  47.7 1.7 %collective-permute-done.22 = f32[128,128]{1,0:T(8,128)S(1)} collective-permute-done((f32[128,128]{1,0:T(8,128)S(1)}, f32[128,128]{1,0:T(8,128)S(1)}, u32[]{:S(2)}, u32[]{:S(2)}) %collective-permute-start.22) | collective-permute-done | bytes 65568 | tf_op jit(solution)/shard_map/ppermute | solution.py:194
  49.3 1.6 %collective-permute-done.21 = f32[128,128]{1,0:T(8,128)S(1)} collective-permute-done((f32[128,128]{1,0:T(8,128)S(1)}, f32[128,128]{1,0:T(8,128)S(1)}, u32[]{:S(2)}, u32[]{:S(2)}) %collective-permute-start.21) | collective-permute-done | bytes 65568 | tf_op jit(solution)/shard_map/ppermute | solution.py:194
  50.9 0.5 collective-permute-done.20
  51.4 0.6 %add_bitcast_fusion = f32[1,128,128]{2,1,0:T(8,128)} fusion(f32[128,128]{1,0:T(8,128)S(1)} %collective-permute-done.21, f32[128,128]{1,0:T(8,128)S(1)} %collective-permute-done.22, f32[128,128]{1,0:T(8,128)S(1)} %add_add_fusion, f32[128,128]{1,0:T(8,128)S(1)} %collective-permute-done.20), kind=kLoop, calls=%fused_computation.2 | loop fusion | flops 49152 | bytes 327680 | tf_op jit(solution)/shard_map/broadcast_in_dim | solution.py:250
  (11 shorter events, 0.0 us)
Async XLA Ops:
  0.0 21.6 %collective-permute-start.3 = (bf16[7,512,512]{2,1,0:T(8,128)(2,1)}, bf16[7,512,512]{2,1,0:T(8,128)(2,1)S(1)}, u32[]{:S(2)}, u32[]{:S(2)}) collective-permute-start(bf16[7,512,512]{2,1,0:T(8,128)(2,1)} %own_hbm.1), channel_id=1, source_target_pairs={{0,1},{1,0},{2,3},{3,2},{4,5},{5,4},{6,7},{7,6},{8,9},{9,8},{10,11... | collective-permute-start | bytes 11010056 | tf_op jit(solution)/shard_map/ppermute | solution.py:194
  0.5 0.7 %copy-start = (bf16[1,1,8,512]{3,2,1,0:T(8,128)(2,1)S(1)}, bf16[1,1,8,512]{3,2,1,0:T(8,128)(2,1)}, u32[]{:S(2)}) copy-start(bf16[1,1,8,512]{3,2,1,0:T(8,128)(2,1)} %param.8) | copy-start | bytes 24580
  2.8 15.4 %collective-permute-start.6 = (bf16[544,128]{1,0:T(8,128)(2,1)S(1)}, bf16[544,128]{1,0:T(8,128)(2,1)S(1)}, u32[]{:S(2)}, u32[]{:S(2)}) collective-permute-start(bf16[544,128]{1,0:T(8,128)(2,1)S(1)} %shard_map.73.refs_3_), channel_id=1, source_target_pairs={{0,8},{1,9},{2,10},{3,11},{4,12},{5,13},{6,14},{7,15},{8,0},{9,1},... | collective-permute-start | bytes 417800 | tf_op jit(solution)/shard_map/ppermute | solution.py:194
  5.5 9.7 %collective-permute-start.2 = (bf16[544,128]{1,0:T(8,128)(2,1)S(1)}, bf16[544,128]{1,0:T(8,128)(2,1)S(1)}, u32[]{:S(2)}, u32[]{:S(2)}) collective-permute-start(bf16[544,128]{1,0:T(8,128)(2,1)S(1)} %shard_map.73.refs_3_), channel_id=1, source_target_pairs={{0,16},{1,17},{2,18},{3,19},{4,20},{5,21},{6,22},{7,23},{8,24},{9,... | collective-permute-start | bytes 417800 | tf_op jit(solution)/shard_map/ppermute | solution.py:194
  8.0 8.6 %collective-permute-start = (bf16[544,128]{1,0:T(8,128)(2,1)S(1)}, bf16[544,128]{1,0:T(8,128)(2,1)S(1)}, u32[]{:S(2)}, u32[]{:S(2)}) collective-permute-start(bf16[544,128]{1,0:T(8,128)(2,1)S(1)} %shard_map.73.refs_3_), channel_id=1, source_target_pairs={{0,2},{1,3},{2,0},{3,1},{4,6},{5,7},{6,4},{7,5},{8,10},{9,11},{10,... | collective-permute-start | bytes 417800 | tf_op jit(solution)/shard_map/ppermute | solution.py:194
  10.2 18.6 %copy-start.1 = (s32[7]{0:T(128)}, s32[7]{0:T(128)S(1)}, u32[]{:S(2)}) copy-start(s32[7]{0:T(128)S(1)} %bitcast_add_fusion.own_codes) | copy-start | bytes 88
  10.2 1.1 %collective-permute-start.1 = (s32[7]{0:T(128)S(1)}, s32[7]{0:T(128)S(1)}, u32[]{:S(2)}, u32[]{:S(2)}) collective-permute-start(s32[7]{0:T(128)S(1)} %bitcast_add_fusion.own_codes), channel_id=1, source_target_pairs={{0,1},{1,0},{2,3},{3,2},{4,5},{5,4},{6,7},{7,6},{8,9},{9,8},{10,11... | collective-permute-start | bytes 92 | tf_op jit(solution)/shard_map/ppermute | solution.py:194
  11.4 17.4 %copy-start.2 = (s32[7]{0:T(128)}, s32[7]{0:T(128)S(1)}, u32[]{:S(2)}) copy-start(s32[7]{0:T(128)S(1)} %collective-permute-done.1.other_codes) | copy-start | bytes 88
  11.4 7.4 %collective-permute-start.4 = (bf16[544,128]{1,0:T(8,128)(2,1)S(1)}, bf16[544,128]{1,0:T(8,128)(2,1)S(1)}, u32[]{:S(2)}, u32[]{:S(2)}) collective-permute-start(bf16[544,128]{1,0:T(8,128)(2,1)S(1)} %shard_map.73.refs_3_), channel_id=1, source_target_pairs={{0,4},{1,5},{2,6},{3,7},{4,0},{5,1},{6,2},{7,3},{8,12},{9,13},{10,... | collective-permute-start | bytes 417800 | tf_op jit(solution)/shard_map/ppermute | solution.py:194
  15.2 6.4 %collective-permute-start.11 = (bf16[544,128]{1,0:T(8,128)(2,1)S(1)}, bf16[544,128]{1,0:T(8,128)(2,1)S(1)}, u32[]{:S(2)}, u32[]{:S(2)}) collective-permute-start(bf16[544,128]{1,0:T(8,128)(2,1)S(1)} %collective-permute-done.2.refs_11_), channel_id=1, source_target_pairs={{0,4},{1,5},{2,6},{3,7},{4,0},{5,1},{6,2},{7,3},{8,12},{9,13},{10,... | collective-permute-start | bytes 417800 | tf_op jit(solution)/shard_map/ppermute | solution.py:194
  16.7 7.0 %collective-permute-start.10 = (bf16[544,128]{1,0:T(8,128)(2,1)S(1)}, bf16[544,128]{1,0:T(8,128)(2,1)S(1)}, u32[]{:S(2)}, u32[]{:S(2)}) collective-permute-start(bf16[544,128]{1,0:T(8,128)(2,1)S(1)} %collective-permute-done.2.refs_11_), channel_id=1, source_target_pairs={{0,2},{1,3},{2,0},{3,1},{4,6},{5,7},{6,4},{7,5},{8,10},{9,11},{10,... | collective-permute-start | bytes 417800 | tf_op jit(solution)/shard_map/ppermute | solution.py:194
  18.2 7.0 %collective-permute-start.8 = (bf16[544,128]{1,0:T(8,128)(2,1)S(1)}, bf16[544,128]{1,0:T(8,128)(2,1)S(1)}, u32[]{:S(2)}, u32[]{:S(2)}) collective-permute-start(bf16[544,128]{1,0:T(8,128)(2,1)S(1)} %collective-permute-done.6.refs_7_), channel_id=1, source_target_pairs={{0,4},{1,5},{2,6},{3,7},{4,0},{5,1},{6,2},{7,3},{8,12},{9,13},{10,... | collective-permute-start | bytes 417800 | tf_op jit(solution)/shard_map/ppermute | solution.py:194
  18.7 7.0 %collective-permute-start.7 = (bf16[544,128]{1,0:T(8,128)(2,1)S(1)}, bf16[544,128]{1,0:T(8,128)(2,1)S(1)}, u32[]{:S(2)}, u32[]{:S(2)}) collective-permute-start(bf16[544,128]{1,0:T(8,128)(2,1)S(1)} %collective-permute-done.6.refs_7_), channel_id=1, source_target_pairs={{0,2},{1,3},{2,0},{3,1},{4,6},{5,7},{6,4},{7,5},{8,10},{9,11},{10,... | collective-permute-start | bytes 417800 | tf_op jit(solution)/shard_map/ppermute | solution.py:194
  21.6 5.1 %collective-permute-start.15 = (bf16[544,128]{1,0:T(8,128)(2,1)S(1)}, bf16[544,128]{1,0:T(8,128)(2,1)S(1)}, u32[]{:S(2)}, u32[]{:S(2)}) collective-permute-start(bf16[544,128]{1,0:T(8,128)(2,1)S(1)} %collective-permute-done.11.refs_13_), channel_id=1, source_target_pairs={{0,8},{1,9},{2,10},{3,11},{4,12},{5,13},{6,14},{7,15},{8,0},{9,1},... | collective-permute-start | bytes 417800 | tf_op jit(solution)/shard_map/ppermute | solution.py:194
  21.6 6.1 %collective-permute-start.5 = (bf16[544,128]{1,0:T(8,128)(2,1)S(1)}, bf16[544,128]{1,0:T(8,128)(2,1)S(1)}, u32[]{:S(2)}, u32[]{:S(2)}) collective-permute-start(bf16[544,128]{1,0:T(8,128)(2,1)S(1)} %collective-permute-done.refs_4_), channel_id=1, source_target_pairs={{0,4},{1,5},{2,6},{3,7},{4,0},{5,1},{6,2},{7,3},{8,12},{9,13},{10,... | collective-permute-start | bytes 417800 | tf_op jit(solution)/shard_map/ppermute | solution.py:194
  23.7 7.3 %collective-permute-start.14 = (bf16[544,128]{1,0:T(8,128)(2,1)S(1)}, bf16[544,128]{1,0:T(8,128)(2,1)S(1)}, u32[]{:S(2)}, u32[]{:S(2)}) collective-permute-start(bf16[544,128]{1,0:T(8,128)(2,1)S(1)} %collective-permute-done.10.refs_12_), channel_id=1, source_target_pairs={{0,8},{1,9},{2,10},{3,11},{4,12},{5,13},{6,14},{7,15},{8,0},{9,1},... | collective-permute-start | bytes 417800 | tf_op jit(solution)/shard_map/ppermute | solution.py:194
  25.2 5.8 %collective-permute-start.12 = (bf16[544,128]{1,0:T(8,128)(2,1)S(1)}, bf16[544,128]{1,0:T(8,128)(2,1)S(1)}, u32[]{:S(2)}, u32[]{:S(2)}) collective-permute-start(bf16[544,128]{1,0:T(8,128)(2,1)S(1)} %collective-permute-done.10.refs_12_), channel_id=1, source_target_pairs={{0,4},{1,5},{2,6},{3,7},{4,0},{5,1},{6,2},{7,3},{8,12},{9,13},{10,... | collective-permute-start | bytes 417800 | tf_op jit(solution)/shard_map/ppermute | solution.py:194
  25.7 5.2 %collective-permute-start.9 = (bf16[544,128]{1,0:T(8,128)(2,1)S(1)}, bf16[544,128]{1,0:T(8,128)(2,1)S(1)}, u32[]{:S(2)}, u32[]{:S(2)}) collective-permute-start(bf16[544,128]{1,0:T(8,128)(2,1)S(1)} %collective-permute-done.8.refs_9_), channel_id=1, source_target_pairs={{0,2},{1,3},{2,0},{3,1},{4,6},{5,7},{6,4},{7,5},{8,10},{9,11},{10,... | collective-permute-start | bytes 417800 | tf_op jit(solution)/shard_map/ppermute | solution.py:194
  26.7 5.6 %collective-permute-start.16 = (bf16[544,128]{1,0:T(8,128)(2,1)S(1)}, bf16[544,128]{1,0:T(8,128)(2,1)S(1)}, u32[]{:S(2)}, u32[]{:S(2)}) collective-permute-start(bf16[544,128]{1,0:T(8,128)(2,1)S(1)} %collective-permute-done.15.refs_17_), channel_id=1, source_target_pairs={{0,2},{1,3},{2,0},{3,1},{4,6},{5,7},{6,4},{7,5},{8,10},{9,11},{10,... | collective-permute-start | bytes 417800 | tf_op jit(solution)/shard_map/ppermute | solution.py:194
  27.8 5.1 %collective-permute-start.13 = (bf16[544,128]{1,0:T(8,128)(2,1)S(1)}, bf16[544,128]{1,0:T(8,128)(2,1)S(1)}, u32[]{:S(2)}, u32[]{:S(2)}) collective-permute-start(bf16[544,128]{1,0:T(8,128)(2,1)S(1)} %collective-permute-done.2.refs_11_), channel_id=1, source_target_pairs={{0,8},{1,9},{2,10},{3,11},{4,12},{5,13},{6,14},{7,15},{8,0},{9,1},... | collective-permute-start | bytes 417800 | tf_op jit(solution)/shard_map/ppermute | solution.py:194
  35.6 5.9 %collective-permute-start.18 = (f32[128,128]{1,0:T(8,128)S(1)}, f32[128,128]{1,0:T(8,128)S(1)}, u32[]{:S(2)}, u32[]{:S(2)}) collective-permute-start(f32[128,128]{1,0:T(8,128)S(1)} %get-tuple-element.20), channel_id=1, source_target_pairs={{0,16},{1,17},{2,18},{3,19},{4,20},{5,21},{6,22},{7,23},{8,24},{9,... | collective-permute-start | bytes 196616 | tf_op jit(solution)/shard_map/ppermute | solution.py:194
  37.5 6.2 %collective-permute-start.19 = (f32[128,128]{1,0:T(8,128)S(1)}, f32[128,128]{1,0:T(8,128)S(1)}, u32[]{:S(2)}, u32[]{:S(2)}) collective-permute-start(f32[128,128]{1,0:T(8,128)S(1)} %get-tuple-element.19), channel_id=1, source_target_pairs={{0,18},{1,19},{2,16},{3,17},{4,22},{5,23},{6,20},{7,21},{8,26},{9,... | collective-permute-start | bytes 196616 | tf_op jit(solution)/shard_map/ppermute | solution.py:194
  39.1 5.0 %collective-permute-start.17 = (f32[128,128]{1,0:T(8,128)S(1)}, f32[128,128]{1,0:T(8,128)S(1)}, u32[]{:S(2)}, u32[]{:S(2)}) collective-permute-start(f32[128,128]{1,0:T(8,128)S(1)} %get-tuple-element.19), channel_id=1, source_target_pairs={{0,2},{1,3},{2,0},{3,1},{4,6},{5,7},{6,4},{7,5},{8,10},{9,11},{10,... | collective-permute-start | bytes 196616 | tf_op jit(solution)/shard_map/ppermute | solution.py:194
  44.1 5.2 %collective-permute-start.22 = (f32[128,128]{1,0:T(8,128)S(1)}, f32[128,128]{1,0:T(8,128)S(1)}, u32[]{:S(2)}, u32[]{:S(2)}) collective-permute-start(f32[128,128]{1,0:T(8,128)S(1)} %add_add_fusion), channel_id=1, source_target_pairs={{0,12},{1,13},{2,14},{3,15},{4,8},{5,9},{6,10},{7,11},{8,4},{9,5},... | collective-permute-start | bytes 196616 | tf_op jit(solution)/shard_map/ppermute | solution.py:194
  46.6 4.3 %collective-permute-start.21 = (f32[128,128]{1,0:T(8,128)S(1)}, f32[128,128]{1,0:T(8,128)S(1)}, u32[]{:S(2)}, u32[]{:S(2)}) collective-permute-start(f32[128,128]{1,0:T(8,128)S(1)} %add_add_fusion), channel_id=1, source_target_pairs={{0,8},{1,9},{2,10},{3,11},{4,12},{5,13},{6,14},{7,15},{8,0},{9,1},... | collective-permute-start | bytes 196616 | tf_op jit(solution)/shard_map/ppermute | solution.py:194
  47.1 4.3 %collective-permute-start.20 = (f32[128,128]{1,0:T(8,128)S(1)}, f32[128,128]{1,0:T(8,128)S(1)}, u32[]{:S(2)}, u32[]{:S(2)}) collective-permute-start(f32[128,128]{1,0:T(8,128)S(1)} %add_add_fusion), channel_id=1, source_target_pairs={{0,4},{1,5},{2,6},{3,7},{4,0},{5,1},{6,2},{7,3},{8,12},{9,13},{10,... | collective-permute-start | bytes 196616 | tf_op jit(solution)/shard_map/ppermute | solution.py:194
